TPU v7x, 1024 devices: a whole 8x8x8 slice. The times are simulated.
1024 devices in a mesh: dp: 64 (over x, y), tensor: 16 (over z, core).
Axes of the slice: x: 8, y: 8, z: 8, core: 2. Of those that a mesh axis runs over, the one named last changes fastest.
Arguments:
- attn_output: bfloat16 [49152, 2560], P('dp', 'tensor'), may hold values from -6 to 6
- readout_vectors: bfloat16 [49152, 2560], P('dp', 'tensor'), may hold values from -0.0390625 to 0.0390625
- w_out: bfloat16 [2560, 2560], P('tensor'), may hold values from -0.125 to 0.125
- log_gap: bfloat16 [49152], P('dp'), may hold values from -0.8984375 to 0.8984375
- magnitude: bfloat16 [49152], P('dp'), may hold values from 0.29882812 to 3
- reward_sign: int32 [49152], P('dp'), may hold values from 0 to 1
- keep_mask: int32 [49152], P('dp'), may hold values 0 or 1
- move_plan: int32 [64, 64], replicated, may hold values from 0 to 12, as said below
Outputs:
- grad_shard: float32 [2560, 2560], P('tensor', 'dp')
- statistics: float32 [3], replicated
Inputs may be any that keep to these rules, and one draw needn't show every extreme that they name: Data index i's live slots are its first sum_j move_plan[i, j] slots; they go in order, the first move_plan[i, 0] to index 0, the next move_plan[i, 1] to index 1, and so on. Every entry is at most 12; each column sums to at most 384, some column to exactly 384; some row sums to exactly 768.
All inputs are finite; a program needn't handle non-finite values. No bound on the sum of `keep_mask` on one device may be relied on, other than what follows from the above.
Results may differ from a plain program's by a relative error of at most 0.008.
Values may be sent and summed in bfloat16 or wider, within the bound.
No kernel may reach another device: no remote copies, remote signals or barrier semaphores. Data moves between devices by JAX's collectives and lax.ppermute only.
A program may use at most 64 MiB of HBM per device.

v0:
```python
import jax
import jax.numpy as jnp
from jax import lax
from jax.sharding import PartitionSpec as P

EPS_LOW = 0.2
EPS_HIGH = 0.28
LOSS_SCALE = 16384.0


def body(
    attn_output, readout_vectors, w_out, log_gap, magnitude, reward_sign, keep_mask, move_plan
):
    local_rows = attn_output.shape[0]
    dp_index = lax.axis_index("dp")
    send_counts = lax.dynamic_slice_in_dim(move_plan, dp_index, 1, 0)[0]
    live_total = jnp.sum(send_counts)
    slot_ids = jnp.arange(local_rows, dtype=jnp.int32)
    weight_int = (slot_ids < live_total).astype(jnp.int32) * keep_mask
    local_count = jnp.sum(weight_int)
    advantage = (2 * reward_sign - 1).astype(jnp.float32) * magnitude.astype(jnp.float32)
    gap_rows = log_gap.astype(jnp.float32)
    weight_rows = weight_int.astype(jnp.float32)
    outputs_t = lax.psum_scatter(
        lax.dot_general(
            w_out, attn_output, (((0,), (1,)), ((), ())), preferred_element_type=jnp.float32
        ).astype(jnp.bfloat16),
        "tensor",
        scatter_dimension=0,
        tiled=True,
    ).astype(jnp.float32)
    partial_sum = jnp.sum(outputs_t * jnp.transpose(readout_vectors).astype(jnp.float32), axis=0)
    log_shift = lax.psum(partial_sum, "tensor")
    prob_ratio = jnp.exp(gap_rows + log_shift)
    base_ratio = jnp.exp(gap_rows)
    clip_high = ((advantage > 0) & (base_ratio > 1.0 + EPS_HIGH)).astype(jnp.float32)
    clip_low = ((advantage < 0) & (base_ratio < 1.0 - EPS_LOW)).astype(jnp.float32)
    surrogate = jnp.minimum(
        prob_ratio * advantage, jnp.clip(prob_ratio, 1.0 - EPS_LOW, 1.0 + EPS_HIGH) * advantage
    )
    loss_part = jnp.sum(weight_rows * surrogate)
    high_part = jnp.sum(weight_rows * clip_high)
    low_part = jnp.sum(weight_rows * clip_low)
    total_count, loss_sum, high_sum, low_sum = lax.psum(
        (local_count.astype(jnp.float32), loss_part, high_part, low_part), "dp"
    )
    divisor = jnp.maximum(total_count, 1.0)
    coefficient = (
        -LOSS_SCALE * weight_rows * advantage * prob_ratio * (1.0 - clip_high - clip_low) / divisor
    )
    upstream = (coefficient[:, None] * readout_vectors.astype(jnp.float32)).astype(jnp.bfloat16)
    local_grad = lax.dot_general(
        attn_output,
        lax.all_gather(upstream, "tensor", axis=1, tiled=True),
        (((0,), (0,)), ((), ())),
        preferred_element_type=jnp.float32,
    )
    grad_shard = lax.psum_scatter(local_grad, "dp", scatter_dimension=1, tiled=True)
    statistics = jnp.stack([-loss_sum / divisor, high_sum / divisor, low_sum / divisor])
    return (grad_shard, statistics)


def solution(mesh):
    placed = (
        P("dp", "tensor"),
        P("dp", "tensor"),
        P("tensor", None),
        P("dp"),
        P("dp"),
        P("dp"),
        P("dp"),
        P(),
    )
    return jax.shard_map(
        body, mesh=mesh, in_specs=placed, out_specs=(P("tensor", "dp"), P()), check_vma=False
    )
```

profile of v0, /device:TPU:16, one launch (start us, length us, event | category | flops | bytes accessed | tf_op | source)
XLA Modules:
  0.0 491.0 jit_solution(10685124189753518384)
XLA Ops:
  7.2 0.0 copy-start
  7.2 0.0 reduce-scatter.3.cloned.1.call-start
  7.2 1.1 copy-done
  8.3 4.1 convolution_convert_fusion
  12.4 0.0 copy-start.6
  12.4 0.0 copy-start.2
  12.4 0.0 reduce-scatter.3.cloned.1.call-update
  12.4 0.0 all-gather.2.cloned.1.call-start
  12.5 1.5 dynamic-slice_reduce_fusion
  14.0 0.0 copy-done.3
  14.0 1.3 fusion.9
  15.9 77.4 %reduce-scatter.3.cloned.1.call-done = bf16[160,768]{1,0:T(8,128)(2,1)} async-done(((bf16[2560,768]{1,0:T(8,128)(2,1)}), bf16[160,768]{1,0:T(8,128)(2,1)}) %reduce-scatter.3.cloned.1.call-update) | async-done | bytes 245776 | tf_op jit(solution)/shard_map/reduce_scatter | solution.py:24
  93.4 0.0 copy-done.1
  93.4 1.0 fusion.1
  94.4 23.7 %psum.35 = f32[768]{0:T(1024)S(1)} all-reduce(f32[768]{0:T(1024)S(1)} %fusion.1), channel_id=1, replica_groups=mesh['dp'=64,'tensor'=16] {'tensor'}, use_global_device_ids=true, to_apply=%region_3.0 | all-reduce | flops 768 | bytes 6144 | tf_op jit(solution)/shard_map/psum | solution.py:33
  118.1 0.0 copy-done.4
  118.1 0.0 copy-done.5
  118.1 0.0 copy-done.6
  118.1 1.3 multiply_reduce_fusion
  119.5 140.4 %all-reduce.1 = (f32[]{:T(128)}, f32[]{:T(128)}, f32[]{:T(128)}, f32[]{:T(128)}) all-reduce(f32[]{:T(128)S(6)} %convert_element_type.50, f32[]{:T(128)} %get-tuple-element.7, f32[]{:T(128)} %get-tuple-element.8, f32[]{:T(128)} %get-tuple-element.6), channel_id=1, replica_groups=mesh['dp'=64,'tensor'=16] {'dp'}, use_global_device_ids=true, to_apply=%region_5.6 | all-reduce | flops 4 | bytes 32 | tf_op jit(solution)/shard_map/psum | solution.py:44
  260.5 0.7 multiply_divide_fusion
  261.1 0.8 fusion.2
  261.9 0.0 all-gather.2.cloned.1.call-update
  261.9 0.0 all-reduce.4.cloned.1.call-start
  262.0 45.3 %all-gather.2.cloned.1.call-done = bf16[768,2560]{0,1:T(8,128)(2,1)} async-done(((bf16[768,160]{0,1:T(8,128)(2,1)}), bf16[768,2560]{0,1:T(8,128)(2,1)}) %all-gather.2.cloned.1.call-update) | async-done | bytes 3932176 | tf_op jit(solution)/shard_map/all_gather | solution.py:54
  307.3 4.7 convolution_bitcast_fusion
  312.0 0.0 all-reduce.4.cloned.1.call-update
  312.0 1.3 dynamic-slice
  315.9 0.6 pad_maximum_fusion
  316.5 166.3 %all-reduce.4.cloned.1.call-done = f32[160,2560]{1,0:T(8,128)} async-done(((f32[160,2560]{1,0:T(8,128)}), f32[160,2560]{1,0:T(8,128)}) %all-reduce.4.cloned.1.call-update) | async-done | bytes 1638416
  482.8 1.0 constant_dynamic-slice_fusion
  483.8 0.7 copy.11
  (5 shorter events, 0.0 us)
Async XLA Ops:
  7.2 1.2 copy-start
  7.2 86.2 %reduce-scatter.3.cloned.1.call-start = ((), (), s32[]{:S(2)}) async-start(), calls=%async_computation.1 | async-start | bytes 4177920 | tf_op jit(solution)/shard_map/reduce_scatter | solution.py:24
  12.4 1.6 copy-start.3
  12.4 81.0 %copy-start.1 = (bf16[768,160]{0,1:T(8,128)(2,1)S(1)}, bf16[768,160]{0,1:T(8,128)(2,1)}, u32[]{:S(2)}) copy-start(bf16[768,160]{0,1:T(8,128)(2,1)} %param.9) | copy-start | bytes 737284
  12.4 105.7 %copy-start.4 = (s32[768]{0:T(1024)S(1)}, s32[768]{0:T(1024)}, u32[]{:S(2)}) copy-start(s32[768]{0:T(1024)} %param.13) | copy-start | bytes 9220
  12.4 105.7 %copy-start.5 = (bf16[768]{0:T(1024)(128)(2,1)S(1)}, bf16[768]{0:T(1024)(128)(2,1)}, u32[]{:S(2)}) copy-start(bf16[768]{0:T(1024)(128)(2,1)} %param.11) | copy-start | bytes 4612
  12.4 105.7 %copy-start.6 = (bf16[768]{0:T(1024)(128)(2,1)S(1)}, bf16[768]{0:T(1024)(128)(2,1)}, u32[]{:S(2)}) copy-start(bf16[768]{0:T(1024)(128)(2,1)} %param.12) | copy-start | bytes 4612
  12.4 294.9 %copy-start.2 = (bf16[768,160]{0,1:T(8,128)(2,1)S(1)}, bf16[768,160]{0,1:T(8,128)(2,1)}, u32[]{:S(2)}) copy-start(bf16[768,160]{0,1:T(8,128)(2,1)} %param.8) | copy-start | bytes 737284
  12.4 294.8 %all-gather.2.cloned.1.call-start = ((), (), s32[]{:S(2)}) async-start(), calls=%async_computation.2 | async-start | bytes 4177920 | tf_op jit(solution)/shard_map/all_gather | solution.py:54
  261.9 220.9 %all-reduce.4.cloned.1.call-start = ((), (), s32[]{:S(2)}) async-start(), calls=%async_computation.3 | async-start | bytes 3276800
Sparse Core Ops, SparseCore 0:
  12.6 80.7 reduce-scatter.2
  262.0 45.2 all-gather.1
  312.2 170.5 all-reduce.3
where the time goes:
time: 492 us; the launch traced here: 491 us
  waiting for transfers between devices  289 us (59%)
  blocking collectives  164 us (33%)
  between operations  17.7 us (4%)
  matrix products  8.78 us (2%)
  other arithmetic  7.16 us (1%)
    unnamed x4, waiting for transfers between devices  166 us
    psum x1, blocking collectives, body(): lax.psum((local_count.astype(jnp.float32), loss_part, high_part, low_part...  140 us
    reduce_scatter x1, waiting for transfers between devices, body(): lax.psum_scatter(lax.dot_general(w_out, attn_output, (((0,), (1,)), ((),...  77.4 us
    all_gather x1, waiting for transfers between devices, body(): lax.all_gather(upstream, 'tensor', axis=1, tiled=True)  45.3 us
    psum x1, blocking collectives, body(): log_shift = lax.psum(partial_sum, 'tensor')  23.7 us
  transfers between devices with their start and end apart: 3, of which 3 were waited for; matrix products, arithmetic and copies ran while one was open for 1% of the time, Pallas kernels for 0%

commit v1 on v0

v1 whole, which is shorter than its diff:
```python
import jax
import jax.numpy as jnp
from jax import lax
from jax.experimental import pallas as pl
from jax.experimental.pallas import tpu as pltpu
from jax.sharding import PartitionSpec as P

EPS_LOW = 0.2
EPS_HIGH = 0.28
LOSS_SCALE = 16384.0
N_DP = 64
N_TENSOR = 16
CHUNK_ROWS = 56
LANES = 128


def vmem_spec():
    return pl.BlockSpec(memory_space=pltpu.VMEM)


def grad_kernel(recv_ref, aux_ref, sums_ref, attn_ref, readout_ref, out_ref, scaled_ref, stats_ref):
    @pl.when(pl.program_id(0) == 0)
    def _():
        shift = jnp.sum(recv_ref[...], axis=0)
        gap, signed, base = aux_ref[0], aux_ref[1], aux_ref[2]
        ratio = jnp.exp(gap + shift)
        loss = jnp.sum(
            jnp.minimum(ratio * signed, jnp.clip(ratio, 1.0 - EPS_LOW, 1.0 + EPS_HIGH) * signed)
        )
        coefficient = base * ratio
        row = jnp.concatenate([coefficient[r : r + 1] for r in range(6)], axis=1)
        scaled_ref[...] = (attn_ref[...].astype(jnp.float32) * row).astype(jnp.bfloat16)
        lane = lax.broadcasted_iota(jnp.int32, (8, LANES), 1)
        is_loss = (lane == 35) | (lane == 39) | (lane == 43)
        value = jnp.where(is_loss, loss, jnp.broadcast_to(sums_ref[...], (8, LANES)))
        high = value.astype(jnp.bfloat16).astype(jnp.float32)
        middle = (value - high).astype(jnp.bfloat16).astype(jnp.float32)
        low = value - high - middle
        stats_ref[...] = jnp.where(lane < 36, high, jnp.where(lane < 40, middle, low))

    product = lax.dot_general(
        readout_ref[...],
        scaled_ref[...],
        (((1,), (1,)), ((), ())),
        preferred_element_type=jnp.float32,
    )
    for q in range(4):
        part = product[40 * q : 40 * q + 40]
        rest = part[:, LANES:]
        first = jnp.concatenate([rest[8 * k : 8 * k + 8] for k in range(4)], axis=1)
        second = jnp.concatenate([rest[32:40], stats_ref[:, 32:]], axis=1)
        out_ref[q] = jnp.concatenate([part[:, :LANES], first, second], axis=0).astype(jnp.bfloat16)


def finish_kernel(recv_ref, grad_ref, stats_ref):
    total = jnp.sum(recv_ref[...].astype(jnp.float32), axis=0)
    first, second = total[40:48], total[48:56]
    lane = lax.broadcasted_iota(jnp.int32, (1, LANES), 1)
    row = second[0:1]

    def pick(k):
        mine = (lane == 32 + k) | (lane == 36 + k) | (lane == 40 + k)
        return jnp.sum(jnp.where(mine, row, 0.0), axis=1, keepdims=True)

    divisor = jnp.maximum(pick(0), 1.0)
    rest = jnp.concatenate([first[:, 32 * k : 32 * k + 32] for k in range(4)] + [second[:, :32]], axis=0)
    grad_ref[...] = jnp.concatenate([total[:40], rest], axis=1) / divisor
    stats_ref[...] = (
        jnp.where(lane == 0, -pick(3), jnp.where(lane == 1, pick(1), jnp.where(lane == 2, pick(2), 0.0)))
        / divisor
    )


def body(
    attn_output, readout_vectors, w_out, log_gap, magnitude, reward_sign, keep_mask, move_plan
):
    local_rows, width = attn_output.shape
    attn_t, readout_t = attn_output.T, readout_vectors.T
    dp_index = lax.axis_index("dp")
    live_total = jnp.sum(lax.dynamic_slice_in_dim(move_plan, dp_index, 1, 0))
    slot_ids = jnp.arange(local_rows, dtype=jnp.int32)
    weight = ((slot_ids < live_total).astype(jnp.int32) * keep_mask).astype(jnp.float32)
    advantage = (2 * reward_sign - 1).astype(jnp.float32) * magnitude.astype(jnp.float32)
    gap = log_gap.astype(jnp.float32)
    base_ratio = jnp.exp(gap)
    clip_high = ((advantage > 0) & (base_ratio > 1.0 + EPS_HIGH)).astype(jnp.float32)
    clip_low = ((advantage < 0) & (base_ratio < 1.0 - EPS_LOW)).astype(jnp.float32)
    signed = weight * advantage
    base = -LOSS_SCALE * signed * (1.0 - clip_high - clip_low)
    aux = jnp.pad(jnp.stack([gap, signed, base]).reshape(3, 6, LANES), ((0, 0), (0, 2), (0, 0)))
    four = jnp.stack(
        [jnp.sum(weight), jnp.sum(weight * clip_high), jnp.sum(weight * clip_low), jnp.float32(0)]
    )
    sums = jnp.pad(jnp.tile(four, 3), (32, LANES - 44))[None]

    readout_all = lax.all_gather(readout_t, "tensor", axis=0, tiled=True)
    projected = lax.dot_general(
        w_out, readout_all, (((1,), (0,)), ((), ())), preferred_element_type=jnp.float32
    )
    partial_shift = jnp.sum(projected * attn_t.astype(jnp.float32), axis=0)
    mine = jnp.pad(partial_shift.reshape(6, LANES), ((0, 2), (0, 0)))
    shifts = lax.all_to_all(
        jnp.broadcast_to(mine[None], (N_TENSOR, 8, LANES)), "tensor", 0, 0, tiled=True
    )
    chunks = pl.pallas_call(
        grad_kernel,
        grid=(N_TENSOR,),
        in_specs=[
            pl.BlockSpec((N_TENSOR, 8, LANES), lambda k: (0, 0, 0)),
            pl.BlockSpec((3, 8, LANES), lambda k: (0, 0, 0)),
            pl.BlockSpec((1, LANES), lambda k: (0, 0)),
            pl.BlockSpec((width, local_rows), lambda k: (0, 0)),
            pl.BlockSpec((width, local_rows), lambda k: (k, 0)),
        ],
        out_specs=pl.BlockSpec((4, CHUNK_ROWS, LANES), lambda k: (k, 0, 0)),
        out_shape=jax.ShapeDtypeStruct((N_DP, CHUNK_ROWS, LANES), jnp.bfloat16),
        scratch_shapes=[
            pltpu.VMEM((width, local_rows), jnp.bfloat16),
            pltpu.VMEM((8, LANES), jnp.float32),
        ],
        compiler_params=pltpu.CompilerParams(vmem_limit_bytes=24 << 20),
    )(shifts, aux, sums, attn_t, readout_all)
    received = lax.all_to_all(chunks, "dp", 0, 0, tiled=True)
    grad_t, stats = pl.pallas_call(
        finish_kernel,
        in_specs=[vmem_spec()],
        out_specs=[vmem_spec(), vmem_spec()],
        out_shape=[
            jax.ShapeDtypeStruct((40, width), jnp.float32),
            jax.ShapeDtypeStruct((1, LANES), jnp.float32),
        ],
        compiler_params=pltpu.CompilerParams(vmem_limit_bytes=24 << 20),
    )(received)
    return grad_t.T, stats[0, :3]


def solution(mesh):
    placed = (
        P("dp", "tensor"),
        P("dp", "tensor"),
        P("tensor", None),
        P("dp"),
        P("dp"),
        P("dp"),
        P("dp"),
        P(),
    )
    return jax.shard_map(
        body, mesh=mesh, in_specs=placed, out_specs=(P("tensor", "dp"), P()), check_vma=False
    )
```

time: 492 us -> 143 us (0.29)
  the two profiles are of different devices: /device:TPU:16 before, /device:TPU:4 now
where the time goes in v1:
time: 143 us
  waiting for transfers between devices  65.7 us (46%)
  blocking collectives  40.8 us (29%)
  between operations  14.1 us (10%)
  other arithmetic  6.02 us (4%)
  Pallas kernels  5.86 us (4%)
  starting transfers between devices  3.91 us (3%)
  local copies, waits for them, and re-layouts  3.43 us (2%)
  matrix products  2.95 us (2%)
    all_gather x1, waiting for transfers between devices, body(): readout_all = lax.all_gather(readout_t, 'tensor', axis=0, tiled=True)  57.2 us
    all_to_all x1, blocking collectives, body(): received = lax.all_to_all(chunks, 'dp', 0, 0, tiled=True)  40.8 us
    all_to_all x1, waiting for transfers between devices, body(): lax.all_to_all(jnp.broadcast_to(mine[None], (N_TENSOR, 8, LANES)), 'tenso...  7.79 us
    pallas_call x1, Pallas kernels, body(): pl.pallas_call(grad_kernel, grid=(N_TENSOR,), in_specs=[pl.BlockSpec((N_T...  5.07 us
    all_to_all x1, starting transfers between devices, body(): lax.all_to_all(jnp.broadcast_to(mine[None], (N_TENSOR, 8, LANES)), 'tenso...  3.88 us
    dot_general x1, matrix products, body(): lax.dot_general(w_out, readout_all, (((1,), (0,)), ((), ())), preferred_e...  2.95 us
  transfers between devices with their start and end apart: 2, of which 2 were waited for; matrix products, arithmetic and copies ran while one was open for 4% of the time, Pallas kernels for 0%

profile of v1, /device:TPU:4, one launch (start us, length us, event | category | flops | bytes accessed | tf_op | source)
XLA Modules:
  0.0 142.8 jit_solution(11157754485862958123)
XLA Ops:
  7.2 0.0 copy-start
  7.2 0.0 copy-start.2
  7.2 0.0 all-gather.2.cloned.1.call-start
  7.2 0.7 all-gather.2.cloned.1.call-update
  7.9 1.3 dynamic-slice_reduce_fusion
  9.3 2.0 %select_reduce_fusion.1 = (f32[]{:T(128)}, f32[]{:T(128)}, f32[]{:T(128)}, f32[1,6,128]{2,1,0:T(8,128)S(1)}, f32[1,6,128]{2,1,0:T(8,128)S(1)}) fusion(s32[768]{0:T(1024)} %param.14, s32[]{:T(128)} %dynamic-slice_reduce_fusion, bf16[768]{0:T(1024)(128)(2,1)} %param.11, bf16[768]{0:T(1024)(128)(2,1)} %param.12, s32[768]{0:T(1024)} %param.13), kind=kLoop, calls=%fused_computation.10 | loop fusion | flops 20733 | bytes 15376 | tf_op jit(solution)/shard_map/reduce_sum | solution.py:92
  11.3 2.0 %pad_maximum_fusion = f32[4]{0:T(128)S(1)} fusion(f32[1]{0:T(128)} %constant.31.clone.1, f32[1]{0:T(128)} %bitcast.8, f32[1]{0:T(128)} %bitcast.7, f32[1]{0:T(128)} %bitcast.6), kind=kLoop, calls=%fused_computation.20 | loop fusion | flops 12 | bytes 32 | tf_op jit(solution)/shard_map/stack | solution.py:91
  13.3 0.1 tile.10
  13.3 0.7 convert_bitcast_fusion
  14.0 57.2 %all-gather.2.cloned.1.call-done.readout_ref = bf16[2560,768]{1,0:T(8,128)(2,1)} async-done(((bf16[160,768]{1,0:T(8,128)(2,1)}), bf16[2560,768]{1,0:T(8,128)(2,1)}) %all-gather.2.cloned.1.call-update) | async-done | bytes 3932176 | tf_op jit(solution)/shard_map/all_gather | solution.py:96
  71.3 0.0 copy-done
  71.3 3.0 %fusion = f32[768]{0:T(1024)S(1)} fusion(bf16[160,2560]{1,0:T(8,128)(2,1)S(1)} %copy-done, bf16[2560,768]{1,0:T(8,128)(2,1)} %all-gather.2.cloned.1.call-done.readout_ref, bf16[768,160]{0,1:T(8,128)(2,1)} %param.8), kind=kOutput, calls=%fused_computation.1 | convolution fusion | flops 629513472 | bytes 5000192 | tf_op jit(solution)/shard_map/dot_general | solution.py:97
  74.3 0.6 broadcast_in_dim.4
  74.9 3.9 %all-to-all-start = ((f32[16,8,128]{2,1,0:T(8,128)}), f32[16,8,128]{2,1,0:T(8,128)S(1)}, u32[]{:S(2)}, u32[]{:S(2)}) async-start(f32[16,8,128]{2,1,0:T(8,128)} %broadcast_in_dim.4), calls=%async_computation | async-start | bytes 131072 | tf_op jit(solution)/shard_map/all_to_all | solution.py:102
  78.8 0.1 pad_bitcast_fusion.sums_ref
  78.8 7.8 %all-to-all-done.recv_ref = f32[16,8,128]{2,1,0:T(8,128)S(1)} async-done(((f32[16,8,128]{2,1,0:T(8,128)}), f32[16,8,128]{2,1,0:T(8,128)S(1)}, u32[]{:S(2)}, u32[]{:S(2)}) %all-to-all-start) | async-done | bytes 65568 | tf_op jit(solution)/shard_map/all_to_all | solution.py:102
  86.6 0.0 copy-done.2
  86.6 0.0 copy-start.1
  86.6 2.1 %copy-done.1 = bf16[2560,768]{1,0:T(8,128)(2,1)S(1)} copy-done((bf16[2560,768]{1,0:T(8,128)(2,1)S(1)}, bf16[2560,768]{1,0:T(8,128)(2,1)}, u32[]{:S(2)}) %copy-start.1) | copy-done | bytes 3932184
  88.8 5.1 %shard_map.95 = bf16[64,56,128]{2,1,0:T(8,128)(2,1)S(1)} custom-call(f32[16,8,128]{2,1,0:T(8,128)S(1)} %all-to-all-done.recv_ref, f32[3,8,128]{2,1,0:T(8,128)S(1)} %select_maximum_fusion.aux_ref, f32[1,128]{1,0:T(1,128)S(1)} %pad_bitcast_fusion.sums_ref, bf16[160,768]{1,0:T(8,128)(2,1)S(1)} %bitcast.20, bf16[2560,768]{1,0:T(8,128)(2,1)S(1)} %copy-done.1), custom_call_target="tpu_custom_call" | custom-call | tf_op jit(solution)/shard_map/pallas_call | solution.py:105
  93.8 40.8 %all_to_all.10.recv_ref = bf16[64,56,128]{2,1,0:T(8,128)(2,1)S(1)} all-to-all(bf16[64,56,128]{2,1,0:T(8,128)(2,1)S(1)} %shard_map.95), channel_id=1, replica_groups=mesh['dp'=64,'tensor'=16] {'dp'}, dimensions={0} | all-to-all | bytes 1835008 | tf_op jit(solution)/shard_map/all_to_all | solution.py:123
  134.6 0.8 shard_map.96
  135.4 0.5 slice_bitcast_fusion
  (3 shorter events, 0.0 us)
Async XLA Ops:
  7.2 64.1 %copy-start = (bf16[160,2560]{1,0:T(8,128)(2,1)S(1)}, bf16[160,2560]{1,0:T(8,128)(2,1)}, u32[]{:S(2)}) copy-start(bf16[160,2560]{1,0:T(8,128)(2,1)} %param.10) | copy-start | bytes 2457604
  7.2 79.5 %copy-start.2 = (bf16[768,160]{0,1:T(8,128)(2,1)S(1)}, bf16[768,160]{0,1:T(8,128)(2,1)}, u32[]{:S(2)}) copy-start(bf16[768,160]{0,1:T(8,128)(2,1)} %param.8) | copy-start | bytes 737284
  7.2 64.1 %all-gather.2.cloned.1.call-start = ((), (), s32[]{:S(2)}) async-start(), calls=%async_computation.2 | async-start | bytes 4177920 | tf_op jit(solution)/shard_map/all_gather | solution.py:96
  74.9 11.8 %all-to-all-start = ((f32[16,8,128]{2,1,0:T(8,128)}), f32[16,8,128]{2,1,0:T(8,128)S(1)}, u32[]{:S(2)}, u32[]{:S(2)}) async-start(f32[16,8,128]{2,1,0:T(8,128)} %broadcast_in_dim.4), calls=%async_computation | async-start | bytes 131072 | tf_op jit(solution)/shard_map/all_to_all | solution.py:102
  86.6 2.1 %copy-start.1 = (bf16[2560,768]{1,0:T(8,128)(2,1)S(1)}, bf16[2560,768]{1,0:T(8,128)(2,1)}, u32[]{:S(2)}) copy-start(bf16[2560,768]{1,0:T(8,128)(2,1)} %all-gather.2.cloned.1.call-done.readout_ref) | copy-start | bytes 11796484
Sparse Core Ops, SparseCore 0:
  10.7 60.5 all-gather.1

commit v2 on v1

v2 whole, which is shorter than its diff:
```python
import jax
import jax.numpy as jnp
from jax import lax
from jax.experimental import pallas as pl
from jax.experimental.pallas import tpu as pltpu
from jax.sharding import PartitionSpec as P

EPS_LOW = 0.2
EPS_HIGH = 0.28
LOSS_SCALE = 16384.0
N_DP = 64
N_TENSOR = 16
CHUNK_ROWS = 56
LANES = 128
N_Z = 8
NEAR = 7
STEPS = (0, -1, 1, -2, 2, -3, 3)


def vmem_spec():
    return pl.BlockSpec(memory_space=pltpu.VMEM)


def piece_index(place):
    device = lax.axis_index("tensor")
    core = device & 1
    if place < NEAR:
        step, side = STEPS[place], core
    elif place < 2 * NEAR:
        step, side = STEPS[place - NEAR], 1 - core
    else:
        step, side = 4, (core, 1 - core)[place - 2 * NEAR]
    return (((device >> 1) + N_Z + step) & (N_Z - 1)) * 2 + side


def prepare_kernel(w_ref, gap_ref, size_ref, sign_ref, keep_ref, plan_ref, out_ref, aux_ref, sums_ref):
    width = out_ref.shape[2]
    for k in range(N_TENSOR):
        out_ref[k] = w_ref[:, width * k : width * k + width]
    owner = lax.broadcasted_iota(jnp.int32, plan_ref.shape, 0)
    live_total = jnp.sum(jnp.where(owner == lax.axis_index("dp"), plan_ref[...], 0))
    shape = gap_ref.shape
    slot_ids = lax.broadcasted_iota(jnp.int32, shape, 0) * LANES + lax.broadcasted_iota(jnp.int32, shape, 1)
    weight = jnp.where(slot_ids < live_total, keep_ref[...], 0).astype(jnp.float32)
    gap = gap_ref[...]
    advantage = (2 * sign_ref[...] - 1).astype(jnp.float32) * size_ref[...]
    base_ratio = jnp.exp(gap)
    clip_high = jnp.where((advantage > 0) & (base_ratio > 1.0 + EPS_HIGH), 1.0, 0.0)
    clip_low = jnp.where((advantage < 0) & (base_ratio < 1.0 - EPS_LOW), 1.0, 0.0)
    signed = weight * advantage
    zeros = jnp.zeros((2, LANES), jnp.float32)
    base = -LOSS_SCALE * signed * (1.0 - clip_high - clip_low)
    for k, value in enumerate((gap, signed, base)):
        aux_ref[k] = jnp.concatenate([value, zeros], axis=0)
    lane = lax.broadcasted_iota(jnp.int32, (8, LANES), 1)
    which = jnp.where((lane >= 32) & (lane < 44), lane & 3, 3)
    count, high, low = jnp.sum(weight), jnp.sum(weight * clip_high), jnp.sum(weight * clip_low)
    sums_ref[...] = jnp.where(
        which == 0, count, jnp.where(which == 1, high, jnp.where(which == 2, low, 0.0))
    )


def project(w_ref, places, pieces):
    total = None
    for place, piece in zip(places, pieces):
        product = jnp.dot(w_ref[piece_index(place)], piece, preferred_element_type=jnp.float32)
        total = product if total is None else total + product
    return total


def first_kernel(w_ref, mine_ref, out_ref):
    width = w_ref.shape[1]
    pieces = [mine_ref[width * k : width * k + width] for k in range(NEAR)]
    out_ref[...] = project(w_ref, range(NEAR), pieces)


def shift_kernel(w_ref, attn_ref, first_ref, other_ref, far_ref, far_other_ref, out_ref):
    width = w_ref.shape[1]
    pieces = [other_ref[width * k : width * k + width] for k in range(NEAR)]
    pieces += [far_ref[...], far_other_ref[...]]
    total = first_ref[...] + project(w_ref, range(NEAR, N_TENSOR), pieces)
    row = jnp.sum(total * attn_ref[...].astype(jnp.float32), axis=0, keepdims=True)
    rows = [row[:, LANES * r : LANES * r + LANES] for r in range(6)]
    block = jnp.concatenate(rows + [jnp.zeros((2, LANES), jnp.float32)], axis=0)
    for k in range(N_TENSOR):
        out_ref[k] = block


def grad_kernel(
    recv_ref,
    aux_ref,
    sums_ref,
    attn_ref,
    mine_ref,
    other_ref,
    far_ref,
    far_other_ref,
    out_ref,
):
    width = attn_ref.shape[0]
    shift = jnp.sum(recv_ref[...], axis=0)
    gap, signed, base = aux_ref[0], aux_ref[1], aux_ref[2]
    ratio = jnp.exp(gap + shift)
    loss = jnp.sum(
        jnp.minimum(ratio * signed, jnp.clip(ratio, 1.0 - EPS_LOW, 1.0 + EPS_HIGH) * signed)
    )
    coefficient = base * ratio
    row = jnp.concatenate([coefficient[r : r + 1] for r in range(6)], axis=1)
    scaled = (attn_ref[...].astype(jnp.float32) * row).astype(jnp.bfloat16)
    lane = lax.broadcasted_iota(jnp.int32, (8, LANES), 1)
    is_loss = (lane == 35) | (lane == 39) | (lane == 43)
    value = jnp.where(is_loss, loss, sums_ref[...])
    high = value.astype(jnp.bfloat16).astype(jnp.float32)
    middle = (value - high).astype(jnp.bfloat16).astype(jnp.float32)
    low = value - high - middle
    stats = jnp.where(lane < 36, high, jnp.where(lane < 40, middle, low))[:, 32:]
    for place in range(N_TENSOR):
        if place < NEAR:
            piece = mine_ref[width * place : width * place + width]
        elif place < 2 * NEAR:
            k = place - NEAR
            piece = other_ref[width * k : width * k + width]
        else:
            piece = (far_ref, far_other_ref)[place - 2 * NEAR][...]
        product = lax.dot_general(
            piece, scaled, (((1,), (1,)), ((), ())), preferred_element_type=jnp.float32
        )
        block = piece_index(place)
        for q in range(4):
            part = product[40 * q : 40 * q + 40]
            rest = part[:, LANES:]
            first = jnp.concatenate([rest[8 * k : 8 * k + 8] for k in range(4)], axis=1)
            second = jnp.concatenate([rest[32:40], stats], axis=1)
            out_ref[4 * block + q] = jnp.concatenate([part[:, :LANES], first, second], axis=0).astype(
                jnp.bfloat16
            )


def finish_kernel(recv_ref, grad_ref, stats_ref):
    total = jnp.sum(recv_ref[...].astype(jnp.float32), axis=0)
    first, second = total[40:48], total[48:56]
    lane = lax.broadcasted_iota(jnp.int32, (1, LANES), 1)
    row = second[0:1]

    def pick(k):
        mine = (lane == 32 + k) | (lane == 36 + k) | (lane == 40 + k)
        return jnp.sum(jnp.where(mine, row, 0.0), axis=1, keepdims=True)

    divisor = jnp.maximum(pick(0), 1.0)
    rest = jnp.concatenate([first[:, 32 * k : 32 * k + 32] for k in range(4)] + [second[:, :32]], axis=0)
    grad_ref[...] = jnp.concatenate([total[:40], rest], axis=1) / divisor
    stats_ref[...] = (
        jnp.where(lane == 0, -pick(3), jnp.where(lane == 1, pick(1), jnp.where(lane == 2, pick(2), 0.0)))
        / divisor
    )


def body(
    attn_output, readout_vectors, w_out, log_gap, magnitude, reward_sign, keep_mask, move_plan
):
    local_rows, width = attn_output.shape
    attn_t, readout_t = attn_output.T, readout_vectors.T
    up, down, cross, swap = [], [], [], []
    for z in range(N_Z):
        for c in range(2):
            up.append((2 * z + c, 2 * ((z + 1) % N_Z) + c))
            down.append((2 * ((z + 1) % N_Z) + c, 2 * z + c))
            cross.append((2 * ((z + 1) % N_Z) + 1 - c, 2 * z + c))
            swap.append((2 * z + 1 - c, 2 * z + c))
    rising, falling, nearby = readout_t, readout_t, [readout_t]
    for _ in range(3):
        rising = lax.ppermute(rising, "tensor", up)
        falling = lax.ppermute(falling, "tensor", down)
        nearby += [rising, falling]
    far_mine = lax.ppermute(rising, "tensor", up)
    far_other = lax.ppermute(falling, "tensor", cross)
    mine = jnp.concatenate(nearby, axis=0)
    other = lax.ppermute(mine, "tensor", swap)

    params = pltpu.CompilerParams(vmem_limit_bytes=24 << 20)
    tiled = (local_rows // LANES, LANES)
    w_blocks, aux, sums = pl.pallas_call(
        prepare_kernel,
        in_specs=[vmem_spec()] * 6,
        out_specs=[vmem_spec()] * 3,
        out_shape=[
            jax.ShapeDtypeStruct((N_TENSOR, width, width), w_out.dtype),
            jax.ShapeDtypeStruct((3, 8, LANES), jnp.float32),
            jax.ShapeDtypeStruct((8, LANES), jnp.float32),
        ],
        compiler_params=params,
    )(
        w_out,
        log_gap.astype(jnp.float32).reshape(tiled),
        magnitude.astype(jnp.float32).reshape(tiled),
        reward_sign.reshape(tiled),
        keep_mask.reshape(tiled),
        move_plan,
    )
    first = pl.pallas_call(
        first_kernel,
        in_specs=[vmem_spec()] * 2,
        out_specs=vmem_spec(),
        out_shape=jax.ShapeDtypeStruct((width, local_rows), jnp.float32),
        compiler_params=params,
    )(w_blocks, mine)
    partial_shift = pl.pallas_call(
        shift_kernel,
        in_specs=[vmem_spec()] * 6,
        out_specs=vmem_spec(),
        out_shape=jax.ShapeDtypeStruct((N_TENSOR, 8, LANES), jnp.float32),
        compiler_params=params,
    )(w_blocks, attn_t, first, other, far_mine, far_other)
    shifts = lax.all_to_all(partial_shift, "tensor", 0, 0, tiled=True)
    chunks = pl.pallas_call(
        grad_kernel,
        in_specs=[vmem_spec()] * 8,
        out_specs=vmem_spec(),
        out_shape=jax.ShapeDtypeStruct((N_DP, CHUNK_ROWS, LANES), jnp.bfloat16),
        compiler_params=params,
    )(shifts, aux, sums, attn_t, mine, other, far_mine, far_other)
    received = lax.all_to_all(chunks, "dp", 0, 0, tiled=True)
    grad_t, stats = pl.pallas_call(
        finish_kernel,
        in_specs=[vmem_spec()],
        out_specs=[vmem_spec(), vmem_spec()],
        out_shape=[
            jax.ShapeDtypeStruct((40, width), jnp.float32),
            jax.ShapeDtypeStruct((1, LANES), jnp.float32),
        ],
        compiler_params=pltpu.CompilerParams(vmem_limit_bytes=24 << 20),
    )(received)
    return grad_t.T, stats[0, :3]


def solution(mesh):
    placed = (
        P("dp", "tensor"),
        P("dp", "tensor"),
        P("tensor", None),
        P("dp"),
        P("dp"),
        P("dp"),
        P("dp"),
        P(),
    )
    return jax.shard_map(
        body, mesh=mesh, in_specs=placed, out_specs=(P("tensor", "dp"), P()), check_vma=False
    )
```

time: 143 us -> 119 us (0.83)
  waiting for transfers between devices: 65.7 us -> 14.5 us
  starting transfers between devices: 3.91 us -> 43 us
  blocking collectives: 40.8 us -> 54.3 us
  between operations: 14.1 us -> 0.91 us
  other arithmetic: 6.02 us -> 0.01 us
  matrix products: 2.95 us -> 0 us
  Pallas kernels: 5.86 us -> 3.88 us
  local copies, waits for them, and re-layouts: 3.43 us -> 1.61 us
    all_gather x1 -> x0, waiting for transfers between devices: 57.2 us -> none  [body(): readout_all = lax.all_gather(readout_t, 'tensor', axis=0, tiled=True)]
    ppermute x0 -> x9, starting transfers between devices: none -> 43 us  [the longest x3 24.3 us: body(): falling = lax.ppermute(falling, 'tensor', down)]
    ppermute x0 -> x9, waiting for transfers between devices: none -> 14.5 us  [the longest x3 8.56 us: body(): rising = lax.ppermute(rising, 'tensor', up)]
    all_to_all x0 -> x1, blocking collectives: none -> 12.7 us  [body(): shifts = lax.all_to_all(partial_shift, 'tensor', 0, 0, tiled=True)]
    all_to_all x1 -> x0, waiting for transfers between devices: 7.79 us -> none  [body(): lax.all_to_all(jnp.broadcast_to(mine[None], (N_TENSOR, 8, LANES)), 'tenso...]
    all_to_all x1 -> x0, starting transfers between devices: 3.88 us -> none  [body(): lax.all_to_all(jnp.broadcast_to(mine[None], (N_TENSOR, 8, LANES)), 'tenso...]
    reduce_sum x2 -> x0, other arithmetic: 3.37 us -> none  [the longest x1 2.04 us: body(): jnp.sum(weight * clip_high)]
    dot_general x1 -> x0, matrix products: 2.95 us -> none  [body(): lax.dot_general(w_out, readout_all, (((1,), (0,)), ((), ())), preferred_e...]
  transfers between devices with their start and end apart: 2 -> 9, of which waited for: 2 -> 6; matrix products, arithmetic and copies ran while one was open for 4% -> 1% of each run, Pallas kernels for 0% -> 1%
where the time goes in v2:
time: 119 us; the launch traced here: 118 us
  blocking collectives  54.3 us (46%)
  starting transfers between devices  43 us (36%)
  waiting for transfers between devices  14.5 us (12%)
  Pallas kernels  3.88 us (3%)
  local copies, waits for them, and re-layouts  1.61 us (1%)
    all_to_all x1, blocking collectives, body(): received = lax.all_to_all(chunks, 'dp', 0, 0, tiled=True)  41.6 us
    ppermute x3, starting transfers between devices, body(): falling = lax.ppermute(falling, 'tensor', down)  24.3 us
    all_to_all x1, blocking collectives, body(): shifts = lax.all_to_all(partial_shift, 'tensor', 0, 0, tiled=True)  12.7 us
    ppermute x3, starting transfers between devices, body(): rising = lax.ppermute(rising, 'tensor', up)  9.14 us
    ppermute x3, waiting for transfers between devices, body(): rising = lax.ppermute(rising, 'tensor', up)  8.56 us
    ppermute x1, starting transfers between devices, body(): far_other = lax.ppermute(falling, 'tensor', cross)  5.7 us
    ppermute x1, waiting for transfers between devices, body(): far_mine = lax.ppermute(rising, 'tensor', up)  3.45 us
  transfers between devices with their start and end apart: 9, of which 6 were waited for; matrix products, arithmetic and copies ran while one was open for 1% of the time, Pallas kernels for 1%

profile of v2, /device:TPU:4, one launch (start us, length us, event | category | flops | bytes accessed | tf_op | source)
XLA Modules:
  0.0 118.2 jit_solution(15672543209874982152)
XLA Ops:
  0.6 0.0 copy-start.5
  0.6 0.0 copy-start.6
  0.7 0.0 copy-start.1
  0.7 0.0 copy-start.2
  0.7 5.3 %collective-permute-start = (bf16[160,768]{1,0:T(8,128)(2,1)}, bf16[160,768]{1,0:T(8,128)(2,1)S(1)}, u32[]{:S(2)}, u32[]{:S(2)}) collective-permute-start(bf16[160,768]{1,0:T(8,128)(2,1)} %bitcast.18), channel_id=1, source_target_pairs={{0,2},{1,3},{2,4},{3,5},{4,6},{5,7},{6,8},{7,9},{8,10},{9,11},{10,... | collective-permute-start | bytes 737288 | tf_op jit(solution)/shard_map/ppermute | solution.py:172
  6.0 14.0 %collective-permute-start.1 = (bf16[160,768]{1,0:T(8,128)(2,1)}, bf16[160,768]{1,0:T(8,128)(2,1)S(1)}, u32[]{:S(2)}, u32[]{:S(2)}) collective-permute-start(bf16[160,768]{1,0:T(8,128)(2,1)} %bitcast.19), channel_id=1, source_target_pairs={{2,0},{3,1},{4,2},{5,3},{6,4},{7,5},{8,6},{9,7},{10,8},{11,9},{12,... | collective-permute-start | bytes 737288 | tf_op jit(solution)/shard_map/ppermute | solution.py:173
  20.1 4.2 %collective-permute-done = bf16[160,768]{1,0:T(8,128)(2,1)S(1)} collective-permute-done((bf16[160,768]{1,0:T(8,128)(2,1)}, bf16[160,768]{1,0:T(8,128)(2,1)S(1)}, u32[]{:S(2)}, u32[]{:S(2)}) %collective-permute-start) | collective-permute-done | bytes 245792 | tf_op jit(solution)/shard_map/ppermute | solution.py:172
  24.3 1.9 %collective-permute-start.2 = (bf16[160,768]{1,0:T(8,128)(2,1)S(1)}, bf16[160,768]{1,0:T(8,128)(2,1)S(1)}, u32[]{:S(2)}, u32[]{:S(2)}) collective-permute-start(bf16[160,768]{1,0:T(8,128)(2,1)S(1)} %collective-permute-done), channel_id=1, source_target_pairs={{0,2},{1,3},{2,4},{3,5},{4,6},{5,7},{6,8},{7,9},{8,10},{9,11},{10,... | collective-permute-start | bytes 737288 | tf_op jit(solution)/shard_map/ppermute | solution.py:172
  26.2 0.0 collective-permute-done.1
  26.2 5.1 %collective-permute-start.3 = (bf16[160,768]{1,0:T(8,128)(2,1)S(1)}, bf16[160,768]{1,0:T(8,128)(2,1)S(1)}, u32[]{:S(2)}, u32[]{:S(2)}) collective-permute-start(bf16[160,768]{1,0:T(8,128)(2,1)S(1)} %collective-permute-done.1), channel_id=1, source_target_pairs={{2,0},{3,1},{4,2},{5,3},{6,4},{7,5},{8,6},{9,7},{10,8},{11,9},{12,... | collective-permute-start | bytes 737288 | tf_op jit(solution)/shard_map/ppermute | solution.py:173
  31.4 1.0 constant_dynamic-update-slice_fusion.6
  32.4 2.2 %collective-permute-done.2 = bf16[160,768]{1,0:T(8,128)(2,1)S(1)} collective-permute-done((bf16[160,768]{1,0:T(8,128)(2,1)S(1)}, bf16[160,768]{1,0:T(8,128)(2,1)S(1)}, u32[]{:S(2)}, u32[]{:S(2)}) %collective-permute-start.2) | collective-permute-done | bytes 245792 | tf_op jit(solution)/shard_map/ppermute | solution.py:172
  34.5 1.9 %collective-permute-start.4 = (bf16[160,768]{1,0:T(8,128)(2,1)S(1)}, bf16[160,768]{1,0:T(8,128)(2,1)S(1)}, u32[]{:S(2)}, u32[]{:S(2)}) collective-permute-start(bf16[160,768]{1,0:T(8,128)(2,1)S(1)} %collective-permute-done.2), channel_id=1, source_target_pairs={{0,2},{1,3},{2,4},{3,5},{4,6},{5,7},{6,8},{7,9},{8,10},{9,11},{10,... | collective-permute-start | bytes 737288 | tf_op jit(solution)/shard_map/ppermute | solution.py:172
  36.5 0.0 collective-permute-done.3
  36.5 5.1 %collective-permute-start.5 = (bf16[160,768]{1,0:T(8,128)(2,1)S(1)}, bf16[160,768]{1,0:T(8,128)(2,1)S(1)}, u32[]{:S(2)}, u32[]{:S(2)}) collective-permute-start(bf16[160,768]{1,0:T(8,128)(2,1)S(1)} %collective-permute-done.3), channel_id=1, source_target_pairs={{2,0},{3,1},{4,2},{5,3},{6,4},{7,5},{8,6},{9,7},{10,8},{11,9},{12,... | collective-permute-start | bytes 737288 | tf_op jit(solution)/shard_map/ppermute | solution.py:173
  41.7 2.2 %collective-permute-done.4 = bf16[160,768]{1,0:T(8,128)(2,1)S(1)} collective-permute-done((bf16[160,768]{1,0:T(8,128)(2,1)S(1)}, bf16[160,768]{1,0:T(8,128)(2,1)S(1)}, u32[]{:S(2)}, u32[]{:S(2)}) %collective-permute-start.4) | collective-permute-done | bytes 245792 | tf_op jit(solution)/shard_map/ppermute | solution.py:172
  43.9 1.5 %collective-permute-done.5 = bf16[160,768]{1,0:T(8,128)(2,1)S(1)} collective-permute-done((bf16[160,768]{1,0:T(8,128)(2,1)S(1)}, bf16[160,768]{1,0:T(8,128)(2,1)S(1)}, u32[]{:S(2)}, u32[]{:S(2)}) %collective-permute-start.5) | collective-permute-done | bytes 245792 | tf_op jit(solution)/shard_map/ppermute | solution.py:173
  45.3 1.9 %collective-permute-start.6 = (bf16[1120,768]{1,0:T(8,128)(2,1)S(1)}, bf16[1120,768]{1,0:T(8,128)(2,1)S(1)}, u32[]{:S(2)}, u32[]{:S(2)}) collective-permute-start(bf16[1120,768]{1,0:T(8,128)(2,1)S(1)} %constant_dynamic-update-slice_fusion.mine_ref), channel_id=1, source_target_pairs={{1,0},{0,1},{3,2},{2,3},{5,4},{4,5},{7,6},{6,7},{9,8},{8,9},{11,10... | collective-permute-start | bytes 5160968 | tf_op jit(solution)/shard_map/ppermute | solution.py:178
  47.3 1.9 %collective-permute-start.7 = (bf16[160,768]{1,0:T(8,128)(2,1)S(1)}, bf16[160,768]{1,0:T(8,128)(2,1)S(1)}, u32[]{:S(2)}, u32[]{:S(2)}) collective-permute-start(bf16[160,768]{1,0:T(8,128)(2,1)S(1)} %collective-permute-done.4), channel_id=1, source_target_pairs={{0,2},{1,3},{2,4},{3,5},{4,6},{5,7},{6,8},{7,9},{8,10},{9,11},{10,... | collective-permute-start | bytes 737288 | tf_op jit(solution)/shard_map/ppermute | solution.py:175
  49.2 5.7 %collective-permute-start.8 = (bf16[160,768]{1,0:T(8,128)(2,1)S(1)}, bf16[160,768]{1,0:T(8,128)(2,1)S(1)}, u32[]{:S(2)}, u32[]{:S(2)}) collective-permute-start(bf16[160,768]{1,0:T(8,128)(2,1)S(1)} %collective-permute-done.5), channel_id=1, source_target_pairs={{3,0},{2,1},{5,2},{4,3},{7,4},{6,5},{9,6},{8,7},{11,8},{10,9},{13,... | collective-permute-start | bytes 737288 | tf_op jit(solution)/shard_map/ppermute | solution.py:176
  55.0 0.4 shard_map.95
  55.4 0.0 copy-start
  55.4 0.6 shard_map.96.first_ref
  56.0 3.4 %collective-permute-done.7.far_ref = bf16[160,768]{1,0:T(8,128)(2,1)S(1)} collective-permute-done((bf16[160,768]{1,0:T(8,128)(2,1)S(1)}, bf16[160,768]{1,0:T(8,128)(2,1)S(1)}, u32[]{:S(2)}, u32[]{:S(2)}) %collective-permute-start.7) | collective-permute-done | bytes 245792 | tf_op jit(solution)/shard_map/ppermute | solution.py:175
  59.5 1.1 collective-permute-done.8.far_other_ref
  60.6 0.0 collective-permute-done.6.other_ref
  60.6 0.7 shard_map.97
  61.3 12.7 %all_to_all.10.recv_ref = f32[16,8,128]{2,1,0:T(8,128)S(1)} all-to-all(f32[16,8,128]{2,1,0:T(8,128)S(1)} %shard_map.97), channel_id=1, replica_groups=mesh['dp'=64,'tensor'=16] {'tensor'}, dimensions={0} | all-to-all | bytes 131072 | tf_op jit(solution)/shard_map/all_to_all | solution.py:214
  74.0 1.3 %shard_map.98 = bf16[64,56,128]{2,1,0:T(8,128)(2,1)S(1)} custom-call(f32[16,8,128]{2,1,0:T(8,128)S(1)} %all_to_all.10.recv_ref, f32[3,8,128]{2,1,0:T(8,128)S(1)} %get-tuple-element.8.aux_ref, f32[8,128]{1,0:T(8,128)S(1)} %get-tuple-element.9.sums_ref, bf16[160,768]{1,0:T(8,128)(2,1)S(1)} %bitcast.15, ...), custom_call_target="tpu_custom_call" | custom-call | tf_op jit(solution)/shard_map/pallas_call | solution.py:215
  75.3 41.6 %all_to_all.11.recv_ref = bf16[64,56,128]{2,1,0:T(8,128)(2,1)S(1)} all-to-all(bf16[64,56,128]{2,1,0:T(8,128)(2,1)S(1)} %shard_map.98), channel_id=1, replica_groups=mesh['dp'=64,'tensor'=16] {'dp'}, dimensions={0} | all-to-all | bytes 1835008 | tf_op jit(solution)/shard_map/all_to_all | solution.py:222
  116.9 0.8 shard_map.99
  117.7 0.5 slice_bitcast_fusion
  (16 shorter events, 0.1 us)
Async XLA Ops:
  0.6 54.3 %copy-start.5 = (bf16[768]{0:T(1024)(128)(2,1)S(1)}, bf16[768]{0:T(1024)(128)(2,1)}, u32[]{:S(2)}) copy-start(bf16[768]{0:T(1024)(128)(2,1)} %param.12) | copy-start | bytes 4612
  0.6 54.3 %copy-start.6 = (bf16[768]{0:T(1024)(128)(2,1)S(1)}, bf16[768]{0:T(1024)(128)(2,1)}, u32[]{:S(2)}) copy-start(bf16[768]{0:T(1024)(128)(2,1)} %param.11) | copy-start | bytes 4612
  0.7 54.3 %copy-start.1 = (bf16[160,2560]{1,0:T(8,128)(2,1)S(1)}, bf16[160,2560]{1,0:T(8,128)(2,1)}, u32[]{:S(2)}) copy-start(bf16[160,2560]{1,0:T(8,128)(2,1)} %w_ref.1) | copy-start | bytes 2457604
  0.7 54.3 %copy-start.2 = (s32[64,64]{1,0:T(8,128)S(1)}, s32[64,64]{1,0:T(8,128)}, u32[]{:S(2)}) copy-start(s32[64,64]{1,0:T(8,128)} %plan_ref.1) | copy-start | bytes 49156
  0.7 54.3 %copy-start.3 = (s32[768]{0:T(1024)S(1)}, s32[768]{0:T(1024)}, u32[]{:S(2)}) copy-start(s32[768]{0:T(1024)} %param.13) | copy-start | bytes 9220
  0.7 54.3 %copy-start.4 = (s32[768]{0:T(1024)S(1)}, s32[768]{0:T(1024)}, u32[]{:S(2)}) copy-start(s32[768]{0:T(1024)} %param.14) | copy-start | bytes 9220
  0.7 23.6 %collective-permute-start = (bf16[160,768]{1,0:T(8,128)(2,1)}, bf16[160,768]{1,0:T(8,128)(2,1)S(1)}, u32[]{:S(2)}, u32[]{:S(2)}) collective-permute-start(bf16[160,768]{1,0:T(8,128)(2,1)} %bitcast.18), channel_id=1, source_target_pairs={{0,2},{1,3},{2,4},{3,5},{4,6},{5,7},{6,8},{7,9},{8,10},{9,11},{10,... | collective-permute-start | bytes 737288 | tf_op jit(solution)/shard_map/ppermute | solution.py:172
  6.0 20.2 %collective-permute-start.1 = (bf16[160,768]{1,0:T(8,128)(2,1)}, bf16[160,768]{1,0:T(8,128)(2,1)S(1)}, u32[]{:S(2)}, u32[]{:S(2)}) collective-permute-start(bf16[160,768]{1,0:T(8,128)(2,1)} %bitcast.19), channel_id=1, source_target_pairs={{2,0},{3,1},{4,2},{5,3},{6,4},{7,5},{8,6},{9,7},{10,8},{11,9},{12,... | collective-permute-start | bytes 737288 | tf_op jit(solution)/shard_map/ppermute | solution.py:173
  24.3 10.2 %collective-permute-start.2 = (bf16[160,768]{1,0:T(8,128)(2,1)S(1)}, bf16[160,768]{1,0:T(8,128)(2,1)S(1)}, u32[]{:S(2)}, u32[]{:S(2)}) collective-permute-start(bf16[160,768]{1,0:T(8,128)(2,1)S(1)} %collective-permute-done), channel_id=1, source_target_pairs={{0,2},{1,3},{2,4},{3,5},{4,6},{5,7},{6,8},{7,9},{8,10},{9,11},{10,... | collective-permute-start | bytes 737288 | tf_op jit(solution)/shard_map/ppermute | solution.py:172
  26.2 10.3 %collective-permute-start.3 = (bf16[160,768]{1,0:T(8,128)(2,1)S(1)}, bf16[160,768]{1,0:T(8,128)(2,1)S(1)}, u32[]{:S(2)}, u32[]{:S(2)}) collective-permute-start(bf16[160,768]{1,0:T(8,128)(2,1)S(1)} %collective-permute-done.1), channel_id=1, source_target_pairs={{2,0},{3,1},{4,2},{5,3},{6,4},{7,5},{8,6},{9,7},{10,8},{11,9},{12,... | collective-permute-start | bytes 737288 | tf_op jit(solution)/shard_map/ppermute | solution.py:173
  34.5 9.3 %collective-permute-start.4 = (bf16[160,768]{1,0:T(8,128)(2,1)S(1)}, bf16[160,768]{1,0:T(8,128)(2,1)S(1)}, u32[]{:S(2)}, u32[]{:S(2)}) collective-permute-start(bf16[160,768]{1,0:T(8,128)(2,1)S(1)} %collective-permute-done.2), channel_id=1, source_target_pairs={{0,2},{1,3},{2,4},{3,5},{4,6},{5,7},{6,8},{7,9},{8,10},{9,11},{10,... | collective-permute-start | bytes 737288 | tf_op jit(solution)/shard_map/ppermute | solution.py:172
  36.5 8.8 %collective-permute-start.5 = (bf16[160,768]{1,0:T(8,128)(2,1)S(1)}, bf16[160,768]{1,0:T(8,128)(2,1)S(1)}, u32[]{:S(2)}, u32[]{:S(2)}) collective-permute-start(bf16[160,768]{1,0:T(8,128)(2,1)S(1)} %collective-permute-done.3), channel_id=1, source_target_pairs={{2,0},{3,1},{4,2},{5,3},{6,4},{7,5},{8,6},{9,7},{10,8},{11,9},{12,... | collective-permute-start | bytes 737288 | tf_op jit(solution)/shard_map/ppermute | solution.py:173
  45.3 15.2 %collective-permute-start.6 = (bf16[1120,768]{1,0:T(8,128)(2,1)S(1)}, bf16[1120,768]{1,0:T(8,128)(2,1)S(1)}, u32[]{:S(2)}, u32[]{:S(2)}) collective-permute-start(bf16[1120,768]{1,0:T(8,128)(2,1)S(1)} %constant_dynamic-update-slice_fusion.mine_ref), channel_id=1, source_target_pairs={{1,0},{0,1},{3,2},{2,3},{5,4},{4,5},{7,6},{6,7},{9,8},{8,9},{11,10... | collective-permute-start | bytes 5160968 | tf_op jit(solution)/shard_map/ppermute | solution.py:178
  47.3 12.2 %collective-permute-start.7 = (bf16[160,768]{1,0:T(8,128)(2,1)S(1)}, bf16[160,768]{1,0:T(8,128)(2,1)S(1)}, u32[]{:S(2)}, u32[]{:S(2)}) collective-permute-start(bf16[160,768]{1,0:T(8,128)(2,1)S(1)} %collective-permute-done.4), channel_id=1, source_target_pairs={{0,2},{1,3},{2,4},{3,5},{4,6},{5,7},{6,8},{7,9},{8,10},{9,11},{10,... | collective-permute-start | bytes 737288 | tf_op jit(solution)/shard_map/ppermute | solution.py:175
  49.2 11.4 %collective-permute-start.8 = (bf16[160,768]{1,0:T(8,128)(2,1)S(1)}, bf16[160,768]{1,0:T(8,128)(2,1)S(1)}, u32[]{:S(2)}, u32[]{:S(2)}) collective-permute-start(bf16[160,768]{1,0:T(8,128)(2,1)S(1)} %collective-permute-done.5), channel_id=1, source_target_pairs={{3,0},{2,1},{5,2},{4,3},{7,4},{6,5},{9,6},{8,7},{11,8},{10,9},{13,... | collective-permute-start | bytes 737288 | tf_op jit(solution)/shard_map/ppermute | solution.py:176
  55.4 5.2 %copy-start = (bf16[768,160]{0,1:T(8,128)(2,1)S(1)}, bf16[768,160]{0,1:T(8,128)(2,1)}, u32[]{:S(2)}) copy-start(bf16[768,160]{0,1:T(8,128)(2,1)} %param.8) | copy-start | bytes 737284

commit v3 on v2

--- a/solution.py
+++ b/solution.py
@@ -68,15 +68,20 @@
     return total
 
 
-def first_kernel(w_ref, mine_ref, out_ref):
+def first_kernel(w_ref, *refs):
+    piece_refs, (out_ref, mine_ref) = refs[:NEAR], refs[NEAR:]
     width = w_ref.shape[1]
-    pieces = [mine_ref[width * k : width * k + width] for k in range(NEAR)]
+    pieces = [piece_ref[...] for piece_ref in piece_refs]
     out_ref[...] = project(w_ref, range(NEAR), pieces)
-
-
-def shift_kernel(w_ref, attn_ref, first_ref, other_ref, far_ref, far_other_ref, out_ref):
+    for side in range(2):
+        for k, piece in enumerate(pieces):
+            mine_ref[side, width * k : width * k + width] = piece
+
+
+def shift_kernel(w_ref, attn_ref, first_ref, pair_ref, far_ref, far_other_ref, out_ref):
     width = w_ref.shape[1]
-    pieces = [other_ref[width * k : width * k + width] for k in range(NEAR)]
+    side = 1 - (lax.axis_index("tensor") & 1)
+    pieces = [pair_ref[side, width * k : width * k + width] for k in range(NEAR)]
     pieces += [far_ref[...], far_other_ref[...]]
     total = first_ref[...] + project(w_ref, range(NEAR, N_TENSOR), pieces)
     row = jnp.sum(total * attn_ref[...].astype(jnp.float32), axis=0, keepdims=True)
@@ -91,13 +96,13 @@
     aux_ref,
     sums_ref,
     attn_ref,
-    mine_ref,
-    other_ref,
+    pair_ref,
     far_ref,
     far_other_ref,
     out_ref,
 ):
     width = attn_ref.shape[0]
+    core = lax.axis_index("tensor") & 1
     shift = jnp.sum(recv_ref[...], axis=0)
     gap, signed, base = aux_ref[0], aux_ref[1], aux_ref[2]
     ratio = jnp.exp(gap + shift)
@@ -115,11 +120,9 @@
     low = value - high - middle
     stats = jnp.where(lane < 36, high, jnp.where(lane < 40, middle, low))[:, 32:]
     for place in range(N_TENSOR):
-        if place < NEAR:
-            piece = mine_ref[width * place : width * place + width]
-        elif place < 2 * NEAR:
-            k = place - NEAR
-            piece = other_ref[width * k : width * k + width]
+        if place < 2 * NEAR:
+            side, k = (core, 1 - core)[place // NEAR], place % NEAR
+            piece = pair_ref[side, width * k : width * k + width]
         else:
             piece = (far_ref, far_other_ref)[place - 2 * NEAR][...]
         product = lax.dot_general(
@@ -160,13 +163,13 @@
 ):
     local_rows, width = attn_output.shape
     attn_t, readout_t = attn_output.T, readout_vectors.T
-    up, down, cross, swap = [], [], [], []
+    up, down, cross = [], [], []
+    cores = [[2 * z, 2 * z + 1] for z in range(N_Z)]
     for z in range(N_Z):
         for c in range(2):
             up.append((2 * z + c, 2 * ((z + 1) % N_Z) + c))
             down.append((2 * ((z + 1) % N_Z) + c, 2 * z + c))
             cross.append((2 * ((z + 1) % N_Z) + 1 - c, 2 * z + c))
-            swap.append((2 * z + 1 - c, 2 * z + c))
     rising, falling, nearby = readout_t, readout_t, [readout_t]
     for _ in range(3):
         rising = lax.ppermute(rising, "tensor", up)
@@ -174,8 +177,6 @@
         nearby += [rising, falling]
     far_mine = lax.ppermute(rising, "tensor", up)
     far_other = lax.ppermute(falling, "tensor", cross)
-    mine = jnp.concatenate(nearby, axis=0)
-    other = lax.ppermute(mine, "tensor", swap)
 
     params = pltpu.CompilerParams(vmem_limit_bytes=24 << 20)
     tiled = (local_rows // LANES, LANES)
@@ -197,28 +198,32 @@
         keep_mask.reshape(tiled),
         move_plan,
     )
-    first = pl.pallas_call(
+    first, mine = pl.pallas_call(
         first_kernel,
-        in_specs=[vmem_spec()] * 2,
-        out_specs=vmem_spec(),
-        out_shape=jax.ShapeDtypeStruct((width, local_rows), jnp.float32),
-        compiler_params=params,
-    )(w_blocks, mine)
+        in_specs=[vmem_spec()] * (1 + NEAR),
+        out_specs=[vmem_spec()] * 2,
+        out_shape=[
+            jax.ShapeDtypeStruct((width, local_rows), jnp.float32),
+            jax.ShapeDtypeStruct((2, NEAR * width, local_rows), readout_t.dtype),
+        ],
+        compiler_params=params,
+    )(w_blocks, *nearby)
+    pair = lax.all_to_all(mine, "tensor", 0, 0, tiled=True, axis_index_groups=cores)
     partial_shift = pl.pallas_call(
         shift_kernel,
         in_specs=[vmem_spec()] * 6,
         out_specs=vmem_spec(),
         out_shape=jax.ShapeDtypeStruct((N_TENSOR, 8, LANES), jnp.float32),
         compiler_params=params,
-    )(w_blocks, attn_t, first, other, far_mine, far_other)
+    )(w_blocks, attn_t, first, pair, far_mine, far_other)
     shifts = lax.all_to_all(partial_shift, "tensor", 0, 0, tiled=True)
     chunks = pl.pallas_call(
         grad_kernel,
-        in_specs=[vmem_spec()] * 8,
+        in_specs=[vmem_spec()] * 7,
         out_specs=vmem_spec(),
         out_shape=jax.ShapeDtypeStruct((N_DP, CHUNK_ROWS, LANES), jnp.bfloat16),
         compiler_params=params,
-    )(shifts, aux, sums, attn_t, mine, other, far_mine, far_other)
+    )(shifts, aux, sums, attn_t, pair, far_mine, far_other)
     received = lax.all_to_all(chunks, "dp", 0, 0, tiled=True)
     grad_t, stats = pl.pallas_call(
         finish_kernel,

time: 119 us -> 121 us (1.017)
  blocking collectives: 54.3 us -> 60.5 us
  starting transfers between devices: 43 us -> 38.1 us
  waiting for transfers between devices: 14.5 us -> 11.2 us
  local copies, waits for them, and re-layouts: 1.61 us -> 4.73 us
    all_to_all x0 -> x1, blocking collectives: none -> 6.61 us  [body(): lax.all_to_all(mine, 'tensor', 0, 0, tiled=True, axis_index_groups=cores)]
    ppermute x3, waiting for transfers between devices: 1.46 us -> 7.71 us  [body(): falling = lax.ppermute(falling, 'tensor', down)]
    ppermute x3, waiting for transfers between devices: 8.56 us -> 3.53 us  [body(): rising = lax.ppermute(rising, 'tensor', up)]
    ppermute x3, starting transfers between devices: 24.3 us -> 28.4 us  [body(): falling = lax.ppermute(falling, 'tensor', down)]
    ppermute x1, starting transfers between devices: 5.7 us -> 2.09 us  [body(): far_other = lax.ppermute(falling, 'tensor', cross)]
    ppermute x1, waiting for transfers between devices: 3.45 us -> 0.01 us  [body(): far_mine = lax.ppermute(rising, 'tensor', up)]
    ppermute x3, starting transfers between devices: 9.14 us -> 5.76 us  [body(): rising = lax.ppermute(rising, 'tensor', up)]
    unnamed x20 -> x12, local copies, waits for them, and re-layouts: 1.08 us -> 4.22 us
  transfers between devices with their start and end apart: 9 -> 8, of which waited for: 6 -> 4; matrix products, arithmetic and copies ran while one was open for 1% -> 1% of each run, Pallas kernels for 1% -> 1%
where the time goes in v3:
time: 121 us; the launch traced here: 120 us
  blocking collectives  60.5 us (50%)
  starting transfers between devices  38.1 us (31%)
  waiting for transfers between devices  11.2 us (9%)
  local copies, waits for them, and re-layouts  4.73 us (4%)
  Pallas kernels  3.93 us (3%)
    all_to_all x1, blocking collectives, body(): received = lax.all_to_all(chunks, 'dp', 0, 0, tiled=True)  41.6 us
    ppermute x3, starting transfers between devices, body(): falling = lax.ppermute(falling, 'tensor', down)  28.4 us
    all_to_all x1, blocking collectives, body(): shifts = lax.all_to_all(partial_shift, 'tensor', 0, 0, tiled=True)  12.3 us
    ppermute x3, waiting for transfers between devices, body(): falling = lax.ppermute(falling, 'tensor', down)  7.71 us
    all_to_all x1, blocking collectives, body(): lax.all_to_all(mine, 'tensor', 0, 0, tiled=True, axis_index_groups=cores)  6.61 us
    ppermute x3, starting transfers between devices, body(): rising = lax.ppermute(rising, 'tensor', up)  5.76 us
    unnamed x12, local copies, waits for them, and re-layouts  4.22 us
    ppermute x3, waiting for transfers between devices, body(): rising = lax.ppermute(rising, 'tensor', up)  3.53 us
  transfers between devices with their start and end apart: 8, of which 4 were waited for; matrix products, arithmetic and copies ran while one was open for 1% of the time, Pallas kernels for 1%

profile of v3, /device:TPU:4, one launch (start us, length us, event | category | flops | bytes accessed | tf_op | source)
XLA Modules:
  0.0 120.0 jit_solution(3359533339179630418)
XLA Ops:
  0.6 17.3 %collective-permute-start.1 = (bf16[160,768]{1,0:T(8,128)(2,1)}, bf16[160,768]{1,0:T(8,128)(2,1)S(1)}, u32[]{:S(2)}, u32[]{:S(2)}) collective-permute-start(bf16[160,768]{1,0:T(8,128)(2,1)} %bitcast.15), channel_id=1, source_target_pairs={{2,0},{3,1},{4,2},{5,3},{6,4},{7,5},{8,6},{9,7},{10,8},{11,9},{12,... | collective-permute-start | bytes 737288 | tf_op jit(solution)/shard_map/ppermute | solution.py:176
  18.0 1.9 %collective-permute-start = (bf16[160,768]{1,0:T(8,128)(2,1)}, bf16[160,768]{1,0:T(8,128)(2,1)S(1)}, u32[]{:S(2)}, u32[]{:S(2)}) collective-permute-start(bf16[160,768]{1,0:T(8,128)(2,1)} %bitcast.16), channel_id=1, source_target_pairs={{0,2},{1,3},{2,4},{3,5},{4,6},{5,7},{6,8},{7,9},{8,10},{9,11},{10,... | collective-permute-start | bytes 737288 | tf_op jit(solution)/shard_map/ppermute | solution.py:175
  19.9 3.6 %collective-permute-done.1.refs_2_ = bf16[160,768]{1,0:T(8,128)(2,1)S(1)} collective-permute-done((bf16[160,768]{1,0:T(8,128)(2,1)}, bf16[160,768]{1,0:T(8,128)(2,1)S(1)}, u32[]{:S(2)}, u32[]{:S(2)}) %collective-permute-start.1) | collective-permute-done | bytes 245792 | tf_op jit(solution)/shard_map/ppermute | solution.py:176
  23.5 5.5 %collective-permute-start.3 = (bf16[160,768]{1,0:T(8,128)(2,1)S(1)}, bf16[160,768]{1,0:T(8,128)(2,1)S(1)}, u32[]{:S(2)}, u32[]{:S(2)}) collective-permute-start(bf16[160,768]{1,0:T(8,128)(2,1)S(1)} %collective-permute-done.1.refs_2_), channel_id=1, source_target_pairs={{2,0},{3,1},{4,2},{5,3},{6,4},{7,5},{8,6},{9,7},{10,8},{11,9},{12,... | collective-permute-start | bytes 737288 | tf_op jit(solution)/shard_map/ppermute | solution.py:176
  29.0 0.0 collective-permute-done.refs_1_
  29.0 1.9 %collective-permute-start.2 = (bf16[160,768]{1,0:T(8,128)(2,1)S(1)}, bf16[160,768]{1,0:T(8,128)(2,1)S(1)}, u32[]{:S(2)}, u32[]{:S(2)}) collective-permute-start(bf16[160,768]{1,0:T(8,128)(2,1)S(1)} %collective-permute-done.refs_1_), channel_id=1, source_target_pairs={{0,2},{1,3},{2,4},{3,5},{4,6},{5,7},{6,8},{7,9},{8,10},{9,11},{10,... | collective-permute-start | bytes 737288 | tf_op jit(solution)/shard_map/ppermute | solution.py:175
  30.9 2.4 %collective-permute-done.3.refs_4_ = bf16[160,768]{1,0:T(8,128)(2,1)S(1)} collective-permute-done((bf16[160,768]{1,0:T(8,128)(2,1)S(1)}, bf16[160,768]{1,0:T(8,128)(2,1)S(1)}, u32[]{:S(2)}, u32[]{:S(2)}) %collective-permute-start.3) | collective-permute-done | bytes 245792 | tf_op jit(solution)/shard_map/ppermute | solution.py:176
  33.3 5.6 %collective-permute-start.5 = (bf16[160,768]{1,0:T(8,128)(2,1)S(1)}, bf16[160,768]{1,0:T(8,128)(2,1)S(1)}, u32[]{:S(2)}, u32[]{:S(2)}) collective-permute-start(bf16[160,768]{1,0:T(8,128)(2,1)S(1)} %collective-permute-done.3.refs_4_), channel_id=1, source_target_pairs={{2,0},{3,1},{4,2},{5,3},{6,4},{7,5},{8,6},{9,7},{10,8},{11,9},{12,... | collective-permute-start | bytes 737288 | tf_op jit(solution)/shard_map/ppermute | solution.py:176
  38.9 1.9 %collective-permute-start.4 = (bf16[160,768]{1,0:T(8,128)(2,1)S(1)}, bf16[160,768]{1,0:T(8,128)(2,1)S(1)}, u32[]{:S(2)}, u32[]{:S(2)}) collective-permute-start(bf16[160,768]{1,0:T(8,128)(2,1)S(1)} %collective-permute-done.2.refs_3_), channel_id=1, source_target_pairs={{0,2},{1,3},{2,4},{3,5},{4,6},{5,7},{6,8},{7,9},{8,10},{9,11},{10,... | collective-permute-start | bytes 737288 | tf_op jit(solution)/shard_map/ppermute | solution.py:175
  40.8 1.8 %collective-permute-done.5.refs_6_ = bf16[160,768]{1,0:T(8,128)(2,1)S(1)} collective-permute-done((bf16[160,768]{1,0:T(8,128)(2,1)S(1)}, bf16[160,768]{1,0:T(8,128)(2,1)S(1)}, u32[]{:S(2)}, u32[]{:S(2)}) %collective-permute-start.5) | collective-permute-done | bytes 245792 | tf_op jit(solution)/shard_map/ppermute | solution.py:176
  42.6 2.1 %collective-permute-start.7 = (bf16[160,768]{1,0:T(8,128)(2,1)S(1)}, bf16[160,768]{1,0:T(8,128)(2,1)S(1)}, u32[]{:S(2)}, u32[]{:S(2)}) collective-permute-start(bf16[160,768]{1,0:T(8,128)(2,1)S(1)} %collective-permute-done.5.refs_6_), channel_id=1, source_target_pairs={{3,0},{2,1},{5,2},{4,3},{7,4},{6,5},{9,6},{8,7},{11,8},{10,9},{13,... | collective-permute-start | bytes 737288 | tf_op jit(solution)/shard_map/ppermute | solution.py:179
  44.7 3.5 %collective-permute-done.4.refs_5_ = bf16[160,768]{1,0:T(8,128)(2,1)S(1)} collective-permute-done((bf16[160,768]{1,0:T(8,128)(2,1)S(1)}, bf16[160,768]{1,0:T(8,128)(2,1)S(1)}, u32[]{:S(2)}, u32[]{:S(2)}) %collective-permute-start.4) | collective-permute-done | bytes 245792 | tf_op jit(solution)/shard_map/ppermute | solution.py:175
  48.2 1.9 %collective-permute-start.6 = (bf16[160,768]{1,0:T(8,128)(2,1)S(1)}, bf16[160,768]{1,0:T(8,128)(2,1)S(1)}, u32[]{:S(2)}, u32[]{:S(2)}) collective-permute-start(bf16[160,768]{1,0:T(8,128)(2,1)S(1)} %collective-permute-done.4.refs_5_), channel_id=1, source_target_pairs={{0,2},{1,3},{2,4},{3,5},{4,6},{5,7},{6,8},{7,9},{8,10},{9,11},{10,... | collective-permute-start | bytes 737288 | tf_op jit(solution)/shard_map/ppermute | solution.py:178
  50.1 0.7 bitcast_convert_fusion
  50.8 1.1 copy-done.1
  51.9 0.8 copy-done.3
  52.7 0.7 copy-done.4
  53.4 0.7 copy-done.5
  54.1 0.4 shard_map.95
  54.5 0.0 copy-start.2
  54.5 0.9 copy-done.2
  55.4 0.6 shard_map.96
  56.1 0.0 copy-start
  56.1 6.6 %all_to_all.15.pair_ref = bf16[2,1120,768]{2,1,0:T(8,128)(2,1)S(1)} all-to-all(bf16[2,1120,768]{2,1,0:T(8,128)(2,1)S(1)} %get-tuple-element.11), channel_id=1, replica_groups={{0,1},{2,3},{4,5},{6,7},{8,9},{10,11},{12,13},{14,15},{16,17},{18,19},{..., dimensions={0} | all-to-all | bytes 6881280 | tf_op jit(solution)/shard_map/all_to_all | solution.py:211
  62.7 0.0 collective-permute-done.7.far_other_ref
  62.7 0.0 collective-permute-done.6.far_ref
  62.7 0.8 shard_map.97
  63.5 12.3 %all_to_all.16.recv_ref = f32[16,8,128]{2,1,0:T(8,128)S(1)} all-to-all(f32[16,8,128]{2,1,0:T(8,128)S(1)} %shard_map.97), channel_id=1, replica_groups=mesh['dp'=64,'tensor'=16] {'tensor'}, dimensions={0} | all-to-all | bytes 131072 | tf_op jit(solution)/shard_map/all_to_all | solution.py:219
  75.8 1.3 %shard_map.98 = bf16[64,56,128]{2,1,0:T(8,128)(2,1)S(1)} custom-call(f32[16,8,128]{2,1,0:T(8,128)S(1)} %all_to_all.16.recv_ref, f32[3,8,128]{2,1,0:T(8,128)S(1)} %get-tuple-element.12.aux_ref, f32[8,128]{1,0:T(8,128)S(1)} %get-tuple-element.13.sums_ref, bf16[160,768]{1,0:T(8,128)(2,1)S(1)} %bitcast.14, bf16[2,1120,768]{2,1,0:T(8,128)(2,1)S(1)} %all_to_all.15.pair_ref, ...), custom_call_target="tpu_custom_call" | custom-call | tf_op jit(solution)/shard_map/pallas_call | solution.py:220
  77.1 41.6 %all_to_all.17.recv_ref = bf16[64,56,128]{2,1,0:T(8,128)(2,1)S(1)} all-to-all(bf16[64,56,128]{2,1,0:T(8,128)(2,1)S(1)} %shard_map.98), channel_id=1, replica_groups=mesh['dp'=64,'tensor'=16] {'dp'}, dimensions={0} | all-to-all | bytes 1835008 | tf_op jit(solution)/shard_map/all_to_all | solution.py:227
  118.7 0.8 shard_map.99
  119.5 0.5 slice_bitcast_fusion
  (6 shorter events, 0.0 us)
Async XLA Ops:
  0.6 22.8 %collective-permute-start.1 = (bf16[160,768]{1,0:T(8,128)(2,1)}, bf16[160,768]{1,0:T(8,128)(2,1)S(1)}, u32[]{:S(2)}, u32[]{:S(2)}) collective-permute-start(bf16[160,768]{1,0:T(8,128)(2,1)} %bitcast.15), channel_id=1, source_target_pairs={{2,0},{3,1},{4,2},{5,3},{6,4},{7,5},{8,6},{9,7},{10,8},{11,9},{12,... | collective-permute-start | bytes 737288 | tf_op jit(solution)/shard_map/ppermute | solution.py:176
  18.0 11.0 %collective-permute-start = (bf16[160,768]{1,0:T(8,128)(2,1)}, bf16[160,768]{1,0:T(8,128)(2,1)S(1)}, u32[]{:S(2)}, u32[]{:S(2)}) collective-permute-start(bf16[160,768]{1,0:T(8,128)(2,1)} %bitcast.16), channel_id=1, source_target_pairs={{0,2},{1,3},{2,4},{3,5},{4,6},{5,7},{6,8},{7,9},{8,10},{9,11},{10,... | collective-permute-start | bytes 737288 | tf_op jit(solution)/shard_map/ppermute | solution.py:175
  23.5 9.8 %collective-permute-start.3 = (bf16[160,768]{1,0:T(8,128)(2,1)S(1)}, bf16[160,768]{1,0:T(8,128)(2,1)S(1)}, u32[]{:S(2)}, u32[]{:S(2)}) collective-permute-start(bf16[160,768]{1,0:T(8,128)(2,1)S(1)} %collective-permute-done.1.refs_2_), channel_id=1, source_target_pairs={{2,0},{3,1},{4,2},{5,3},{6,4},{7,5},{8,6},{9,7},{10,8},{11,9},{12,... | collective-permute-start | bytes 737288 | tf_op jit(solution)/shard_map/ppermute | solution.py:176
  29.0 9.9 %collective-permute-start.2 = (bf16[160,768]{1,0:T(8,128)(2,1)S(1)}, bf16[160,768]{1,0:T(8,128)(2,1)S(1)}, u32[]{:S(2)}, u32[]{:S(2)}) collective-permute-start(bf16[160,768]{1,0:T(8,128)(2,1)S(1)} %collective-permute-done.refs_1_), channel_id=1, source_target_pairs={{0,2},{1,3},{2,4},{3,5},{4,6},{5,7},{6,8},{7,9},{8,10},{9,11},{10,... | collective-permute-start | bytes 737288 | tf_op jit(solution)/shard_map/ppermute | solution.py:175
  33.3 9.3 %collective-permute-start.5 = (bf16[160,768]{1,0:T(8,128)(2,1)S(1)}, bf16[160,768]{1,0:T(8,128)(2,1)S(1)}, u32[]{:S(2)}, u32[]{:S(2)}) collective-permute-start(bf16[160,768]{1,0:T(8,128)(2,1)S(1)} %collective-permute-done.3.refs_4_), channel_id=1, source_target_pairs={{2,0},{3,1},{4,2},{5,3},{6,4},{7,5},{8,6},{9,7},{10,8},{11,9},{12,... | collective-permute-start | bytes 737288 | tf_op jit(solution)/shard_map/ppermute | solution.py:176
  38.9 9.3 %collective-permute-start.4 = (bf16[160,768]{1,0:T(8,128)(2,1)S(1)}, bf16[160,768]{1,0:T(8,128)(2,1)S(1)}, u32[]{:S(2)}, u32[]{:S(2)}) collective-permute-start(bf16[160,768]{1,0:T(8,128)(2,1)S(1)} %collective-permute-done.2.refs_3_), channel_id=1, source_target_pairs={{0,2},{1,3},{2,4},{3,5},{4,6},{5,7},{6,8},{7,9},{8,10},{9,11},{10,... | collective-permute-start | bytes 737288 | tf_op jit(solution)/shard_map/ppermute | solution.py:175
  42.6 20.2 %collective-permute-start.7 = (bf16[160,768]{1,0:T(8,128)(2,1)S(1)}, bf16[160,768]{1,0:T(8,128)(2,1)S(1)}, u32[]{:S(2)}, u32[]{:S(2)}) collective-permute-start(bf16[160,768]{1,0:T(8,128)(2,1)S(1)} %collective-permute-done.5.refs_6_), channel_id=1, source_target_pairs={{3,0},{2,1},{5,2},{4,3},{7,4},{6,5},{9,6},{8,7},{11,8},{10,9},{13,... | collective-permute-start | bytes 737288 | tf_op jit(solution)/shard_map/ppermute | solution.py:179
  48.2 14.6 %collective-permute-start.6 = (bf16[160,768]{1,0:T(8,128)(2,1)S(1)}, bf16[160,768]{1,0:T(8,128)(2,1)S(1)}, u32[]{:S(2)}, u32[]{:S(2)}) collective-permute-start(bf16[160,768]{1,0:T(8,128)(2,1)S(1)} %collective-permute-done.4.refs_5_), channel_id=1, source_target_pairs={{0,2},{1,3},{2,4},{3,5},{4,6},{5,7},{6,8},{7,9},{8,10},{9,11},{10,... | collective-permute-start | bytes 737288 | tf_op jit(solution)/shard_map/ppermute | solution.py:178
  50.8 1.1 copy-start.1
  51.9 0.8 copy-start.3
  52.7 0.7 copy-start.4
  53.4 0.7 copy-start.5
  54.5 0.9 copy-start.2
  56.1 6.6 %copy-start = (bf16[768,160]{0,1:T(8,128)(2,1)S(1)}, bf16[768,160]{0,1:T(8,128)(2,1)}, u32[]{:S(2)}) copy-start(bf16[768,160]{0,1:T(8,128)(2,1)} %param.8) | copy-start | bytes 737284

commit v4 on v2

v4 whole, which is shorter than its diff:
```python
import jax
import jax.numpy as jnp
from jax import lax
from jax.experimental import pallas as pl
from jax.experimental.pallas import tpu as pltpu
from jax.sharding import PartitionSpec as P

EPS_LOW = 0.2
EPS_HIGH = 0.28
LOSS_SCALE = 16384.0
N_DP = 64
N_TENSOR = 16
CHUNK_ROWS = 56
LANES = 128
QUAD = 4


def vmem_spec():
    return pl.BlockSpec(memory_space=pltpu.VMEM)


def split_kernel(w_ref, keep_ref, send_ref):
    width = w_ref.shape[0]
    chip = (lax.axis_index("tensor") >> 1) & 1
    for place in range(QUAD):
        columns = [w_ref[:, width * (QUAD * k + place) :][:, :width] for k in range(QUAD)]
        part = jnp.concatenate(columns, axis=1)

        @pl.when(chip == place // 2)
        def _():
            keep_ref[place % 2] = part

        @pl.when(chip != place // 2)
        def _():
            send_ref[place % 2] = part


def shift_kernel(w_ref, attn_ref, readout_ref, out_ref):
    width = w_ref.shape[1] // 2
    chip = (lax.axis_index("tensor") >> 1) & 1
    readout = readout_ref[...]
    row = None
    for place in range(QUAD):
        start = pl.multiple_of((chip ^ (place // 2)) * width, width)
        projected = jnp.dot(
            w_ref[place % 2, pl.ds(start, width)], readout, preferred_element_type=jnp.float32
        )
        attn = attn_ref[width * place : width * place + width].astype(jnp.float32)
        part = jnp.sum(projected * attn, axis=0, keepdims=True)
        row = part if row is None else row + part
    rows = [row[:, LANES * r : LANES * r + LANES] for r in range(6)]
    block = jnp.concatenate(rows + [jnp.zeros((2, LANES), jnp.float32)], axis=0)
    for k in range(N_TENSOR):
        out_ref[k] = block


def weight_kernel(gap_ref, size_ref, sign_ref, keep_ref, plan_ref, aux_ref, sums_ref):
    owner = lax.broadcasted_iota(jnp.int32, plan_ref.shape, 0)
    live_total = jnp.sum(jnp.where(owner == lax.axis_index("dp"), plan_ref[...], 0))
    shape = gap_ref.shape
    slot_ids = lax.broadcasted_iota(jnp.int32, shape, 0) * LANES + lax.broadcasted_iota(jnp.int32, shape, 1)
    weight = jnp.where(slot_ids < live_total, keep_ref[...], 0).astype(jnp.float32)
    gap = gap_ref[...]
    advantage = (2 * sign_ref[...] - 1).astype(jnp.float32) * size_ref[...]
    base_ratio = jnp.exp(gap)
    clip_high = jnp.where((advantage > 0) & (base_ratio > 1.0 + EPS_HIGH), 1.0, 0.0)
    clip_low = jnp.where((advantage < 0) & (base_ratio < 1.0 - EPS_LOW), 1.0, 0.0)
    signed = weight * advantage
    zeros = jnp.zeros((2, LANES), jnp.float32)
    base = -LOSS_SCALE * signed * (1.0 - clip_high - clip_low)
    for k, value in enumerate((gap, signed, base)):
        aux_ref[k] = jnp.concatenate([value, zeros], axis=0)
    lane = lax.broadcasted_iota(jnp.int32, (8, LANES), 1)
    which = jnp.where((lane >= 32) & (lane < 44), lane & 3, 3)
    count, high, low = jnp.sum(weight), jnp.sum(weight * clip_high), jnp.sum(weight * clip_low)
    sums_ref[...] = jnp.where(
        which == 0, count, jnp.where(which == 1, high, jnp.where(which == 2, low, 0.0))
    )


def grad_kernel(recv_ref, aux_ref, sums_ref, attn_ref, readout_ref, out_ref):
    width = attn_ref.shape[0] // QUAD
    shift = jnp.sum(recv_ref[...], axis=0)
    gap, signed, base = aux_ref[0], aux_ref[1], aux_ref[2]
    ratio = jnp.exp(gap + shift)
    loss = jnp.sum(
        jnp.minimum(ratio * signed, jnp.clip(ratio, 1.0 - EPS_LOW, 1.0 + EPS_HIGH) * signed)
    )
    coefficient = base * ratio
    row = jnp.concatenate([coefficient[r : r + 1] for r in range(6)], axis=1)
    scaled = (attn_ref[...].astype(jnp.float32) * row).astype(jnp.bfloat16)
    lane = lax.broadcasted_iota(jnp.int32, (8, LANES), 1)
    is_loss = (lane == 35) | (lane == 39) | (lane == 43)
    value = jnp.where(is_loss, loss, sums_ref[...])
    high = value.astype(jnp.bfloat16).astype(jnp.float32)
    middle = (value - high).astype(jnp.bfloat16).astype(jnp.float32)
    low = value - high - middle
    stats = jnp.where(lane < 36, high, jnp.where(lane < 40, middle, low))[:, 32:]
    for place in range(QUAD):
        mine = scaled[width * place : width * place + width]
        for k in range(QUAD):
            product = lax.dot_general(
                readout_ref[width * k : width * k + width],
                mine,
                (((1,), (1,)), ((), ())),
                preferred_element_type=jnp.float32,
            )
            for q in range(4):
                part = product[40 * q : 40 * q + 40]
                rest = part[:, LANES:]
                first = jnp.concatenate([rest[8 * r : 8 * r + 8] for r in range(4)], axis=1)
                second = jnp.concatenate([rest[32:40], stats], axis=1)
                out_ref[16 * k + 4 * place + q] = jnp.concatenate(
                    [part[:, :LANES], first, second], axis=0
                ).astype(jnp.bfloat16)


def finish_kernel(recv_ref, grad_ref, stats_ref):
    total = jnp.sum(recv_ref[...].astype(jnp.float32), axis=0)
    first, second = total[40:48], total[48:56]
    lane = lax.broadcasted_iota(jnp.int32, (1, LANES), 1)
    row = second[0:1]

    def pick(k):
        mine = (lane == 32 + k) | (lane == 36 + k) | (lane == 40 + k)
        return jnp.sum(jnp.where(mine, row, 0.0), axis=1, keepdims=True)

    divisor = jnp.maximum(pick(0), 1.0)
    rest = jnp.concatenate([first[:, 32 * k : 32 * k + 32] for k in range(4)] + [second[:, :32]], axis=0)
    grad_ref[...] = jnp.concatenate([total[:40], rest], axis=1) / divisor
    stats_ref[...] = (
        jnp.where(lane == 0, -pick(3), jnp.where(lane == 1, pick(1), jnp.where(lane == 2, pick(2), 0.0)))
        / divisor
    )


def body(
    attn_output, readout_vectors, w_out, log_gap, magnitude, reward_sign, keep_mask, move_plan
):
    local_rows, width = attn_output.shape
    attn_t, readout_t = attn_output.T, readout_vectors.T
    params = pltpu.CompilerParams(vmem_limit_bytes=24 << 20)
    quads = [[QUAD * q + p for p in range(QUAD)] for q in range(QUAD)]
    strided = [[QUAD * q + p for q in range(QUAD)] for p in range(QUAD)]
    cores = [[2 * z, 2 * z + 1] for z in range(N_TENSOR // 2)]

    columns = jax.ShapeDtypeStruct((2, width, QUAD * width), w_out.dtype)
    kept, sent = pl.pallas_call(
        split_kernel,
        in_specs=[vmem_spec()],
        out_specs=[vmem_spec()] * 2,
        out_shape=[columns] * 2,
        compiler_params=params,
    )(w_out)
    got = lax.ppermute(sent, "tensor", [(t, t ^ 2) for t in range(N_TENSOR)])
    attn_all = lax.all_gather(attn_t, "tensor", axis=0, tiled=True, axis_index_groups=quads)
    readout_all = lax.all_gather(readout_t, "tensor", axis=0, tiled=True, axis_index_groups=strided)
    weights = lax.all_to_all(
        jnp.concatenate([kept, got], axis=1), "tensor", 0, 0, tiled=True, axis_index_groups=cores
    )
    partial_shift = pl.pallas_call(
        shift_kernel,
        in_specs=[vmem_spec()] * 3,
        out_specs=vmem_spec(),
        out_shape=jax.ShapeDtypeStruct((N_TENSOR, 8, LANES), jnp.float32),
        compiler_params=params,
    )(weights, attn_all, readout_all)
    shifts = lax.all_to_all(partial_shift, "tensor", 0, 0, tiled=True)

    tiled = (local_rows // LANES, LANES)
    aux, sums = pl.pallas_call(
        weight_kernel,
        in_specs=[vmem_spec()] * 5,
        out_specs=[vmem_spec()] * 2,
        out_shape=[
            jax.ShapeDtypeStruct((3, 8, LANES), jnp.float32),
            jax.ShapeDtypeStruct((8, LANES), jnp.float32),
        ],
        compiler_params=params,
    )(
        log_gap.astype(jnp.float32).reshape(tiled),
        magnitude.astype(jnp.float32).reshape(tiled),
        reward_sign.reshape(tiled),
        keep_mask.reshape(tiled),
        move_plan,
    )
    chunks = pl.pallas_call(
        grad_kernel,
        in_specs=[vmem_spec()] * 5,
        out_specs=vmem_spec(),
        out_shape=jax.ShapeDtypeStruct((N_DP, CHUNK_ROWS, LANES), jnp.bfloat16),
        compiler_params=params,
    )(shifts, aux, sums, attn_all, readout_all)
    received = lax.all_to_all(chunks, "dp", 0, 0, tiled=True)
    grad_t, stats = pl.pallas_call(
        finish_kernel,
        in_specs=[vmem_spec()],
        out_specs=[vmem_spec(), vmem_spec()],
        out_shape=[
            jax.ShapeDtypeStruct((40, width), jnp.float32),
            jax.ShapeDtypeStruct((1, LANES), jnp.float32),
        ],
        compiler_params=params,
    )(received)
    homes = []
    for m in range(N_DP):
        for t in range(N_TENSOR):
            low, high = t % QUAD, m // 4 % QUAD
            homes.append((N_TENSOR * m + t, N_TENSOR * (m + 4 * (low - high)) + t + high - low))
    grad_t = lax.ppermute(grad_t, ("dp", "tensor"), homes)
    return grad_t.T, stats[0, :3]


def solution(mesh):
    placed = (
        P("dp", "tensor"),
        P("dp", "tensor"),
        P("tensor", None),
        P("dp"),
        P("dp"),
        P("dp"),
        P("dp"),
        P(),
    )
    return jax.shard_map(
        body, mesh=mesh, in_specs=placed, out_specs=(P("tensor", "dp"), P()), check_vma=False
    )
```

time: 119 us -> 128 us (1.076)
  the two profiles are of different devices: /device:TPU:4 before, /device:TPU:7 now
where the time goes in v4:
time: 128 us; the launch traced here: 127 us
  blocking collectives  91.6 us (72%)
  starting transfers between devices  15.9 us (12%)
  waiting for transfers between devices  12.8 us (10%)
  Pallas kernels  3.92 us (3%)
  local copies, waits for them, and re-layouts  2.29 us (2%)
    all_to_all x1, blocking collectives, body(): received = lax.all_to_all(chunks, 'dp', 0, 0, tiled=True)  38.7 us
    all_gather x1, blocking collectives, body(): lax.all_gather(readout_t, 'tensor', axis=0, tiled=True, axis_index_groups...  30.4 us
    all_gather x1, blocking collectives, body(): lax.all_gather(attn_t, 'tensor', axis=0, tiled=True, axis_index_groups=qu...  16.4 us
    all_to_all x1, waiting for transfers between devices, body(): shifts = lax.all_to_all(partial_shift, 'tensor', 0, 0, tiled=True)  7.48 us
    all_to_all x1, blocking collectives, body(): lax.all_to_all(jnp.concatenate([kept, got], axis=1), 'tensor', 0, 0, tile...  6.02 us
    all_to_all x1, starting transfers between devices, body(): shifts = lax.all_to_all(partial_shift, 'tensor', 0, 0, tiled=True)  5.78 us
    ppermute x1, waiting for transfers between devices, body(): grad_t = lax.ppermute(grad_t, ('dp', 'tensor'), homes)  5.35 us
    ppermute x1, starting transfers between devices, body(): grad_t = lax.ppermute(grad_t, ('dp', 'tensor'), homes)  5.19 us
  transfers between devices with their start and end apart: 3, of which 2 were waited for; matrix products, arithmetic and copies ran while one was open for 0% of the time, Pallas kernels for 0%

profile of v4, /device:TPU:7, one launch (start us, length us, event | category | flops | bytes accessed | tf_op | source)
XLA Modules:
  0.0 127.4 jit_solution(15148095331442961513)
XLA Ops:
  0.6 0.0 copy-start
  0.6 1.1 copy-done
  1.8 0.0 copy-start.4
  1.8 0.0 copy-start.5
  1.8 0.6 shard_map.95
  2.4 4.9 %collective-permute-start = (bf16[2,160,640]{2,1,0:T(8,128)(2,1)S(1)}, bf16[2,160,640]{2,1,0:T(8,128)(2,1)S(1)}, u32[]{:S(2)}, u32[]{:S(2)}) collective-permute-start(bf16[2,160,640]{2,1,0:T(8,128)(2,1)S(1)} %get-tuple-element.9), channel_id=1, source_target_pairs={{0,2},{1,3},{2,0},{3,1},{4,6},{5,7},{6,4},{7,5},{8,10},{9,11},{10,... | collective-permute-start | bytes 1228808 | tf_op jit(solution)/shard_map/ppermute | solution.py:155
  7.3 0.0 copy-done.4
  7.3 16.4 %all_gather.6.attn_ref = bf16[640,768]{1,0:T(8,128)(2,1)S(1)} all-gather(bf16[160,768]{1,0:T(8,128)(2,1)S(1)} %bitcast.15), channel_id=1, replica_groups={{0,1,2,3},{4,5,6,7},{8,9,10,11},{12,13,14,15},{16,17,18,19},{20,21,22,2..., dimensions={0}, use_global_device_ids=true | all-gather | bytes 1228800 | tf_op jit(solution)/shard_map/all_gather | solution.py:156
  23.7 0.0 copy-done.5
  23.7 30.4 %all_gather.7.readout_ref = bf16[640,768]{1,0:T(8,128)(2,1)S(1)} all-gather(bf16[160,768]{1,0:T(8,128)(2,1)S(1)} %bitcast.16), channel_id=1, replica_groups={{0,4,8,12},{1,5,9,13},{2,6,10,14},{3,7,11,15},{16,20,24,28},{17,21,25,2..., dimensions={0}, use_global_device_ids=true | all-gather | bytes 1228800 | tf_op jit(solution)/shard_map/all_gather | solution.py:157
  54.1 0.0 collective-permute-done
  54.1 0.1 pad_maximum_fusion
  54.2 6.0 %all_to_all.15.w_ref = bf16[2,320,640]{2,1,0:T(8,128)(2,1)S(1)} all-to-all(bf16[2,320,640]{2,1,0:T(8,128)(2,1)S(1)} %pad_maximum_fusion), channel_id=1, replica_groups={{0,1},{2,3},{4,5},{6,7},{8,9},{10,11},{12,13},{14,15},{16,17},{18,19},{..., dimensions={0} | all-to-all | bytes 1638400 | tf_op jit(solution)/shard_map/all_to_all | solution.py:158
  60.2 0.0 copy-start.6
  60.2 0.0 copy-start.7
  60.2 0.0 copy-start.1
  60.2 1.6 %shard_map.96 = f32[16,8,128]{2,1,0:T(8,128)} custom-call(bf16[2,320,640]{2,1,0:T(8,128)(2,1)S(1)} %all_to_all.15.w_ref, bf16[640,768]{1,0:T(8,128)(2,1)S(1)} %all_gather.6.attn_ref, bf16[640,768]{1,0:T(8,128)(2,1)S(1)} %all_gather.7.readout_ref), custom_call_target="tpu_custom_call" | custom-call | tf_op jit(solution)/shard_map/pallas_call | solution.py:161
  61.8 5.8 %all-to-all-start.1 = ((f32[16,8,128]{2,1,0:T(8,128)}), f32[16,8,128]{2,1,0:T(8,128)S(1)}, u32[]{:S(2)}, u32[]{:S(2)}) async-start(f32[16,8,128]{2,1,0:T(8,128)} %shard_map.96), calls=%async_computation.1 | async-start | bytes 131072 | tf_op jit(solution)/shard_map/all_to_all | solution.py:168
  67.6 0.0 copy-done.6
  67.6 0.0 copy-done.7
  67.6 0.0 copy-done.1
  67.7 0.0 copy-done.2
  67.7 0.0 copy-done.3
  67.7 0.3 shard_map.97
  67.9 7.5 %all-to-all-done.1.recv_ref = f32[16,8,128]{2,1,0:T(8,128)S(1)} async-done(((f32[16,8,128]{2,1,0:T(8,128)}), f32[16,8,128]{2,1,0:T(8,128)S(1)}, u32[]{:S(2)}, u32[]{:S(2)}) %all-to-all-start.1) | async-done | bytes 65568 | tf_op jit(solution)/shard_map/all_to_all | solution.py:168
  75.4 1.3 %shard_map.98 = bf16[64,56,128]{2,1,0:T(8,128)(2,1)S(1)} custom-call(f32[16,8,128]{2,1,0:T(8,128)S(1)} %all-to-all-done.1.recv_ref, f32[3,8,128]{2,1,0:T(8,128)S(1)} %get-tuple-element.10.aux_ref, f32[8,128]{1,0:T(8,128)S(1)} %get-tuple-element.11.sums_ref, bf16[640,768]{1,0:T(8,128)(2,1)S(1)} %all_gather.6.attn_ref, bf16[640,768]{1,0:T(8,128)(2,1)S(1)} %all_gather.7.readout_ref), custom_call_target="tpu_custom_call" | custom-call | tf_op jit(solution)/shard_map/pallas_call | solution.py:187
  76.7 38.7 %all_to_all.16.recv_ref = bf16[64,56,128]{2,1,0:T(8,128)(2,1)S(1)} all-to-all(bf16[64,56,128]{2,1,0:T(8,128)(2,1)S(1)} %shard_map.98), channel_id=1, replica_groups=mesh['dp'=64,'tensor'=16] {'dp'}, dimensions={0} | all-to-all | bytes 1835008 | tf_op jit(solution)/shard_map/all_to_all | solution.py:194
  115.5 0.2 shard_map.99
  115.7 5.2 %collective-permute-start.1 = (f32[40,160]{1,0:T(8,128)S(1)}, f32[40,160]{1,0:T(8,128)S(1)}, u32[]{:S(2)}, u32[]{:S(2)}) collective-permute-start(f32[40,160]{1,0:T(8,128)S(1)} %get-tuple-element.12), channel_id=1, source_target_pairs={{0,0},{1,64},{2,128},{3,192},{4,4},{5,68},{6,132},{7,196},{8,8},{9... | collective-permute-start | bytes 76808 | tf_op jit(solution)/shard_map/ppermute | solution.py:210
  120.9 0.5 slice_bitcast_fusion
  121.4 5.4 %collective-permute-done.1 = f32[40,160]{1,0:T(8,128)S(1)} collective-permute-done((f32[40,160]{1,0:T(8,128)S(1)}, f32[40,160]{1,0:T(8,128)S(1)}, u32[]{:S(2)}, u32[]{:S(2)}) %collective-permute-start.1) | collective-permute-done | bytes 25632 | tf_op jit(solution)/shard_map/ppermute | solution.py:210
  126.7 0.6 copy.11
  (3 shorter events, 0.0 us)
Async XLA Ops:
  0.6 1.1 copy-start
  1.8 5.5 %copy-start.4 = (bf16[768,160]{0,1:T(8,128)(2,1)S(1)}, bf16[768,160]{0,1:T(8,128)(2,1)}, u32[]{:S(2)}) copy-start(bf16[768,160]{0,1:T(8,128)(2,1)} %param.8) | copy-start | bytes 737284
  1.8 21.9 %copy-start.5 = (bf16[768,160]{0,1:T(8,128)(2,1)S(1)}, bf16[768,160]{0,1:T(8,128)(2,1)}, u32[]{:S(2)}) copy-start(bf16[768,160]{0,1:T(8,128)(2,1)} %param.9) | copy-start | bytes 737284
  2.4 51.8 %collective-permute-start = (bf16[2,160,640]{2,1,0:T(8,128)(2,1)S(1)}, bf16[2,160,640]{2,1,0:T(8,128)(2,1)S(1)}, u32[]{:S(2)}, u32[]{:S(2)}) collective-permute-start(bf16[2,160,640]{2,1,0:T(8,128)(2,1)S(1)} %get-tuple-element.9), channel_id=1, source_target_pairs={{0,2},{1,3},{2,0},{3,1},{4,6},{5,7},{6,4},{7,5},{8,10},{9,11},{10,... | collective-permute-start | bytes 1228808 | tf_op jit(solution)/shard_map/ppermute | solution.py:155
  60.2 7.4 %copy-start.6 = (bf16[768]{0:T(1024)(128)(2,1)S(1)}, bf16[768]{0:T(1024)(128)(2,1)}, u32[]{:S(2)}) copy-start(bf16[768]{0:T(1024)(128)(2,1)} %param.12) | copy-start | bytes 4612
  60.2 7.4 %copy-start.7 = (bf16[768]{0:T(1024)(128)(2,1)S(1)}, bf16[768]{0:T(1024)(128)(2,1)}, u32[]{:S(2)}) copy-start(bf16[768]{0:T(1024)(128)(2,1)} %param.11) | copy-start | bytes 4612
  60.2 7.4 %copy-start.1 = (s32[64,64]{1,0:T(8,128)S(1)}, s32[64,64]{1,0:T(8,128)}, u32[]{:S(2)}) copy-start(s32[64,64]{1,0:T(8,128)} %plan_ref.1) | copy-start | bytes 49156
  60.2 7.4 %copy-start.2 = (s32[768]{0:T(1024)S(1)}, s32[768]{0:T(1024)}, u32[]{:S(2)}) copy-start(s32[768]{0:T(1024)} %param.13) | copy-start | bytes 9220
  60.2 7.4 %copy-start.3 = (s32[768]{0:T(1024)S(1)}, s32[768]{0:T(1024)}, u32[]{:S(2)}) copy-start(s32[768]{0:T(1024)} %param.14) | copy-start | bytes 9220
  61.8 13.6 %all-to-all-start.1 = ((f32[16,8,128]{2,1,0:T(8,128)}), f32[16,8,128]{2,1,0:T(8,128)S(1)}, u32[]{:S(2)}, u32[]{:S(2)}) async-start(f32[16,8,128]{2,1,0:T(8,128)} %shard_map.96), calls=%async_computation.1 | async-start | bytes 131072 | tf_op jit(solution)/shard_map/all_to_all | solution.py:168
  115.7 11.1 %collective-permute-start.1 = (f32[40,160]{1,0:T(8,128)S(1)}, f32[40,160]{1,0:T(8,128)S(1)}, u32[]{:S(2)}, u32[]{:S(2)}) collective-permute-start(f32[40,160]{1,0:T(8,128)S(1)} %get-tuple-element.12), channel_id=1, source_target_pairs={{0,0},{1,64},{2,128},{3,192},{4,4},{5,68},{6,132},{7,196},{8,8},{9... | collective-permute-start | bytes 76808 | tf_op jit(solution)/shard_map/ppermute | solution.py:210

commit v5 on v3

--- a/solution.py
+++ b/solution.py
@@ -13,8 +13,7 @@
 CHUNK_ROWS = 56
 LANES = 128
 N_Z = 8
-NEAR = 7
-STEPS = (0, -1, 1, -2, 2, -3, 3)
+STEPS = (0, -1, 1, -2, 2, -3, 3, 4)
 
 
 def vmem_spec():
@@ -23,14 +22,8 @@
 
 def piece_index(place):
     device = lax.axis_index("tensor")
-    core = device & 1
-    if place < NEAR:
-        step, side = STEPS[place], core
-    elif place < 2 * NEAR:
-        step, side = STEPS[place - NEAR], 1 - core
-    else:
-        step, side = 4, (core, 1 - core)[place - 2 * NEAR]
-    return (((device >> 1) + N_Z + step) & (N_Z - 1)) * 2 + side
+    side = (device & 1) ^ (place // N_Z)
+    return (((device >> 1) + N_Z + STEPS[place % N_Z]) & (N_Z - 1)) * 2 + side
 
 
 def prepare_kernel(w_ref, gap_ref, size_ref, sign_ref, keep_ref, plan_ref, out_ref, aux_ref, sums_ref):
@@ -69,21 +62,18 @@
 
 
 def first_kernel(w_ref, *refs):
-    piece_refs, (out_ref, mine_ref) = refs[:NEAR], refs[NEAR:]
+    piece_refs, (out_ref, mine_ref) = refs[:N_Z], refs[N_Z:]
     width = w_ref.shape[1]
     pieces = [piece_ref[...] for piece_ref in piece_refs]
-    out_ref[...] = project(w_ref, range(NEAR), pieces)
-    for side in range(2):
-        for k, piece in enumerate(pieces):
-            mine_ref[side, width * k : width * k + width] = piece
-
-
-def shift_kernel(w_ref, attn_ref, first_ref, pair_ref, far_ref, far_other_ref, out_ref):
+    for k, piece in enumerate(pieces):
+        mine_ref[width * k : width * k + width] = piece
+    out_ref[...] = project(w_ref, range(N_Z), pieces)
+
+
+def shift_kernel(w_ref, attn_ref, first_ref, other_ref, out_ref):
     width = w_ref.shape[1]
-    side = 1 - (lax.axis_index("tensor") & 1)
-    pieces = [pair_ref[side, width * k : width * k + width] for k in range(NEAR)]
-    pieces += [far_ref[...], far_other_ref[...]]
-    total = first_ref[...] + project(w_ref, range(NEAR, N_TENSOR), pieces)
+    pieces = [other_ref[width * k : width * k + width] for k in range(N_Z)]
+    total = first_ref[...] + project(w_ref, range(N_Z, N_TENSOR), pieces)
     row = jnp.sum(total * attn_ref[...].astype(jnp.float32), axis=0, keepdims=True)
     rows = [row[:, LANES * r : LANES * r + LANES] for r in range(6)]
     block = jnp.concatenate(rows + [jnp.zeros((2, LANES), jnp.float32)], axis=0)
@@ -96,13 +86,11 @@
     aux_ref,
     sums_ref,
     attn_ref,
-    pair_ref,
-    far_ref,
-    far_other_ref,
+    mine_ref,
+    other_ref,
     out_ref,
 ):
     width = attn_ref.shape[0]
-    core = lax.axis_index("tensor") & 1
     shift = jnp.sum(recv_ref[...], axis=0)
     gap, signed, base = aux_ref[0], aux_ref[1], aux_ref[2]
     ratio = jnp.exp(gap + shift)
@@ -120,11 +108,8 @@
     low = value - high - middle
     stats = jnp.where(lane < 36, high, jnp.where(lane < 40, middle, low))[:, 32:]
     for place in range(N_TENSOR):
-        if place < 2 * NEAR:
-            side, k = (core, 1 - core)[place // NEAR], place % NEAR
-            piece = pair_ref[side, width * k : width * k + width]
-        else:
-            piece = (far_ref, far_other_ref)[place - 2 * NEAR][...]
+        k = place % N_Z
+        piece = (mine_ref, other_ref)[place // N_Z][width * k : width * k + width]
         product = lax.dot_general(
             piece, scaled, (((1,), (1,)), ((), ())), preferred_element_type=jnp.float32
         )
@@ -163,20 +148,18 @@
 ):
     local_rows, width = attn_output.shape
     attn_t, readout_t = attn_output.T, readout_vectors.T
-    up, down, cross = [], [], []
-    cores = [[2 * z, 2 * z + 1] for z in range(N_Z)]
+    up, down, swap = [], [], []
     for z in range(N_Z):
         for c in range(2):
             up.append((2 * z + c, 2 * ((z + 1) % N_Z) + c))
             down.append((2 * ((z + 1) % N_Z) + c, 2 * z + c))
-            cross.append((2 * ((z + 1) % N_Z) + 1 - c, 2 * z + c))
+            swap.append((2 * z + 1 - c, 2 * z + c))
     rising, falling, nearby = readout_t, readout_t, [readout_t]
     for _ in range(3):
         rising = lax.ppermute(rising, "tensor", up)
         falling = lax.ppermute(falling, "tensor", down)
         nearby += [rising, falling]
-    far_mine = lax.ppermute(rising, "tensor", up)
-    far_other = lax.ppermute(falling, "tensor", cross)
+    nearby.append(lax.ppermute(rising, "tensor", up))
 
     params = pltpu.CompilerParams(vmem_limit_bytes=24 << 20)
     tiled = (local_rows // LANES, LANES)
@@ -200,30 +183,30 @@
     )
     first, mine = pl.pallas_call(
         first_kernel,
-        in_specs=[vmem_spec()] * (1 + NEAR),
+        in_specs=[vmem_spec()] * (1 + N_Z),
         out_specs=[vmem_spec()] * 2,
         out_shape=[
             jax.ShapeDtypeStruct((width, local_rows), jnp.float32),
-            jax.ShapeDtypeStruct((2, NEAR * width, local_rows), readout_t.dtype),
+            jax.ShapeDtypeStruct((N_Z * width, local_rows), readout_t.dtype),
         ],
         compiler_params=params,
     )(w_blocks, *nearby)
-    pair = lax.all_to_all(mine, "tensor", 0, 0, tiled=True, axis_index_groups=cores)
+    other = lax.ppermute(mine, "tensor", swap)
     partial_shift = pl.pallas_call(
         shift_kernel,
-        in_specs=[vmem_spec()] * 6,
+        in_specs=[vmem_spec()] * 4,
         out_specs=vmem_spec(),
         out_shape=jax.ShapeDtypeStruct((N_TENSOR, 8, LANES), jnp.float32),
         compiler_params=params,
-    )(w_blocks, attn_t, first, pair, far_mine, far_other)
+    )(w_blocks, attn_t, first, other)
     shifts = lax.all_to_all(partial_shift, "tensor", 0, 0, tiled=True)
     chunks = pl.pallas_call(
         grad_kernel,
-        in_specs=[vmem_spec()] * 7,
+        in_specs=[vmem_spec()] * 6,
         out_specs=vmem_spec(),
         out_shape=jax.ShapeDtypeStruct((N_DP, CHUNK_ROWS, LANES), jnp.bfloat16),
         compiler_params=params,
-    )(shifts, aux, sums, attn_t, pair, far_mine, far_other)
+    )(shifts, aux, sums, attn_t, mine, other)
     received = lax.all_to_all(chunks, "dp", 0, 0, tiled=True)
     grad_t, stats = pl.pallas_call(
         finish_kernel,

time: 121 us -> 116 us (0.959)
  blocking collectives: 60.5 us -> 52 us
  waiting for transfers between devices: 11.2 us -> 16.5 us
    ppermute x3, waiting for transfers between devices: 7.71 us -> 0.01 us  [body(): falling = lax.ppermute(falling, 'tensor', down)]
    ppermute x2, waiting for transfers between devices: 0.01 us -> 6.9 us  [the longest x1 3.94 us: body(): other = lax.ppermute(mine, 'tensor', swap)]
    all_to_all x1 -> x0, blocking collectives: 6.61 us -> none  [body(): lax.all_to_all(mine, 'tensor', 0, 0, tiled=True, axis_index_groups=cores)]
    ppermute x3, waiting for transfers between devices: 3.53 us -> 9.63 us  [body(): rising = lax.ppermute(rising, 'tensor', up)]
    ppermute x3, starting transfers between devices: 28.4 us -> 24.3 us  [body(): falling = lax.ppermute(falling, 'tensor', down)]
    ppermute x3, starting transfers between devices: 5.76 us -> 9.01 us  [body(): rising = lax.ppermute(rising, 'tensor', up)]
    all_to_all x1, blocking collectives: 12.3 us -> 10.4 us  [body(): shifts = lax.all_to_all(partial_shift, 'tensor', 0, 0, tiled=True)]
  transfers between devices with their start and end apart: 8 -> 8, of which waited for: 4 -> 5; matrix products, arithmetic and copies ran while one was open for 1% -> 1% of each run, Pallas kernels for 1% -> 0%
where the time goes in v5:
time: 116 us
  blocking collectives  52 us (45%)
  starting transfers between devices  37.2 us (32%)
  waiting for transfers between devices  16.5 us (14%)
  local copies, waits for them, and re-layouts  4.73 us (4%)
  Pallas kernels  3.87 us (3%)
    all_to_all x1, blocking collectives, body(): received = lax.all_to_all(chunks, 'dp', 0, 0, tiled=True)  41.6 us
    ppermute x3, starting transfers between devices, body(): falling = lax.ppermute(falling, 'tensor', down)  24.3 us
    all_to_all x1, blocking collectives, body(): shifts = lax.all_to_all(partial_shift, 'tensor', 0, 0, tiled=True)  10.4 us
    ppermute x3, waiting for transfers between devices, body(): rising = lax.ppermute(rising, 'tensor', up)  9.63 us
    ppermute x3, starting transfers between devices, body(): rising = lax.ppermute(rising, 'tensor', up)  9.01 us
    unnamed x12, local copies, waits for them, and re-layouts  4.22 us
    ppermute x1, waiting for transfers between devices, body(): other = lax.ppermute(mine, 'tensor', swap)  3.94 us
    ppermute x1, waiting for transfers between devices, body(): nearby.append(lax.ppermute(rising, 'tensor', up))  2.96 us
  transfers between devices with their start and end apart: 8, of which 5 were waited for; matrix products, arithmetic and copies ran while one was open for 1% of the time, Pallas kernels for 0%

profile of v5, /device:TPU:4, one launch (start us, length us, event | category | flops | bytes accessed | tf_op | source)
XLA Modules:
  0.0 115.7 jit_solution(8066193674992312383)
XLA Ops:
  0.6 5.2 %collective-permute-start = (bf16[160,768]{1,0:T(8,128)(2,1)}, bf16[160,768]{1,0:T(8,128)(2,1)S(1)}, u32[]{:S(2)}, u32[]{:S(2)}) collective-permute-start(bf16[160,768]{1,0:T(8,128)(2,1)} %bitcast.15), channel_id=1, source_target_pairs={{0,2},{1,3},{2,4},{3,5},{4,6},{5,7},{6,8},{7,9},{8,10},{9,11},{10,... | collective-permute-start | bytes 737288 | tf_op jit(solution)/shard_map/ppermute | solution.py:159
  5.8 14.0 %collective-permute-start.1 = (bf16[160,768]{1,0:T(8,128)(2,1)}, bf16[160,768]{1,0:T(8,128)(2,1)S(1)}, u32[]{:S(2)}, u32[]{:S(2)}) collective-permute-start(bf16[160,768]{1,0:T(8,128)(2,1)} %bitcast.16), channel_id=1, source_target_pairs={{2,0},{3,1},{4,2},{5,3},{6,4},{7,5},{8,6},{9,7},{10,8},{11,9},{12,... | collective-permute-start | bytes 737288 | tf_op jit(solution)/shard_map/ppermute | solution.py:160
  19.9 4.2 %collective-permute-done.refs_1_ = bf16[160,768]{1,0:T(8,128)(2,1)S(1)} collective-permute-done((bf16[160,768]{1,0:T(8,128)(2,1)}, bf16[160,768]{1,0:T(8,128)(2,1)S(1)}, u32[]{:S(2)}, u32[]{:S(2)}) %collective-permute-start) | collective-permute-done | bytes 245792 | tf_op jit(solution)/shard_map/ppermute | solution.py:159
  24.1 1.9 %collective-permute-start.2 = (bf16[160,768]{1,0:T(8,128)(2,1)S(1)}, bf16[160,768]{1,0:T(8,128)(2,1)S(1)}, u32[]{:S(2)}, u32[]{:S(2)}) collective-permute-start(bf16[160,768]{1,0:T(8,128)(2,1)S(1)} %collective-permute-done.refs_1_), channel_id=1, source_target_pairs={{0,2},{1,3},{2,4},{3,5},{4,6},{5,7},{6,8},{7,9},{8,10},{9,11},{10,... | collective-permute-start | bytes 737288 | tf_op jit(solution)/shard_map/ppermute | solution.py:159
  26.0 0.0 collective-permute-done.1.refs_2_
  26.0 5.1 %collective-permute-start.3 = (bf16[160,768]{1,0:T(8,128)(2,1)S(1)}, bf16[160,768]{1,0:T(8,128)(2,1)S(1)}, u32[]{:S(2)}, u32[]{:S(2)}) collective-permute-start(bf16[160,768]{1,0:T(8,128)(2,1)S(1)} %collective-permute-done.1.refs_2_), channel_id=1, source_target_pairs={{2,0},{3,1},{4,2},{5,3},{6,4},{7,5},{8,6},{9,7},{10,8},{11,9},{12,... | collective-permute-start | bytes 737288 | tf_op jit(solution)/shard_map/ppermute | solution.py:160
  31.2 3.2 %collective-permute-done.2.refs_3_ = bf16[160,768]{1,0:T(8,128)(2,1)S(1)} collective-permute-done((bf16[160,768]{1,0:T(8,128)(2,1)S(1)}, bf16[160,768]{1,0:T(8,128)(2,1)S(1)}, u32[]{:S(2)}, u32[]{:S(2)}) %collective-permute-start.2) | collective-permute-done | bytes 245792 | tf_op jit(solution)/shard_map/ppermute | solution.py:159
  34.3 1.9 %collective-permute-start.4 = (bf16[160,768]{1,0:T(8,128)(2,1)S(1)}, bf16[160,768]{1,0:T(8,128)(2,1)S(1)}, u32[]{:S(2)}, u32[]{:S(2)}) collective-permute-start(bf16[160,768]{1,0:T(8,128)(2,1)S(1)} %collective-permute-done.2.refs_3_), channel_id=1, source_target_pairs={{0,2},{1,3},{2,4},{3,5},{4,6},{5,7},{6,8},{7,9},{8,10},{9,11},{10,... | collective-permute-start | bytes 737288 | tf_op jit(solution)/shard_map/ppermute | solution.py:159
  36.3 0.0 collective-permute-done.3.refs_4_
  36.3 5.1 %collective-permute-start.5 = (bf16[160,768]{1,0:T(8,128)(2,1)S(1)}, bf16[160,768]{1,0:T(8,128)(2,1)S(1)}, u32[]{:S(2)}, u32[]{:S(2)}) collective-permute-start(bf16[160,768]{1,0:T(8,128)(2,1)S(1)} %collective-permute-done.3.refs_4_), channel_id=1, source_target_pairs={{2,0},{3,1},{4,2},{5,3},{6,4},{7,5},{8,6},{9,7},{10,8},{11,9},{12,... | collective-permute-start | bytes 737288 | tf_op jit(solution)/shard_map/ppermute | solution.py:160
  41.4 2.2 %collective-permute-done.4.refs_5_ = bf16[160,768]{1,0:T(8,128)(2,1)S(1)} collective-permute-done((bf16[160,768]{1,0:T(8,128)(2,1)S(1)}, bf16[160,768]{1,0:T(8,128)(2,1)S(1)}, u32[]{:S(2)}, u32[]{:S(2)}) %collective-permute-start.4) | collective-permute-done | bytes 245792 | tf_op jit(solution)/shard_map/ppermute | solution.py:159
  43.7 1.9 %collective-permute-start.6 = (bf16[160,768]{1,0:T(8,128)(2,1)S(1)}, bf16[160,768]{1,0:T(8,128)(2,1)S(1)}, u32[]{:S(2)}, u32[]{:S(2)}) collective-permute-start(bf16[160,768]{1,0:T(8,128)(2,1)S(1)} %collective-permute-done.4.refs_5_), channel_id=1, source_target_pairs={{0,2},{1,3},{2,4},{3,5},{4,6},{5,7},{6,8},{7,9},{8,10},{9,11},{10,... | collective-permute-start | bytes 737288 | tf_op jit(solution)/shard_map/ppermute | solution.py:162
  45.6 0.7 bitcast_convert_fusion
  46.3 0.0 copy-start.1
  46.3 1.1 copy-done.1
  47.4 0.8 copy-done.3
  48.2 0.7 copy-done.4
  48.9 0.7 copy-done.5
  49.6 0.4 shard_map.95
  50.0 0.0 collective-permute-done.5.refs_6_
  50.0 3.0 %collective-permute-done.6.refs_7_ = bf16[160,768]{1,0:T(8,128)(2,1)S(1)} collective-permute-done((bf16[160,768]{1,0:T(8,128)(2,1)S(1)}, bf16[160,768]{1,0:T(8,128)(2,1)S(1)}, u32[]{:S(2)}, u32[]{:S(2)}) %collective-permute-start.6) | collective-permute-done | bytes 245792 | tf_op jit(solution)/shard_map/ppermute | solution.py:162
  52.9 0.9 copy-done.2
  53.9 0.7 shard_map.96
  54.6 1.9 %collective-permute-start.7 = (bf16[1280,768]{1,0:T(8,128)(2,1)S(1)}, bf16[1280,768]{1,0:T(8,128)(2,1)S(1)}, u32[]{:S(2)}, u32[]{:S(2)}) collective-permute-start(bf16[1280,768]{1,0:T(8,128)(2,1)S(1)} %get-tuple-element.11.mine_ref), channel_id=1, source_target_pairs={{1,0},{0,1},{3,2},{2,3},{5,4},{4,5},{7,6},{6,7},{9,8},{8,9},{11,10... | collective-permute-start | bytes 5898248 | tf_op jit(solution)/shard_map/ppermute | solution.py:194
  56.5 3.9 %collective-permute-done.7.other_ref = bf16[1280,768]{1,0:T(8,128)(2,1)S(1)} collective-permute-done((bf16[1280,768]{1,0:T(8,128)(2,1)S(1)}, bf16[1280,768]{1,0:T(8,128)(2,1)S(1)}, u32[]{:S(2)}, u32[]{:S(2)}) %collective-permute-start.7) | collective-permute-done | bytes 1966112 | tf_op jit(solution)/shard_map/ppermute | solution.py:194
  60.4 0.0 copy-done
  60.4 0.7 shard_map.97
  61.1 10.4 %all_to_all.10.recv_ref = f32[16,8,128]{2,1,0:T(8,128)S(1)} all-to-all(f32[16,8,128]{2,1,0:T(8,128)S(1)} %shard_map.97), channel_id=1, replica_groups=mesh['dp'=64,'tensor'=16] {'tensor'}, dimensions={0} | all-to-all | bytes 131072 | tf_op jit(solution)/shard_map/all_to_all | solution.py:202
  71.5 1.3 %shard_map.98 = bf16[64,56,128]{2,1,0:T(8,128)(2,1)S(1)} custom-call(f32[16,8,128]{2,1,0:T(8,128)S(1)} %all_to_all.10.recv_ref, f32[3,8,128]{2,1,0:T(8,128)S(1)} %get-tuple-element.12.aux_ref, f32[8,128]{1,0:T(8,128)S(1)} %get-tuple-element.13.sums_ref, bf16[160,768]{1,0:T(8,128)(2,1)S(1)} %bitcast.14, bf16[1280,768]{1,0:T(8,128)(2,1)S(1)} %get-tuple-element.11.mine_ref, ...), custom_call_target="tpu_custom_call" | custom-call | tf_op jit(solution)/shard_map/pallas_call | solution.py:203
  72.8 41.6 %all_to_all.11.recv_ref = bf16[64,56,128]{2,1,0:T(8,128)(2,1)S(1)} all-to-all(bf16[64,56,128]{2,1,0:T(8,128)(2,1)S(1)} %shard_map.98), channel_id=1, replica_groups=mesh['dp'=64,'tensor'=16] {'dp'}, dimensions={0} | all-to-all | bytes 1835008 | tf_op jit(solution)/shard_map/all_to_all | solution.py:210
  114.4 0.8 shard_map.99
  115.2 0.5 slice_bitcast_fusion
  (5 shorter events, 0.0 us)
Async XLA Ops:
  0.6 23.5 %collective-permute-start = (bf16[160,768]{1,0:T(8,128)(2,1)}, bf16[160,768]{1,0:T(8,128)(2,1)S(1)}, u32[]{:S(2)}, u32[]{:S(2)}) collective-permute-start(bf16[160,768]{1,0:T(8,128)(2,1)} %bitcast.15), channel_id=1, source_target_pairs={{0,2},{1,3},{2,4},{3,5},{4,6},{5,7},{6,8},{7,9},{8,10},{9,11},{10,... | collective-permute-start | bytes 737288 | tf_op jit(solution)/shard_map/ppermute | solution.py:159
  5.8 20.2 %collective-permute-start.1 = (bf16[160,768]{1,0:T(8,128)(2,1)}, bf16[160,768]{1,0:T(8,128)(2,1)S(1)}, u32[]{:S(2)}, u32[]{:S(2)}) collective-permute-start(bf16[160,768]{1,0:T(8,128)(2,1)} %bitcast.16), channel_id=1, source_target_pairs={{2,0},{3,1},{4,2},{5,3},{6,4},{7,5},{8,6},{9,7},{10,8},{11,9},{12,... | collective-permute-start | bytes 737288 | tf_op jit(solution)/shard_map/ppermute | solution.py:160
  24.1 10.2 %collective-permute-start.2 = (bf16[160,768]{1,0:T(8,128)(2,1)S(1)}, bf16[160,768]{1,0:T(8,128)(2,1)S(1)}, u32[]{:S(2)}, u32[]{:S(2)}) collective-permute-start(bf16[160,768]{1,0:T(8,128)(2,1)S(1)} %collective-permute-done.refs_1_), channel_id=1, source_target_pairs={{0,2},{1,3},{2,4},{3,5},{4,6},{5,7},{6,8},{7,9},{8,10},{9,11},{10,... | collective-permute-start | bytes 737288 | tf_op jit(solution)/shard_map/ppermute | solution.py:159
  26.0 10.2 %collective-permute-start.3 = (bf16[160,768]{1,0:T(8,128)(2,1)S(1)}, bf16[160,768]{1,0:T(8,128)(2,1)S(1)}, u32[]{:S(2)}, u32[]{:S(2)}) collective-permute-start(bf16[160,768]{1,0:T(8,128)(2,1)S(1)} %collective-permute-done.1.refs_2_), channel_id=1, source_target_pairs={{2,0},{3,1},{4,2},{5,3},{6,4},{7,5},{8,6},{9,7},{10,8},{11,9},{12,... | collective-permute-start | bytes 737288 | tf_op jit(solution)/shard_map/ppermute | solution.py:160
  34.3 9.3 %collective-permute-start.4 = (bf16[160,768]{1,0:T(8,128)(2,1)S(1)}, bf16[160,768]{1,0:T(8,128)(2,1)S(1)}, u32[]{:S(2)}, u32[]{:S(2)}) collective-permute-start(bf16[160,768]{1,0:T(8,128)(2,1)S(1)} %collective-permute-done.2.refs_3_), channel_id=1, source_target_pairs={{0,2},{1,3},{2,4},{3,5},{4,6},{5,7},{6,8},{7,9},{8,10},{9,11},{10,... | collective-permute-start | bytes 737288 | tf_op jit(solution)/shard_map/ppermute | solution.py:159
  36.3 13.7 %collective-permute-start.5 = (bf16[160,768]{1,0:T(8,128)(2,1)S(1)}, bf16[160,768]{1,0:T(8,128)(2,1)S(1)}, u32[]{:S(2)}, u32[]{:S(2)}) collective-permute-start(bf16[160,768]{1,0:T(8,128)(2,1)S(1)} %collective-permute-done.3.refs_4_), channel_id=1, source_target_pairs={{2,0},{3,1},{4,2},{5,3},{6,4},{7,5},{8,6},{9,7},{10,8},{11,9},{12,... | collective-permute-start | bytes 737288 | tf_op jit(solution)/shard_map/ppermute | solution.py:160
  43.7 9.3 %collective-permute-start.6 = (bf16[160,768]{1,0:T(8,128)(2,1)S(1)}, bf16[160,768]{1,0:T(8,128)(2,1)S(1)}, u32[]{:S(2)}, u32[]{:S(2)}) collective-permute-start(bf16[160,768]{1,0:T(8,128)(2,1)S(1)} %collective-permute-done.4.refs_5_), channel_id=1, source_target_pairs={{0,2},{1,3},{2,4},{3,5},{4,6},{5,7},{6,8},{7,9},{8,10},{9,11},{10,... | collective-permute-start | bytes 737288 | tf_op jit(solution)/shard_map/ppermute | solution.py:162
  46.3 1.1 copy-start.1
  47.4 0.8 copy-start.3
  48.2 0.7 copy-start.4
  48.9 0.7 copy-start.5
  49.5 10.9 %copy-start = (bf16[768,160]{0,1:T(8,128)(2,1)S(1)}, bf16[768,160]{0,1:T(8,128)(2,1)}, u32[]{:S(2)}) copy-start(bf16[768,160]{0,1:T(8,128)(2,1)} %param.8) | copy-start | bytes 737284
  52.9 0.9 copy-start.2
  54.6 5.9 %collective-permute-start.7 = (bf16[1280,768]{1,0:T(8,128)(2,1)S(1)}, bf16[1280,768]{1,0:T(8,128)(2,1)S(1)}, u32[]{:S(2)}, u32[]{:S(2)}) collective-permute-start(bf16[1280,768]{1,0:T(8,128)(2,1)S(1)} %get-tuple-element.11.mine_ref), channel_id=1, source_target_pairs={{1,0},{0,1},{3,2},{2,3},{5,4},{4,5},{7,6},{6,7},{9,8},{8,9},{11,10... | collective-permute-start | bytes 5898248 | tf_op jit(solution)/shard_map/ppermute | solution.py:194

commit v6 on v5

--- a/solution.py
+++ b/solution.py
@@ -8,8 +8,8 @@
 EPS_LOW = 0.2
 EPS_HIGH = 0.28
 LOSS_SCALE = 16384.0
-N_DP = 64
 N_TENSOR = 16
+LINE_ROWS = 408
 CHUNK_ROWS = 56
 LANES = 128
 N_Z = 8
@@ -81,6 +81,23 @@
         out_ref[k] = block
 
 
+def in_three(value, lane):
+    high = value.astype(jnp.bfloat16).astype(jnp.float32)
+    middle = (value - high).astype(jnp.bfloat16).astype(jnp.float32)
+    low = value - high - middle
+    return jnp.where(lane < 36, high, jnp.where(lane < 40, middle, low))
+
+
+def pick(row, lane, k):
+    mine = (lane == 32 + k) | (lane == 36 + k) | (lane == 40 + k)
+    return jnp.sum(jnp.where(mine, row, 0.0), axis=1, keepdims=True)
+
+
+def slot(k, g):
+    place = 5 * k + g
+    return 320 + 8 * (place // 4), 32 * (place % 4)
+
+
 def grad_kernel(
     recv_ref,
     aux_ref,
@@ -89,6 +106,7 @@
     mine_ref,
     other_ref,
     out_ref,
+    wide_ref,
 ):
     width = attn_ref.shape[0]
     shift = jnp.sum(recv_ref[...], axis=0)
@@ -103,25 +121,48 @@
     lane = lax.broadcasted_iota(jnp.int32, (8, LANES), 1)
     is_loss = (lane == 35) | (lane == 39) | (lane == 43)
     value = jnp.where(is_loss, loss, sums_ref[...])
-    high = value.astype(jnp.bfloat16).astype(jnp.float32)
-    middle = (value - high).astype(jnp.bfloat16).astype(jnp.float32)
-    low = value - high - middle
-    stats = jnp.where(lane < 36, high, jnp.where(lane < 40, middle, low))[:, 32:]
+    wide_ref[:, LINE_ROWS - 8 :] = jnp.broadcast_to(in_three(value, lane)[None], (8, 8, LANES))
+    core = lax.axis_index("tensor") & 1
     for place in range(N_TENSOR):
         k = place % N_Z
         piece = (mine_ref, other_ref)[place // N_Z][width * k : width * k + width]
         product = lax.dot_general(
             piece, scaled, (((1,), (1,)), ((), ())), preferred_element_type=jnp.float32
         )
-        block = piece_index(place)
+        side = core ^ (place // N_Z)
         for q in range(4):
             part = product[40 * q : 40 * q + 40]
-            rest = part[:, LANES:]
-            first = jnp.concatenate([rest[8 * k : 8 * k + 8] for k in range(4)], axis=1)
-            second = jnp.concatenate([rest[32:40], stats], axis=1)
-            out_ref[4 * block + q] = jnp.concatenate([part[:, :LANES], first, second], axis=0).astype(
-                jnp.bfloat16
-            )
+            wide_ref[4 * side + q, 40 * k : 40 * k + 40] = part[:, :LANES]
+            for g in range(5):
+                row, column = slot(k, g)
+                wide_ref[4 * side + q, row : row + 8, column : column + 32] = part[
+                    8 * g : 8 * g + 8, LANES:
+                ]
+    out_ref[...] = wide_ref[...].astype(jnp.bfloat16)
+
+
+def line_kernel(recv_ref, out_ref):
+    total = jnp.sum(recv_ref[...].astype(jnp.float32), axis=0)
+    lane = lax.broadcasted_iota(jnp.int32, (8, LANES), 1)
+    row = total[LINE_ROWS - 8 :]
+    value = jnp.where((lane >= 32) & (lane < 44), pick(row, lane, 3), 0.0)
+    for k in range(3):
+        value = jnp.where((lane >= 32) & (lane < 44) & ((lane & 3) == k), pick(row, lane, k), value)
+    stats = in_three(value, lane)[:, 32:]
+    place_z = lax.axis_index("tensor") >> 1
+    for k in range(N_Z):
+        parts = []
+        for g in range(5):
+            row, column = slot(k, g)
+            parts.append(total[row : row + 8, column : column + 32])
+        chunk = [
+            total[40 * k : 40 * k + 40],
+            jnp.concatenate(parts[:4], axis=1),
+            jnp.concatenate([parts[4], stats], axis=1),
+        ]
+        out_ref[(place_z + N_Z + STEPS[k]) & (N_Z - 1)] = jnp.concatenate(chunk, axis=0).astype(
+            jnp.bfloat16
+        )
 
 
 def finish_kernel(recv_ref, grad_ref, stats_ref):
@@ -130,15 +171,11 @@
     lane = lax.broadcasted_iota(jnp.int32, (1, LANES), 1)
     row = second[0:1]
 
-    def pick(k):
-        mine = (lane == 32 + k) | (lane == 36 + k) | (lane == 40 + k)
-        return jnp.sum(jnp.where(mine, row, 0.0), axis=1, keepdims=True)
-
-    divisor = jnp.maximum(pick(0), 1.0)
+    divisor = jnp.maximum(pick(row, lane, 0), 1.0)
     rest = jnp.concatenate([first[:, 32 * k : 32 * k + 32] for k in range(4)] + [second[:, :32]], axis=0)
     grad_ref[...] = jnp.concatenate([total[:40], rest], axis=1) / divisor
     stats_ref[...] = (
-        jnp.where(lane == 0, -pick(3), jnp.where(lane == 1, pick(1), jnp.where(lane == 2, pick(2), 0.0)))
+        jnp.where(lane == 0, -pick(row, lane, 3), jnp.where(lane == 1, pick(row, lane, 1), jnp.where(lane == 2, pick(row, lane, 2), 0.0)))
         / divisor
     )
 
@@ -204,10 +241,21 @@
         grad_kernel,
         in_specs=[vmem_spec()] * 6,
         out_specs=vmem_spec(),
-        out_shape=jax.ShapeDtypeStruct((N_DP, CHUNK_ROWS, LANES), jnp.bfloat16),
+        out_shape=jax.ShapeDtypeStruct((8, LINE_ROWS, LANES), jnp.bfloat16),
+        scratch_shapes=[pltpu.VMEM((8, LINE_ROWS, LANES), jnp.float32)],
         compiler_params=params,
     )(shifts, aux, sums, attn_t, mine, other)
-    received = lax.all_to_all(chunks, "dp", 0, 0, tiled=True)
+    along_y = [[8 * x + y for y in range(8)] for x in range(8)]
+    along_x = [[8 * x + y for x in range(8)] for y in range(8)]
+    received = lax.all_to_all(chunks, "dp", 0, 0, tiled=True, axis_index_groups=along_y)
+    chunks = pl.pallas_call(
+        line_kernel,
+        in_specs=[vmem_spec()],
+        out_specs=vmem_spec(),
+        out_shape=jax.ShapeDtypeStruct((8, CHUNK_ROWS, LANES), jnp.bfloat16),
+        compiler_params=params,
+    )(received)
+    received = lax.all_to_all(chunks, "dp", 0, 0, tiled=True, axis_index_groups=along_x)
     grad_t, stats = pl.pallas_call(
         finish_kernel,
         in_specs=[vmem_spec()],

time: 116 us -> 122 us (1.052)
  the two profiles are of different devices: /device:TPU:4 before, /device:TPU:1 now
where the time goes in v6:
time: 122 us; the launch traced here: 121 us
  blocking collectives  56.5 us (46%)
  starting transfers between devices  41.6 us (34%)
  waiting for transfers between devices  12.7 us (10%)
  local copies, waits for them, and re-layouts  4.73 us (4%)
  Pallas kernels  3.98 us (3%)
    all_to_all x1, blocking collectives, body(): lax.all_to_all(chunks, 'dp', 0, 0, tiled=True, axis_index_groups=along_y)  31.7 us
    ppermute x3, starting transfers between devices, body(): falling = lax.ppermute(falling, 'tensor', down)  23.2 us
    all_to_all x1, blocking collectives, body(): lax.all_to_all(chunks, 'dp', 0, 0, tiled=True, axis_index_groups=along_x)  14.2 us
    all_to_all x1, blocking collectives, body(): shifts = lax.all_to_all(partial_shift, 'tensor', 0, 0, tiled=True)  10.6 us
    ppermute x3, starting transfers between devices, body(): rising = lax.ppermute(rising, 'tensor', up)  9.56 us
    ppermute x3, waiting for transfers between devices, body(): rising = lax.ppermute(rising, 'tensor', up)  7.31 us
    ppermute x1, starting transfers between devices, body(): other = lax.ppermute(mine, 'tensor', swap)  6.9 us
    unnamed x12, local copies, waits for them, and re-layouts  4.22 us
  transfers between devices with their start and end apart: 8, of which 5 were waited for; matrix products, arithmetic and copies ran while one was open for 1% of the time, Pallas kernels for 0%

profile of v6, /device:TPU:1, one launch (start us, length us, event | category | flops | bytes accessed | tf_op | source)
XLA Modules:
  0.0 120.9 jit_solution(17176161316004268803)
XLA Ops:
  0.6 5.7 %collective-permute-start = (bf16[160,768]{1,0:T(8,128)(2,1)}, bf16[160,768]{1,0:T(8,128)(2,1)S(1)}, u32[]{:S(2)}, u32[]{:S(2)}) collective-permute-start(bf16[160,768]{1,0:T(8,128)(2,1)} %bitcast.15), channel_id=1, source_target_pairs={{0,2},{1,3},{2,4},{3,5},{4,6},{5,7},{6,8},{7,9},{8,10},{9,11},{10,... | collective-permute-start | bytes 737288 | tf_op jit(solution)/shard_map/ppermute | solution.py:196
  6.4 14.0 %collective-permute-start.1 = (bf16[160,768]{1,0:T(8,128)(2,1)}, bf16[160,768]{1,0:T(8,128)(2,1)S(1)}, u32[]{:S(2)}, u32[]{:S(2)}) collective-permute-start(bf16[160,768]{1,0:T(8,128)(2,1)} %bitcast.16), channel_id=1, source_target_pairs={{2,0},{3,1},{4,2},{5,3},{6,4},{7,5},{8,6},{9,7},{10,8},{11,9},{12,... | collective-permute-start | bytes 737288 | tf_op jit(solution)/shard_map/ppermute | solution.py:197
  20.4 3.4 %collective-permute-done.refs_1_ = bf16[160,768]{1,0:T(8,128)(2,1)S(1)} collective-permute-done((bf16[160,768]{1,0:T(8,128)(2,1)}, bf16[160,768]{1,0:T(8,128)(2,1)S(1)}, u32[]{:S(2)}, u32[]{:S(2)}) %collective-permute-start) | collective-permute-done | bytes 245792 | tf_op jit(solution)/shard_map/ppermute | solution.py:196
  23.8 1.9 %collective-permute-start.2 = (bf16[160,768]{1,0:T(8,128)(2,1)S(1)}, bf16[160,768]{1,0:T(8,128)(2,1)S(1)}, u32[]{:S(2)}, u32[]{:S(2)}) collective-permute-start(bf16[160,768]{1,0:T(8,128)(2,1)S(1)} %collective-permute-done.refs_1_), channel_id=1, source_target_pairs={{0,2},{1,3},{2,4},{3,5},{4,6},{5,7},{6,8},{7,9},{8,10},{9,11},{10,... | collective-permute-start | bytes 737288 | tf_op jit(solution)/shard_map/ppermute | solution.py:196
  25.8 0.0 collective-permute-done.1.refs_2_
  25.8 4.6 %collective-permute-start.3 = (bf16[160,768]{1,0:T(8,128)(2,1)S(1)}, bf16[160,768]{1,0:T(8,128)(2,1)S(1)}, u32[]{:S(2)}, u32[]{:S(2)}) collective-permute-start(bf16[160,768]{1,0:T(8,128)(2,1)S(1)} %collective-permute-done.1.refs_2_), channel_id=1, source_target_pairs={{2,0},{3,1},{4,2},{5,3},{6,4},{7,5},{8,6},{9,7},{10,8},{11,9},{12,... | collective-permute-start | bytes 737288 | tf_op jit(solution)/shard_map/ppermute | solution.py:197
  30.3 2.3 %collective-permute-done.2.refs_3_ = bf16[160,768]{1,0:T(8,128)(2,1)S(1)} collective-permute-done((bf16[160,768]{1,0:T(8,128)(2,1)S(1)}, bf16[160,768]{1,0:T(8,128)(2,1)S(1)}, u32[]{:S(2)}, u32[]{:S(2)}) %collective-permute-start.2) | collective-permute-done | bytes 245792 | tf_op jit(solution)/shard_map/ppermute | solution.py:196
  32.6 1.9 %collective-permute-start.4 = (bf16[160,768]{1,0:T(8,128)(2,1)S(1)}, bf16[160,768]{1,0:T(8,128)(2,1)S(1)}, u32[]{:S(2)}, u32[]{:S(2)}) collective-permute-start(bf16[160,768]{1,0:T(8,128)(2,1)S(1)} %collective-permute-done.2.refs_3_), channel_id=1, source_target_pairs={{0,2},{1,3},{2,4},{3,5},{4,6},{5,7},{6,8},{7,9},{8,10},{9,11},{10,... | collective-permute-start | bytes 737288 | tf_op jit(solution)/shard_map/ppermute | solution.py:196
  34.5 0.0 collective-permute-done.3.refs_4_
  34.5 4.6 %collective-permute-start.5 = (bf16[160,768]{1,0:T(8,128)(2,1)S(1)}, bf16[160,768]{1,0:T(8,128)(2,1)S(1)}, u32[]{:S(2)}, u32[]{:S(2)}) collective-permute-start(bf16[160,768]{1,0:T(8,128)(2,1)S(1)} %collective-permute-done.3.refs_4_), channel_id=1, source_target_pairs={{2,0},{3,1},{4,2},{5,3},{6,4},{7,5},{8,6},{9,7},{10,8},{11,9},{12,... | collective-permute-start | bytes 737288 | tf_op jit(solution)/shard_map/ppermute | solution.py:197
  39.1 1.6 %collective-permute-done.4.refs_5_ = bf16[160,768]{1,0:T(8,128)(2,1)S(1)} collective-permute-done((bf16[160,768]{1,0:T(8,128)(2,1)S(1)}, bf16[160,768]{1,0:T(8,128)(2,1)S(1)}, u32[]{:S(2)}, u32[]{:S(2)}) %collective-permute-start.4) | collective-permute-done | bytes 245792 | tf_op jit(solution)/shard_map/ppermute | solution.py:196
  40.8 1.9 %collective-permute-start.6 = (bf16[160,768]{1,0:T(8,128)(2,1)S(1)}, bf16[160,768]{1,0:T(8,128)(2,1)S(1)}, u32[]{:S(2)}, u32[]{:S(2)}) collective-permute-start(bf16[160,768]{1,0:T(8,128)(2,1)S(1)} %collective-permute-done.4.refs_5_), channel_id=1, source_target_pairs={{0,2},{1,3},{2,4},{3,5},{4,6},{5,7},{6,8},{7,9},{8,10},{9,11},{10,... | collective-permute-start | bytes 737288 | tf_op jit(solution)/shard_map/ppermute | solution.py:199
  42.7 0.7 bitcast_convert_fusion
  43.4 1.1 copy-done.1
  44.5 0.8 copy-done.3
  45.3 0.7 copy-done.4
  46.0 0.7 copy-done.5
  46.7 0.4 shard_map.95
  47.1 0.0 collective-permute-done.5.refs_6_
  47.1 1.8 %collective-permute-done.6.refs_7_ = bf16[160,768]{1,0:T(8,128)(2,1)S(1)} collective-permute-done((bf16[160,768]{1,0:T(8,128)(2,1)S(1)}, bf16[160,768]{1,0:T(8,128)(2,1)S(1)}, u32[]{:S(2)}, u32[]{:S(2)}) %collective-permute-start.6) | collective-permute-done | bytes 245792 | tf_op jit(solution)/shard_map/ppermute | solution.py:199
  48.9 0.9 copy-done.2
  49.8 0.7 shard_map.96
  50.5 6.9 %collective-permute-start.7 = (bf16[1280,768]{1,0:T(8,128)(2,1)S(1)}, bf16[1280,768]{1,0:T(8,128)(2,1)S(1)}, u32[]{:S(2)}, u32[]{:S(2)}) collective-permute-start(bf16[1280,768]{1,0:T(8,128)(2,1)S(1)} %get-tuple-element.11.mine_ref), channel_id=1, source_target_pairs={{1,0},{0,1},{3,2},{2,3},{5,4},{4,5},{7,6},{6,7},{9,8},{8,9},{11,10... | collective-permute-start | bytes 5898248 | tf_op jit(solution)/shard_map/ppermute | solution.py:231
  57.4 3.6 %collective-permute-done.7.other_ref = bf16[1280,768]{1,0:T(8,128)(2,1)S(1)} collective-permute-done((bf16[1280,768]{1,0:T(8,128)(2,1)S(1)}, bf16[1280,768]{1,0:T(8,128)(2,1)S(1)}, u32[]{:S(2)}, u32[]{:S(2)}) %collective-permute-start.7) | collective-permute-done | bytes 1966112 | tf_op jit(solution)/shard_map/ppermute | solution.py:231
  61.0 0.7 shard_map.97
  61.7 10.6 %all_to_all.15.recv_ref = f32[16,8,128]{2,1,0:T(8,128)S(1)} all-to-all(f32[16,8,128]{2,1,0:T(8,128)S(1)} %shard_map.97), channel_id=1, replica_groups=mesh['dp'=64,'tensor'=16] {'tensor'}, dimensions={0} | all-to-all | bytes 131072 | tf_op jit(solution)/shard_map/all_to_all | solution.py:239
  72.3 1.4 %shard_map.98 = bf16[8,408,128]{2,1,0:T(8,128)(2,1)S(1)} custom-call(f32[16,8,128]{2,1,0:T(8,128)S(1)} %all_to_all.15.recv_ref, f32[3,8,128]{2,1,0:T(8,128)S(1)} %get-tuple-element.12.aux_ref, f32[8,128]{1,0:T(8,128)S(1)} %get-tuple-element.13.sums_ref, bf16[160,768]{1,0:T(8,128)(2,1)S(1)} %bitcast.14, bf16[1280,768]{1,0:T(8,128)(2,1)S(1)} %get-tuple-element.11.mine_ref, ...), custom_call_target="tpu_custom_call" | custom-call | tf_op jit(solution)/shard_map/pallas_call | solution.py:240
  73.7 31.7 %all_to_all.16.recv_ref = bf16[8,408,128]{2,1,0:T(8,128)(2,1)S(1)} all-to-all(bf16[8,408,128]{2,1,0:T(8,128)(2,1)S(1)} %shard_map.98), channel_id=1, replica_groups={{0,16,32,48,64,80,96,112},{128,144,160,176,192,208,224,240},{256,272,28..., dimensions={0} | all-to-all | bytes 1671168 | tf_op jit(solution)/shard_map/all_to_all | solution.py:250
  105.4 0.1 shard_map.99
  105.5 14.2 %all_to_all.17.recv_ref = bf16[8,56,128]{2,1,0:T(8,128)(2,1)S(1)} all-to-all(bf16[8,56,128]{2,1,0:T(8,128)(2,1)S(1)} %shard_map.99), channel_id=1, replica_groups={{0,128,256,384,512,640,768,896},{16,144,272,400,528,656,784,912},{32,16..., dimensions={0} | all-to-all | bytes 229376 | tf_op jit(solution)/shard_map/all_to_all | solution.py:258
  119.7 0.7 shard_map.100
  120.4 0.5 slice_bitcast_fusion
  (7 shorter events, 0.0 us)
Async XLA Ops:
  0.6 23.2 %collective-permute-start = (bf16[160,768]{1,0:T(8,128)(2,1)}, bf16[160,768]{1,0:T(8,128)(2,1)S(1)}, u32[]{:S(2)}, u32[]{:S(2)}) collective-permute-start(bf16[160,768]{1,0:T(8,128)(2,1)} %bitcast.15), channel_id=1, source_target_pairs={{0,2},{1,3},{2,4},{3,5},{4,6},{5,7},{6,8},{7,9},{8,10},{9,11},{10,... | collective-permute-start | bytes 737288 | tf_op jit(solution)/shard_map/ppermute | solution.py:196
  6.4 19.4 %collective-permute-start.1 = (bf16[160,768]{1,0:T(8,128)(2,1)}, bf16[160,768]{1,0:T(8,128)(2,1)S(1)}, u32[]{:S(2)}, u32[]{:S(2)}) collective-permute-start(bf16[160,768]{1,0:T(8,128)(2,1)} %bitcast.16), channel_id=1, source_target_pairs={{2,0},{3,1},{4,2},{5,3},{6,4},{7,5},{8,6},{9,7},{10,8},{11,9},{12,... | collective-permute-start | bytes 737288 | tf_op jit(solution)/shard_map/ppermute | solution.py:197
  23.8 8.8 %collective-permute-start.2 = (bf16[160,768]{1,0:T(8,128)(2,1)S(1)}, bf16[160,768]{1,0:T(8,128)(2,1)S(1)}, u32[]{:S(2)}, u32[]{:S(2)}) collective-permute-start(bf16[160,768]{1,0:T(8,128)(2,1)S(1)} %collective-permute-done.refs_1_), channel_id=1, source_target_pairs={{0,2},{1,3},{2,4},{3,5},{4,6},{5,7},{6,8},{7,9},{8,10},{9,11},{10,... | collective-permute-start | bytes 737288 | tf_op jit(solution)/shard_map/ppermute | solution.py:196
  25.8 8.8 %collective-permute-start.3 = (bf16[160,768]{1,0:T(8,128)(2,1)S(1)}, bf16[160,768]{1,0:T(8,128)(2,1)S(1)}, u32[]{:S(2)}, u32[]{:S(2)}) collective-permute-start(bf16[160,768]{1,0:T(8,128)(2,1)S(1)} %collective-permute-done.1.refs_2_), channel_id=1, source_target_pairs={{2,0},{3,1},{4,2},{5,3},{6,4},{7,5},{8,6},{9,7},{10,8},{11,9},{12,... | collective-permute-start | bytes 737288 | tf_op jit(solution)/shard_map/ppermute | solution.py:197
  32.6 8.1 %collective-permute-start.4 = (bf16[160,768]{1,0:T(8,128)(2,1)S(1)}, bf16[160,768]{1,0:T(8,128)(2,1)S(1)}, u32[]{:S(2)}, u32[]{:S(2)}) collective-permute-start(bf16[160,768]{1,0:T(8,128)(2,1)S(1)} %collective-permute-done.2.refs_3_), channel_id=1, source_target_pairs={{0,2},{1,3},{2,4},{3,5},{4,6},{5,7},{6,8},{7,9},{8,10},{9,11},{10,... | collective-permute-start | bytes 737288 | tf_op jit(solution)/shard_map/ppermute | solution.py:196
  34.5 12.5 %collective-permute-start.5 = (bf16[160,768]{1,0:T(8,128)(2,1)S(1)}, bf16[160,768]{1,0:T(8,128)(2,1)S(1)}, u32[]{:S(2)}, u32[]{:S(2)}) collective-permute-start(bf16[160,768]{1,0:T(8,128)(2,1)S(1)} %collective-permute-done.3.refs_4_), channel_id=1, source_target_pairs={{2,0},{3,1},{4,2},{5,3},{6,4},{7,5},{8,6},{9,7},{10,8},{11,9},{12,... | collective-permute-start | bytes 737288 | tf_op jit(solution)/shard_map/ppermute | solution.py:197
  40.8 8.1 %collective-permute-start.6 = (bf16[160,768]{1,0:T(8,128)(2,1)S(1)}, bf16[160,768]{1,0:T(8,128)(2,1)S(1)}, u32[]{:S(2)}, u32[]{:S(2)}) collective-permute-start(bf16[160,768]{1,0:T(8,128)(2,1)S(1)} %collective-permute-done.4.refs_5_), channel_id=1, source_target_pairs={{0,2},{1,3},{2,4},{3,5},{4,6},{5,7},{6,8},{7,9},{8,10},{9,11},{10,... | collective-permute-start | bytes 737288 | tf_op jit(solution)/shard_map/ppermute | solution.py:199
  43.4 1.1 copy-start.1
  44.5 0.8 copy-start.3
  45.3 0.7 copy-start.4
  46.0 0.7 copy-start.5
  46.7 14.3 %copy-start = (bf16[768,160]{0,1:T(8,128)(2,1)S(1)}, bf16[768,160]{0,1:T(8,128)(2,1)}, u32[]{:S(2)}) copy-start(bf16[768,160]{0,1:T(8,128)(2,1)} %param.8) | copy-start | bytes 737284
  48.9 0.9 copy-start.2
  50.5 10.5 %collective-permute-start.7 = (bf16[1280,768]{1,0:T(8,128)(2,1)S(1)}, bf16[1280,768]{1,0:T(8,128)(2,1)S(1)}, u32[]{:S(2)}, u32[]{:S(2)}) collective-permute-start(bf16[1280,768]{1,0:T(8,128)(2,1)S(1)} %get-tuple-element.11.mine_ref), channel_id=1, source_target_pairs={{1,0},{0,1},{3,2},{2,3},{5,4},{4,5},{7,6},{6,7},{9,8},{8,9},{11,10... | collective-permute-start | bytes 5898248 | tf_op jit(solution)/shard_map/ppermute | solution.py:231

commit v7 on v5

--- a/solution.py
+++ b/solution.py
@@ -23,7 +23,8 @@
 def piece_index(place):
     device = lax.axis_index("tensor")
     side = (device & 1) ^ (place // N_Z)
-    return (((device >> 1) + N_Z + STEPS[place % N_Z]) & (N_Z - 1)) * 2 + side
+    step = (1 - 2 * side) * STEPS[place % N_Z]
+    return (((device >> 1) + N_Z + step) & (N_Z - 1)) * 2 + side
 
 
 def prepare_kernel(w_ref, gap_ref, size_ref, sign_ref, keep_ref, plan_ref, out_ref, aux_ref, sums_ref):
@@ -151,8 +152,9 @@
     up, down, swap = [], [], []
     for z in range(N_Z):
         for c in range(2):
-            up.append((2 * z + c, 2 * ((z + 1) % N_Z) + c))
-            down.append((2 * ((z + 1) % N_Z) + c, 2 * z + c))
+            lower, upper = 2 * z + c, 2 * ((z + 1) % N_Z) + c
+            up.append((upper, lower) if c else (lower, upper))
+            down.append((lower, upper) if c else (upper, lower))
             swap.append((2 * z + 1 - c, 2 * z + c))
     rising, falling, nearby = readout_t, readout_t, [readout_t]
     for _ in range(3):

time: 116 us -> 118 us (1.017)
  starting transfers between devices: 37.2 us -> 38.5 us
    ppermute x3, starting transfers between devices: 24.3 us -> 25.7 us  [body(): falling = lax.ppermute(falling, 'tensor', down)]
where the time goes in v7:
time: 118 us
  blocking collectives  52.2 us (44%)
  starting transfers between devices  38.5 us (33%)
  waiting for transfers between devices  16.9 us (14%)
  local copies, waits for them, and re-layouts  4.73 us (4%)
  Pallas kernels  3.87 us (3%)
    all_to_all x1, blocking collectives, body(): received = lax.all_to_all(chunks, 'dp', 0, 0, tiled=True)  41.6 us
    ppermute x3, starting transfers between devices, body(): falling = lax.ppermute(falling, 'tensor', down)  25.7 us
    all_to_all x1, blocking collectives, body(): shifts = lax.all_to_all(partial_shift, 'tensor', 0, 0, tiled=True)  10.6 us
    ppermute x3, waiting for transfers between devices, body(): rising = lax.ppermute(rising, 'tensor', up)  10 us
    ppermute x3, starting transfers between devices, body(): rising = lax.ppermute(rising, 'tensor', up)  9.01 us
    unnamed x12, local copies, waits for them, and re-layouts  4.22 us
    ppermute x1, waiting for transfers between devices, body(): other = lax.ppermute(mine, 'tensor', swap)  3.94 us
    ppermute x1, waiting for transfers between devices, body(): nearby.append(lax.ppermute(rising, 'tensor', up))  2.96 us
  transfers between devices with their start and end apart: 8, of which 5 were waited for; matrix products, arithmetic and copies ran while one was open for 1% of the time, Pallas kernels for 0%

profile of v7, /device:TPU:4, one launch (start us, length us, event | category | flops | bytes accessed | tf_op | source)
XLA Modules:
  0.0 117.7 jit_solution(1611284813124862050)
XLA Ops:
  0.6 5.2 %collective-permute-start = (bf16[160,768]{1,0:T(8,128)(2,1)}, bf16[160,768]{1,0:T(8,128)(2,1)S(1)}, u32[]{:S(2)}, u32[]{:S(2)}) collective-permute-start(bf16[160,768]{1,0:T(8,128)(2,1)} %bitcast.15), channel_id=1, source_target_pairs={{0,2},{3,1},{2,4},{5,3},{4,6},{7,5},{6,8},{9,7},{8,10},{11,9},{10,... | collective-permute-start | bytes 737288 | tf_op jit(solution)/shard_map/ppermute | solution.py:161
  5.8 14.0 %collective-permute-start.1 = (bf16[160,768]{1,0:T(8,128)(2,1)}, bf16[160,768]{1,0:T(8,128)(2,1)S(1)}, u32[]{:S(2)}, u32[]{:S(2)}) collective-permute-start(bf16[160,768]{1,0:T(8,128)(2,1)} %bitcast.16), channel_id=1, source_target_pairs={{2,0},{1,3},{4,2},{3,5},{6,4},{5,7},{8,6},{7,9},{10,8},{9,11},{12,... | collective-permute-start | bytes 737288 | tf_op jit(solution)/shard_map/ppermute | solution.py:162
  19.9 2.4 %collective-permute-done.refs_1_ = bf16[160,768]{1,0:T(8,128)(2,1)S(1)} collective-permute-done((bf16[160,768]{1,0:T(8,128)(2,1)}, bf16[160,768]{1,0:T(8,128)(2,1)S(1)}, u32[]{:S(2)}, u32[]{:S(2)}) %collective-permute-start) | collective-permute-done | bytes 245792 | tf_op jit(solution)/shard_map/ppermute | solution.py:161
  22.3 1.9 %collective-permute-start.2 = (bf16[160,768]{1,0:T(8,128)(2,1)S(1)}, bf16[160,768]{1,0:T(8,128)(2,1)S(1)}, u32[]{:S(2)}, u32[]{:S(2)}) collective-permute-start(bf16[160,768]{1,0:T(8,128)(2,1)S(1)} %collective-permute-done.refs_1_), channel_id=1, source_target_pairs={{0,2},{3,1},{2,4},{5,3},{4,6},{7,5},{6,8},{9,7},{8,10},{11,9},{10,... | collective-permute-start | bytes 737288 | tf_op jit(solution)/shard_map/ppermute | solution.py:161
  24.2 0.0 collective-permute-done.1.refs_2_
  24.3 5.8 %collective-permute-start.3 = (bf16[160,768]{1,0:T(8,128)(2,1)S(1)}, bf16[160,768]{1,0:T(8,128)(2,1)S(1)}, u32[]{:S(2)}, u32[]{:S(2)}) collective-permute-start(bf16[160,768]{1,0:T(8,128)(2,1)S(1)} %collective-permute-done.1.refs_2_), channel_id=1, source_target_pairs={{2,0},{1,3},{4,2},{3,5},{6,4},{5,7},{8,6},{7,9},{10,8},{9,11},{12,... | collective-permute-start | bytes 737288 | tf_op jit(solution)/shard_map/ppermute | solution.py:162
  30.1 2.9 %collective-permute-done.2.refs_3_ = bf16[160,768]{1,0:T(8,128)(2,1)S(1)} collective-permute-done((bf16[160,768]{1,0:T(8,128)(2,1)S(1)}, bf16[160,768]{1,0:T(8,128)(2,1)S(1)}, u32[]{:S(2)}, u32[]{:S(2)}) %collective-permute-start.2) | collective-permute-done | bytes 245792 | tf_op jit(solution)/shard_map/ppermute | solution.py:161
  32.9 1.9 %collective-permute-start.4 = (bf16[160,768]{1,0:T(8,128)(2,1)S(1)}, bf16[160,768]{1,0:T(8,128)(2,1)S(1)}, u32[]{:S(2)}, u32[]{:S(2)}) collective-permute-start(bf16[160,768]{1,0:T(8,128)(2,1)S(1)} %collective-permute-done.2.refs_3_), channel_id=1, source_target_pairs={{0,2},{3,1},{2,4},{5,3},{4,6},{7,5},{6,8},{9,7},{8,10},{11,9},{10,... | collective-permute-start | bytes 737288 | tf_op jit(solution)/shard_map/ppermute | solution.py:161
  34.8 0.0 collective-permute-done.3.refs_4_
  34.8 5.8 %collective-permute-start.5 = (bf16[160,768]{1,0:T(8,128)(2,1)S(1)}, bf16[160,768]{1,0:T(8,128)(2,1)S(1)}, u32[]{:S(2)}, u32[]{:S(2)}) collective-permute-start(bf16[160,768]{1,0:T(8,128)(2,1)S(1)} %collective-permute-done.3.refs_4_), channel_id=1, source_target_pairs={{2,0},{1,3},{4,2},{3,5},{6,4},{5,7},{8,6},{7,9},{10,8},{9,11},{12,... | collective-permute-start | bytes 737288 | tf_op jit(solution)/shard_map/ppermute | solution.py:162
  40.7 4.7 %collective-permute-done.4.refs_5_ = bf16[160,768]{1,0:T(8,128)(2,1)S(1)} collective-permute-done((bf16[160,768]{1,0:T(8,128)(2,1)S(1)}, bf16[160,768]{1,0:T(8,128)(2,1)S(1)}, u32[]{:S(2)}, u32[]{:S(2)}) %collective-permute-start.4) | collective-permute-done | bytes 245792 | tf_op jit(solution)/shard_map/ppermute | solution.py:161
  45.4 1.9 %collective-permute-start.6 = (bf16[160,768]{1,0:T(8,128)(2,1)S(1)}, bf16[160,768]{1,0:T(8,128)(2,1)S(1)}, u32[]{:S(2)}, u32[]{:S(2)}) collective-permute-start(bf16[160,768]{1,0:T(8,128)(2,1)S(1)} %collective-permute-done.4.refs_5_), channel_id=1, source_target_pairs={{0,2},{3,1},{2,4},{5,3},{4,6},{7,5},{6,8},{9,7},{8,10},{11,9},{10,... | collective-permute-start | bytes 737288 | tf_op jit(solution)/shard_map/ppermute | solution.py:164
  47.3 0.7 bitcast_convert_fusion
  48.0 0.0 copy-start.1
  48.0 1.1 copy-done.1
  49.1 0.8 copy-done.3
  49.9 0.7 copy-done.4
  50.6 0.7 copy-done.5
  51.3 0.4 shard_map.95
  51.7 0.0 collective-permute-done.5.refs_6_
  51.7 3.0 %collective-permute-done.6.refs_7_ = bf16[160,768]{1,0:T(8,128)(2,1)S(1)} collective-permute-done((bf16[160,768]{1,0:T(8,128)(2,1)S(1)}, bf16[160,768]{1,0:T(8,128)(2,1)S(1)}, u32[]{:S(2)}, u32[]{:S(2)}) %collective-permute-start.6) | collective-permute-done | bytes 245792 | tf_op jit(solution)/shard_map/ppermute | solution.py:164
  54.7 0.9 copy-done.2
  55.6 0.7 shard_map.96
  56.3 1.9 %collective-permute-start.7 = (bf16[1280,768]{1,0:T(8,128)(2,1)S(1)}, bf16[1280,768]{1,0:T(8,128)(2,1)S(1)}, u32[]{:S(2)}, u32[]{:S(2)}) collective-permute-start(bf16[1280,768]{1,0:T(8,128)(2,1)S(1)} %get-tuple-element.11.mine_ref), channel_id=1, source_target_pairs={{1,0},{0,1},{3,2},{2,3},{5,4},{4,5},{7,6},{6,7},{9,8},{8,9},{11,10... | collective-permute-start | bytes 5898248 | tf_op jit(solution)/shard_map/ppermute | solution.py:196
  58.2 3.9 %collective-permute-done.7.other_ref = bf16[1280,768]{1,0:T(8,128)(2,1)S(1)} collective-permute-done((bf16[1280,768]{1,0:T(8,128)(2,1)S(1)}, bf16[1280,768]{1,0:T(8,128)(2,1)S(1)}, u32[]{:S(2)}, u32[]{:S(2)}) %collective-permute-start.7) | collective-permute-done | bytes 1966112 | tf_op jit(solution)/shard_map/ppermute | solution.py:196
  62.2 0.0 copy-done
  62.2 0.7 shard_map.97
  62.8 10.6 %all_to_all.10.recv_ref = f32[16,8,128]{2,1,0:T(8,128)S(1)} all-to-all(f32[16,8,128]{2,1,0:T(8,128)S(1)} %shard_map.97), channel_id=1, replica_groups=mesh['dp'=64,'tensor'=16] {'tensor'}, dimensions={0} | all-to-all | bytes 131072 | tf_op jit(solution)/shard_map/all_to_all | solution.py:204
  73.5 1.3 %shard_map.98 = bf16[64,56,128]{2,1,0:T(8,128)(2,1)S(1)} custom-call(f32[16,8,128]{2,1,0:T(8,128)S(1)} %all_to_all.10.recv_ref, f32[3,8,128]{2,1,0:T(8,128)S(1)} %get-tuple-element.12.aux_ref, f32[8,128]{1,0:T(8,128)S(1)} %get-tuple-element.13.sums_ref, bf16[160,768]{1,0:T(8,128)(2,1)S(1)} %bitcast.14, bf16[1280,768]{1,0:T(8,128)(2,1)S(1)} %get-tuple-element.11.mine_ref, ...), custom_call_target="tpu_custom_call" | custom-call | tf_op jit(solution)/shard_map/pallas_call | solution.py:205
  74.8 41.6 %all_to_all.11.recv_ref = bf16[64,56,128]{2,1,0:T(8,128)(2,1)S(1)} all-to-all(bf16[64,56,128]{2,1,0:T(8,128)(2,1)S(1)} %shard_map.98), channel_id=1, replica_groups=mesh['dp'=64,'tensor'=16] {'dp'}, dimensions={0} | all-to-all | bytes 1835008 | tf_op jit(solution)/shard_map/all_to_all | solution.py:212
  116.4 0.8 shard_map.99
  117.2 0.5 slice_bitcast_fusion
  (5 shorter events, 0.0 us)
Async XLA Ops:
  0.6 21.7 %collective-permute-start = (bf16[160,768]{1,0:T(8,128)(2,1)}, bf16[160,768]{1,0:T(8,128)(2,1)S(1)}, u32[]{:S(2)}, u32[]{:S(2)}) collective-permute-start(bf16[160,768]{1,0:T(8,128)(2,1)} %bitcast.15), channel_id=1, source_target_pairs={{0,2},{3,1},{2,4},{5,3},{4,6},{7,5},{6,8},{9,7},{8,10},{11,9},{10,... | collective-permute-start | bytes 737288 | tf_op jit(solution)/shard_map/ppermute | solution.py:161
  5.8 18.4 %collective-permute-start.1 = (bf16[160,768]{1,0:T(8,128)(2,1)}, bf16[160,768]{1,0:T(8,128)(2,1)S(1)}, u32[]{:S(2)}, u32[]{:S(2)}) collective-permute-start(bf16[160,768]{1,0:T(8,128)(2,1)} %bitcast.16), channel_id=1, source_target_pairs={{2,0},{1,3},{4,2},{3,5},{6,4},{5,7},{8,6},{7,9},{10,8},{9,11},{12,... | collective-permute-start | bytes 737288 | tf_op jit(solution)/shard_map/ppermute | solution.py:162
  22.3 10.6 %collective-permute-start.2 = (bf16[160,768]{1,0:T(8,128)(2,1)S(1)}, bf16[160,768]{1,0:T(8,128)(2,1)S(1)}, u32[]{:S(2)}, u32[]{:S(2)}) collective-permute-start(bf16[160,768]{1,0:T(8,128)(2,1)S(1)} %collective-permute-done.refs_1_), channel_id=1, source_target_pairs={{0,2},{3,1},{2,4},{5,3},{4,6},{7,5},{6,8},{9,7},{8,10},{11,9},{10,... | collective-permute-start | bytes 737288 | tf_op jit(solution)/shard_map/ppermute | solution.py:161
  24.3 10.6 %collective-permute-start.3 = (bf16[160,768]{1,0:T(8,128)(2,1)S(1)}, bf16[160,768]{1,0:T(8,128)(2,1)S(1)}, u32[]{:S(2)}, u32[]{:S(2)}) collective-permute-start(bf16[160,768]{1,0:T(8,128)(2,1)S(1)} %collective-permute-done.1.refs_2_), channel_id=1, source_target_pairs={{2,0},{1,3},{4,2},{3,5},{6,4},{5,7},{8,6},{7,9},{10,8},{9,11},{12,... | collective-permute-start | bytes 737288 | tf_op jit(solution)/shard_map/ppermute | solution.py:162
  32.9 12.5 %collective-permute-start.4 = (bf16[160,768]{1,0:T(8,128)(2,1)S(1)}, bf16[160,768]{1,0:T(8,128)(2,1)S(1)}, u32[]{:S(2)}, u32[]{:S(2)}) collective-permute-start(bf16[160,768]{1,0:T(8,128)(2,1)S(1)} %collective-permute-done.2.refs_3_), channel_id=1, source_target_pairs={{0,2},{3,1},{2,4},{5,3},{4,6},{7,5},{6,8},{9,7},{8,10},{11,9},{10,... | collective-permute-start | bytes 737288 | tf_op jit(solution)/shard_map/ppermute | solution.py:161
  34.8 16.9 %collective-permute-start.5 = (bf16[160,768]{1,0:T(8,128)(2,1)S(1)}, bf16[160,768]{1,0:T(8,128)(2,1)S(1)}, u32[]{:S(2)}, u32[]{:S(2)}) collective-permute-start(bf16[160,768]{1,0:T(8,128)(2,1)S(1)} %collective-permute-done.3.refs_4_), channel_id=1, source_target_pairs={{2,0},{1,3},{4,2},{3,5},{6,4},{5,7},{8,6},{7,9},{10,8},{9,11},{12,... | collective-permute-start | bytes 737288 | tf_op jit(solution)/shard_map/ppermute | solution.py:162
  45.4 9.3 %collective-permute-start.6 = (bf16[160,768]{1,0:T(8,128)(2,1)S(1)}, bf16[160,768]{1,0:T(8,128)(2,1)S(1)}, u32[]{:S(2)}, u32[]{:S(2)}) collective-permute-start(bf16[160,768]{1,0:T(8,128)(2,1)S(1)} %collective-permute-done.4.refs_5_), channel_id=1, source_target_pairs={{0,2},{3,1},{2,4},{5,3},{4,6},{7,5},{6,8},{9,7},{8,10},{11,9},{10,... | collective-permute-start | bytes 737288 | tf_op jit(solution)/shard_map/ppermute | solution.py:164
  48.0 1.1 copy-start.1
  49.1 0.8 copy-start.3
  49.9 0.7 copy-start.4
  50.6 0.7 copy-start.5
  51.3 10.9 %copy-start = (bf16[768,160]{0,1:T(8,128)(2,1)S(1)}, bf16[768,160]{0,1:T(8,128)(2,1)}, u32[]{:S(2)}) copy-start(bf16[768,160]{0,1:T(8,128)(2,1)} %param.8) | copy-start | bytes 737284
  54.7 0.9 copy-start.2
  56.3 5.9 %collective-permute-start.7 = (bf16[1280,768]{1,0:T(8,128)(2,1)S(1)}, bf16[1280,768]{1,0:T(8,128)(2,1)S(1)}, u32[]{:S(2)}, u32[]{:S(2)}) collective-permute-start(bf16[1280,768]{1,0:T(8,128)(2,1)S(1)} %get-tuple-element.11.mine_ref), channel_id=1, source_target_pairs={{1,0},{0,1},{3,2},{2,3},{5,4},{4,5},{7,6},{6,7},{9,8},{8,9},{11,10... | collective-permute-start | bytes 5898248 | tf_op jit(solution)/shard_map/ppermute | solution.py:196

commit v8 on v5

--- a/solution.py
+++ b/solution.py
@@ -26,7 +26,10 @@
     return (((device >> 1) + N_Z + STEPS[place % N_Z]) & (N_Z - 1)) * 2 + side
 
 
-def prepare_kernel(w_ref, gap_ref, size_ref, sign_ref, keep_ref, plan_ref, out_ref, aux_ref, sums_ref):
+def prepare_kernel(
+    w_ref, gap_ref, size_ref, sign_ref, keep_ref, plan_ref, readout_ref, out_ref, aux_ref, sums_ref, own_ref
+):
+    own_ref[...] = readout_ref[...]
     width = out_ref.shape[2]
     for k in range(N_TENSOR):
         out_ref[k] = w_ref[:, width * k : width * k + width]
@@ -137,10 +140,8 @@
     divisor = jnp.maximum(pick(0), 1.0)
     rest = jnp.concatenate([first[:, 32 * k : 32 * k + 32] for k in range(4)] + [second[:, :32]], axis=0)
     grad_ref[...] = jnp.concatenate([total[:40], rest], axis=1) / divisor
-    stats_ref[...] = (
-        jnp.where(lane == 0, -pick(3), jnp.where(lane == 1, pick(1), jnp.where(lane == 2, pick(2), 0.0)))
-        / divisor
-    )
+    for k, part in enumerate((-pick(3), pick(1), pick(2))):
+        stats_ref[k] = jnp.sum(part / divisor)
 
 
 def body(
@@ -163,14 +164,15 @@
 
     params = pltpu.CompilerParams(vmem_limit_bytes=24 << 20)
     tiled = (local_rows // LANES, LANES)
-    w_blocks, aux, sums = pl.pallas_call(
+    w_blocks, aux, sums, own = pl.pallas_call(
         prepare_kernel,
-        in_specs=[vmem_spec()] * 6,
-        out_specs=[vmem_spec()] * 3,
+        in_specs=[vmem_spec()] * 7,
+        out_specs=[vmem_spec()] * 4,
         out_shape=[
             jax.ShapeDtypeStruct((N_TENSOR, width, width), w_out.dtype),
             jax.ShapeDtypeStruct((3, 8, LANES), jnp.float32),
             jax.ShapeDtypeStruct((8, LANES), jnp.float32),
+            jax.ShapeDtypeStruct(readout_t.shape, readout_t.dtype),
         ],
         compiler_params=params,
     )(
@@ -180,6 +182,7 @@
         reward_sign.reshape(tiled),
         keep_mask.reshape(tiled),
         move_plan,
+        readout_t,
     )
     first, mine = pl.pallas_call(
         first_kernel,
@@ -190,7 +193,7 @@
             jax.ShapeDtypeStruct((N_Z * width, local_rows), readout_t.dtype),
         ],
         compiler_params=params,
-    )(w_blocks, *nearby)
+    )(w_blocks, own, *nearby[1:])
     other = lax.ppermute(mine, "tensor", swap)
     partial_shift = pl.pallas_call(
         shift_kernel,
@@ -211,14 +214,14 @@
     grad_t, stats = pl.pallas_call(
         finish_kernel,
         in_specs=[vmem_spec()],
-        out_specs=[vmem_spec(), vmem_spec()],
+        out_specs=[vmem_spec(), pl.BlockSpec(memory_space=pltpu.SMEM)],
         out_shape=[
             jax.ShapeDtypeStruct((40, width), jnp.float32),
-            jax.ShapeDtypeStruct((1, LANES), jnp.float32),
+            jax.ShapeDtypeStruct((3,), jnp.float32),
         ],
         compiler_params=pltpu.CompilerParams(vmem_limit_bytes=24 << 20),
     )(received)
-    return grad_t.T, stats[0, :3]
+    return grad_t.T, stats
 
 
 def solution(mesh):

time: 116 us -> 115 us (level)
  no operation moved by 1% of the time
where the time goes in v8:
time: 115 us; the launch traced here: 114 us
  blocking collectives  52 us (45%)
  starting transfers between devices  37.2 us (32%)
  waiting for transfers between devices  15.6 us (14%)
  local copies, waits for them, and re-layouts  4.22 us (4%)
  Pallas kernels  3.91 us (3%)
    all_to_all x1, blocking collectives, body(): received = lax.all_to_all(chunks, 'dp', 0, 0, tiled=True)  41.6 us
    ppermute x3, starting transfers between devices, body(): falling = lax.ppermute(falling, 'tensor', down)  24.3 us
    all_to_all x1, blocking collectives, body(): shifts = lax.all_to_all(partial_shift, 'tensor', 0, 0, tiled=True)  10.4 us
    ppermute x3, waiting for transfers between devices, body(): rising = lax.ppermute(rising, 'tensor', up)  9.63 us
    ppermute x3, starting transfers between devices, body(): rising = lax.ppermute(rising, 'tensor', up)  9.01 us
    unnamed x12, local copies, waits for them, and re-layouts  4.22 us
    ppermute x1, waiting for transfers between devices, body(): other = lax.ppermute(mine, 'tensor', swap)  3.94 us
  transfers between devices with their start and end apart: 8, of which 5 were waited for; matrix products, arithmetic and copies ran while one was open for 1% of the time, Pallas kernels for 0%

profile of v8, /device:TPU:4, one launch (start us, length us, event | category | flops | bytes accessed | tf_op | source)
XLA Modules:
  0.0 114.3 jit_solution(312037941463457873)
XLA Ops:
  0.6 5.2 %collective-permute-start = (bf16[160,768]{1,0:T(8,128)(2,1)}, bf16[160,768]{1,0:T(8,128)(2,1)S(1)}, u32[]{:S(2)}, u32[]{:S(2)}) collective-permute-start(bf16[160,768]{1,0:T(8,128)(2,1)} %bitcast.13), channel_id=1, source_target_pairs={{0,2},{1,3},{2,4},{3,5},{4,6},{5,7},{6,8},{7,9},{8,10},{9,11},{10,... | collective-permute-start | bytes 737288 | tf_op jit(solution)/shard_map/ppermute | solution.py:160
  5.8 14.0 %collective-permute-start.1 = (bf16[160,768]{1,0:T(8,128)(2,1)}, bf16[160,768]{1,0:T(8,128)(2,1)S(1)}, u32[]{:S(2)}, u32[]{:S(2)}) collective-permute-start(bf16[160,768]{1,0:T(8,128)(2,1)} %bitcast.14), channel_id=1, source_target_pairs={{2,0},{3,1},{4,2},{5,3},{6,4},{7,5},{8,6},{9,7},{10,8},{11,9},{12,... | collective-permute-start | bytes 737288 | tf_op jit(solution)/shard_map/ppermute | solution.py:161
  19.9 4.2 %collective-permute-done.refs_1_ = bf16[160,768]{1,0:T(8,128)(2,1)S(1)} collective-permute-done((bf16[160,768]{1,0:T(8,128)(2,1)}, bf16[160,768]{1,0:T(8,128)(2,1)S(1)}, u32[]{:S(2)}, u32[]{:S(2)}) %collective-permute-start) | collective-permute-done | bytes 245792 | tf_op jit(solution)/shard_map/ppermute | solution.py:160
  24.1 1.9 %collective-permute-start.2 = (bf16[160,768]{1,0:T(8,128)(2,1)S(1)}, bf16[160,768]{1,0:T(8,128)(2,1)S(1)}, u32[]{:S(2)}, u32[]{:S(2)}) collective-permute-start(bf16[160,768]{1,0:T(8,128)(2,1)S(1)} %collective-permute-done.refs_1_), channel_id=1, source_target_pairs={{0,2},{1,3},{2,4},{3,5},{4,6},{5,7},{6,8},{7,9},{8,10},{9,11},{10,... | collective-permute-start | bytes 737288 | tf_op jit(solution)/shard_map/ppermute | solution.py:160
  26.0 0.0 collective-permute-done.1.refs_2_
  26.0 5.1 %collective-permute-start.3 = (bf16[160,768]{1,0:T(8,128)(2,1)S(1)}, bf16[160,768]{1,0:T(8,128)(2,1)S(1)}, u32[]{:S(2)}, u32[]{:S(2)}) collective-permute-start(bf16[160,768]{1,0:T(8,128)(2,1)S(1)} %collective-permute-done.1.refs_2_), channel_id=1, source_target_pairs={{2,0},{3,1},{4,2},{5,3},{6,4},{7,5},{8,6},{9,7},{10,8},{11,9},{12,... | collective-permute-start | bytes 737288 | tf_op jit(solution)/shard_map/ppermute | solution.py:161
  31.2 3.2 %collective-permute-done.2.refs_3_ = bf16[160,768]{1,0:T(8,128)(2,1)S(1)} collective-permute-done((bf16[160,768]{1,0:T(8,128)(2,1)S(1)}, bf16[160,768]{1,0:T(8,128)(2,1)S(1)}, u32[]{:S(2)}, u32[]{:S(2)}) %collective-permute-start.2) | collective-permute-done | bytes 245792 | tf_op jit(solution)/shard_map/ppermute | solution.py:160
  34.3 1.9 %collective-permute-start.4 = (bf16[160,768]{1,0:T(8,128)(2,1)S(1)}, bf16[160,768]{1,0:T(8,128)(2,1)S(1)}, u32[]{:S(2)}, u32[]{:S(2)}) collective-permute-start(bf16[160,768]{1,0:T(8,128)(2,1)S(1)} %collective-permute-done.2.refs_3_), channel_id=1, source_target_pairs={{0,2},{1,3},{2,4},{3,5},{4,6},{5,7},{6,8},{7,9},{8,10},{9,11},{10,... | collective-permute-start | bytes 737288 | tf_op jit(solution)/shard_map/ppermute | solution.py:160
  36.3 0.0 collective-permute-done.3.refs_4_
  36.3 5.1 %collective-permute-start.5 = (bf16[160,768]{1,0:T(8,128)(2,1)S(1)}, bf16[160,768]{1,0:T(8,128)(2,1)S(1)}, u32[]{:S(2)}, u32[]{:S(2)}) collective-permute-start(bf16[160,768]{1,0:T(8,128)(2,1)S(1)} %collective-permute-done.3.refs_4_), channel_id=1, source_target_pairs={{2,0},{3,1},{4,2},{5,3},{6,4},{7,5},{8,6},{9,7},{10,8},{11,9},{12,... | collective-permute-start | bytes 737288 | tf_op jit(solution)/shard_map/ppermute | solution.py:161
  41.4 2.2 %collective-permute-done.4.refs_5_ = bf16[160,768]{1,0:T(8,128)(2,1)S(1)} collective-permute-done((bf16[160,768]{1,0:T(8,128)(2,1)S(1)}, bf16[160,768]{1,0:T(8,128)(2,1)S(1)}, u32[]{:S(2)}, u32[]{:S(2)}) %collective-permute-start.4) | collective-permute-done | bytes 245792 | tf_op jit(solution)/shard_map/ppermute | solution.py:160
  43.7 1.9 %collective-permute-start.6 = (bf16[160,768]{1,0:T(8,128)(2,1)S(1)}, bf16[160,768]{1,0:T(8,128)(2,1)S(1)}, u32[]{:S(2)}, u32[]{:S(2)}) collective-permute-start(bf16[160,768]{1,0:T(8,128)(2,1)S(1)} %collective-permute-done.4.refs_5_), channel_id=1, source_target_pairs={{0,2},{1,3},{2,4},{3,5},{4,6},{5,7},{6,8},{7,9},{8,10},{9,11},{10,... | collective-permute-start | bytes 737288 | tf_op jit(solution)/shard_map/ppermute | solution.py:163
  45.6 0.7 bitcast_convert_fusion
  46.3 0.0 copy-start.1
  46.3 1.1 copy-done.1
  47.4 0.0 copy-start.2
  47.4 0.9 copy-done.2
  48.4 0.8 copy-done.3
  49.1 0.7 copy-done.4
  49.8 0.7 copy-done.5
  50.5 0.4 shard_map.95
  50.9 0.0 collective-permute-done.5.refs_6_
  50.9 2.0 %collective-permute-done.6.refs_7_ = bf16[160,768]{1,0:T(8,128)(2,1)S(1)} collective-permute-done((bf16[160,768]{1,0:T(8,128)(2,1)S(1)}, bf16[160,768]{1,0:T(8,128)(2,1)S(1)}, u32[]{:S(2)}, u32[]{:S(2)}) %collective-permute-start.6) | collective-permute-done | bytes 245792 | tf_op jit(solution)/shard_map/ppermute | solution.py:163
  52.9 0.7 shard_map.96
  53.6 1.9 %collective-permute-start.7 = (bf16[1280,768]{1,0:T(8,128)(2,1)S(1)}, bf16[1280,768]{1,0:T(8,128)(2,1)S(1)}, u32[]{:S(2)}, u32[]{:S(2)}) collective-permute-start(bf16[1280,768]{1,0:T(8,128)(2,1)S(1)} %get-tuple-element.13.mine_ref), channel_id=1, source_target_pairs={{1,0},{0,1},{3,2},{2,3},{5,4},{4,5},{7,6},{6,7},{9,8},{8,9},{11,10... | collective-permute-start | bytes 5898248 | tf_op jit(solution)/shard_map/ppermute | solution.py:197
  55.5 3.9 %collective-permute-done.7.other_ref = bf16[1280,768]{1,0:T(8,128)(2,1)S(1)} collective-permute-done((bf16[1280,768]{1,0:T(8,128)(2,1)S(1)}, bf16[1280,768]{1,0:T(8,128)(2,1)S(1)}, u32[]{:S(2)}, u32[]{:S(2)}) %collective-permute-start.7) | collective-permute-done | bytes 1966112 | tf_op jit(solution)/shard_map/ppermute | solution.py:197
  59.5 0.0 copy-done
  59.5 0.7 shard_map.97
  60.2 10.4 %all_to_all.10.recv_ref = f32[16,8,128]{2,1,0:T(8,128)S(1)} all-to-all(f32[16,8,128]{2,1,0:T(8,128)S(1)} %shard_map.97), channel_id=1, replica_groups=mesh['dp'=64,'tensor'=16] {'tensor'}, dimensions={0} | all-to-all | bytes 131072 | tf_op jit(solution)/shard_map/all_to_all | solution.py:205
  70.6 1.3 %shard_map.98 = bf16[64,56,128]{2,1,0:T(8,128)(2,1)S(1)} custom-call(f32[16,8,128]{2,1,0:T(8,128)S(1)} %all_to_all.10.recv_ref, f32[3,8,128]{2,1,0:T(8,128)S(1)} %get-tuple-element.14.aux_ref, f32[8,128]{1,0:T(8,128)S(1)} %get-tuple-element.15.sums_ref, bf16[160,768]{1,0:T(8,128)(2,1)S(1)} %bitcast.12, bf16[1280,768]{1,0:T(8,128)(2,1)S(1)} %get-tuple-element.13.mine_ref, ...), custom_call_target="tpu_custom_call" | custom-call | tf_op jit(solution)/shard_map/pallas_call | solution.py:206
  71.9 41.6 %all_to_all.11.recv_ref = bf16[64,56,128]{2,1,0:T(8,128)(2,1)S(1)} all-to-all(bf16[64,56,128]{2,1,0:T(8,128)(2,1)S(1)} %shard_map.98), channel_id=1, replica_groups=mesh['dp'=64,'tensor'=16] {'dp'}, dimensions={0} | all-to-all | bytes 1835008 | tf_op jit(solution)/shard_map/all_to_all | solution.py:213
  113.5 0.8 shard_map.99
  (4 shorter events, 0.0 us)
Async XLA Ops:
  0.6 23.5 %collective-permute-start = (bf16[160,768]{1,0:T(8,128)(2,1)}, bf16[160,768]{1,0:T(8,128)(2,1)S(1)}, u32[]{:S(2)}, u32[]{:S(2)}) collective-permute-start(bf16[160,768]{1,0:T(8,128)(2,1)} %bitcast.13), channel_id=1, source_target_pairs={{0,2},{1,3},{2,4},{3,5},{4,6},{5,7},{6,8},{7,9},{8,10},{9,11},{10,... | collective-permute-start | bytes 737288 | tf_op jit(solution)/shard_map/ppermute | solution.py:160
  5.8 20.2 %collective-permute-start.1 = (bf16[160,768]{1,0:T(8,128)(2,1)}, bf16[160,768]{1,0:T(8,128)(2,1)S(1)}, u32[]{:S(2)}, u32[]{:S(2)}) collective-permute-start(bf16[160,768]{1,0:T(8,128)(2,1)} %bitcast.14), channel_id=1, source_target_pairs={{2,0},{3,1},{4,2},{5,3},{6,4},{7,5},{8,6},{9,7},{10,8},{11,9},{12,... | collective-permute-start | bytes 737288 | tf_op jit(solution)/shard_map/ppermute | solution.py:161
  24.1 10.2 %collective-permute-start.2 = (bf16[160,768]{1,0:T(8,128)(2,1)S(1)}, bf16[160,768]{1,0:T(8,128)(2,1)S(1)}, u32[]{:S(2)}, u32[]{:S(2)}) collective-permute-start(bf16[160,768]{1,0:T(8,128)(2,1)S(1)} %collective-permute-done.refs_1_), channel_id=1, source_target_pairs={{0,2},{1,3},{2,4},{3,5},{4,6},{5,7},{6,8},{7,9},{8,10},{9,11},{10,... | collective-permute-start | bytes 737288 | tf_op jit(solution)/shard_map/ppermute | solution.py:160
  26.0 10.2 %collective-permute-start.3 = (bf16[160,768]{1,0:T(8,128)(2,1)S(1)}, bf16[160,768]{1,0:T(8,128)(2,1)S(1)}, u32[]{:S(2)}, u32[]{:S(2)}) collective-permute-start(bf16[160,768]{1,0:T(8,128)(2,1)S(1)} %collective-permute-done.1.refs_2_), channel_id=1, source_target_pairs={{2,0},{3,1},{4,2},{5,3},{6,4},{7,5},{8,6},{9,7},{10,8},{11,9},{12,... | collective-permute-start | bytes 737288 | tf_op jit(solution)/shard_map/ppermute | solution.py:161
  34.3 9.3 %collective-permute-start.4 = (bf16[160,768]{1,0:T(8,128)(2,1)S(1)}, bf16[160,768]{1,0:T(8,128)(2,1)S(1)}, u32[]{:S(2)}, u32[]{:S(2)}) collective-permute-start(bf16[160,768]{1,0:T(8,128)(2,1)S(1)} %collective-permute-done.2.refs_3_), channel_id=1, source_target_pairs={{0,2},{1,3},{2,4},{3,5},{4,6},{5,7},{6,8},{7,9},{8,10},{9,11},{10,... | collective-permute-start | bytes 737288 | tf_op jit(solution)/shard_map/ppermute | solution.py:160
  36.3 14.7 %collective-permute-start.5 = (bf16[160,768]{1,0:T(8,128)(2,1)S(1)}, bf16[160,768]{1,0:T(8,128)(2,1)S(1)}, u32[]{:S(2)}, u32[]{:S(2)}) collective-permute-start(bf16[160,768]{1,0:T(8,128)(2,1)S(1)} %collective-permute-done.3.refs_4_), channel_id=1, source_target_pairs={{2,0},{3,1},{4,2},{5,3},{6,4},{7,5},{8,6},{9,7},{10,8},{11,9},{12,... | collective-permute-start | bytes 737288 | tf_op jit(solution)/shard_map/ppermute | solution.py:161
  43.7 9.3 %collective-permute-start.6 = (bf16[160,768]{1,0:T(8,128)(2,1)S(1)}, bf16[160,768]{1,0:T(8,128)(2,1)S(1)}, u32[]{:S(2)}, u32[]{:S(2)}) collective-permute-start(bf16[160,768]{1,0:T(8,128)(2,1)S(1)} %collective-permute-done.4.refs_5_), channel_id=1, source_target_pairs={{0,2},{1,3},{2,4},{3,5},{4,6},{5,7},{6,8},{7,9},{8,10},{9,11},{10,... | collective-permute-start | bytes 737288 | tf_op jit(solution)/shard_map/ppermute | solution.py:163
  46.3 1.1 %copy-start.1 = (bf16[160,2560]{1,0:T(8,128)(2,1)S(1)}, bf16[160,2560]{1,0:T(8,128)(2,1)}, u32[]{:S(2)}) copy-start(bf16[160,2560]{1,0:T(8,128)(2,1)} %w_ref.1) | copy-start | bytes 2457604
  47.4 0.9 copy-start.2
  48.4 0.8 copy-start.3
  49.1 0.7 copy-start.4
  49.8 0.7 copy-start.5
  50.5 9.0 %copy-start = (bf16[768,160]{0,1:T(8,128)(2,1)S(1)}, bf16[768,160]{0,1:T(8,128)(2,1)}, u32[]{:S(2)}) copy-start(bf16[768,160]{0,1:T(8,128)(2,1)} %param.8) | copy-start | bytes 737284
  53.6 5.9 %collective-permute-start.7 = (bf16[1280,768]{1,0:T(8,128)(2,1)S(1)}, bf16[1280,768]{1,0:T(8,128)(2,1)S(1)}, u32[]{:S(2)}, u32[]{:S(2)}) collective-permute-start(bf16[1280,768]{1,0:T(8,128)(2,1)S(1)} %get-tuple-element.13.mine_ref), channel_id=1, source_target_pairs={{1,0},{0,1},{3,2},{2,3},{5,4},{4,5},{7,6},{6,7},{9,8},{8,9},{11,10... | collective-permute-start | bytes 5898248 | tf_op jit(solution)/shard_map/ppermute | solution.py:197

commit v9 on v8

--- a/solution.py
+++ b/solution.py
@@ -27,7 +27,7 @@
 
 
 def prepare_kernel(
-    w_ref, gap_ref, size_ref, sign_ref, keep_ref, plan_ref, readout_ref, out_ref, aux_ref, sums_ref, own_ref
+    w_ref, rows_ref, plan_ref, readout_ref, out_ref, aux_ref, sums_ref, own_ref
 ):
     own_ref[...] = readout_ref[...]
     width = out_ref.shape[2]
@@ -35,11 +35,11 @@
         out_ref[k] = w_ref[:, width * k : width * k + width]
     owner = lax.broadcasted_iota(jnp.int32, plan_ref.shape, 0)
     live_total = jnp.sum(jnp.where(owner == lax.axis_index("dp"), plan_ref[...], 0))
-    shape = gap_ref.shape
+    gap, size, sign, keep = (rows_ref[k] for k in range(4))
+    shape = gap.shape
     slot_ids = lax.broadcasted_iota(jnp.int32, shape, 0) * LANES + lax.broadcasted_iota(jnp.int32, shape, 1)
-    weight = jnp.where(slot_ids < live_total, keep_ref[...], 0).astype(jnp.float32)
-    gap = gap_ref[...]
-    advantage = (2 * sign_ref[...] - 1).astype(jnp.float32) * size_ref[...]
+    weight = jnp.where(slot_ids < live_total, keep, 0.0)
+    advantage = (2.0 * sign - 1.0) * size
     base_ratio = jnp.exp(gap)
     clip_high = jnp.where((advantage > 0) & (base_ratio > 1.0 + EPS_HIGH), 1.0, 0.0)
     clip_low = jnp.where((advantage < 0) & (base_ratio < 1.0 - EPS_LOW), 1.0, 0.0)
@@ -166,7 +166,7 @@
     tiled = (local_rows // LANES, LANES)
     w_blocks, aux, sums, own = pl.pallas_call(
         prepare_kernel,
-        in_specs=[vmem_spec()] * 7,
+        in_specs=[vmem_spec()] * 4,
         out_specs=[vmem_spec()] * 4,
         out_shape=[
             jax.ShapeDtypeStruct((N_TENSOR, width, width), w_out.dtype),
@@ -177,10 +177,12 @@
         compiler_params=params,
     )(
         w_out,
-        log_gap.astype(jnp.float32).reshape(tiled),
-        magnitude.astype(jnp.float32).reshape(tiled),
-        reward_sign.reshape(tiled),
-        keep_mask.reshape(tiled),
+        jnp.stack(
+            [
+                row.astype(jnp.float32).reshape(tiled)
+                for row in (log_gap, magnitude, reward_sign, keep_mask)
+            ]
+        ),
         move_plan,
         readout_t,
     )

time: 115 us -> 115 us (level)
  local copies, waits for them, and re-layouts: 4.22 us -> 2.85 us
    another operation x0 -> x3, other arithmetic: none -> 1.42 us  [body(): jnp.stack([row.astype(jnp.float32).reshape(tiled) for row in (log_gap, ma...]
    unnamed x12 -> x8, local copies, waits for them, and re-layouts: 4.22 us -> 2.85 us
    ppermute x1, waiting for transfers between devices: 2.01 us -> 3.38 us  [body(): nearby.append(lax.ppermute(rising, 'tensor', up))]
where the time goes in v9:
time: 115 us; the launch traced here: 114 us
  blocking collectives  52 us (45%)
  starting transfers between devices  37.1 us (32%)
  waiting for transfers between devices  16.3 us (14%)
  Pallas kernels  3.91 us (3%)
  local copies, waits for them, and re-layouts  2.85 us (2%)
  other arithmetic  1.42 us (1%)
    all_to_all x1, blocking collectives, body(): received = lax.all_to_all(chunks, 'dp', 0, 0, tiled=True)  41.6 us
    ppermute x3, starting transfers between devices, body(): falling = lax.ppermute(falling, 'tensor', down)  24.3 us
    all_to_all x1, blocking collectives, body(): shifts = lax.all_to_all(partial_shift, 'tensor', 0, 0, tiled=True)  10.4 us
    ppermute x3, starting transfers between devices, body(): rising = lax.ppermute(rising, 'tensor', up)  9.01 us
    ppermute x3, waiting for transfers between devices, body(): rising = lax.ppermute(rising, 'tensor', up)  8.94 us
    ppermute x1, waiting for transfers between devices, body(): other = lax.ppermute(mine, 'tensor', swap)  3.94 us
    ppermute x1, waiting for transfers between devices, body(): nearby.append(lax.ppermute(rising, 'tensor', up))  3.38 us
    unnamed x8, local copies, waits for them, and re-layouts  2.85 us
  transfers between devices with their start and end apart: 8, of which 5 were waited for; matrix products, arithmetic and copies ran while one was open for 1% of the time, Pallas kernels for 0%

profile of v9, /device:TPU:4, one launch (start us, length us, event | category | flops | bytes accessed | tf_op | source)
XLA Modules:
  0.0 114.3 jit_solution(17273526093381174788)
XLA Ops:
  0.6 5.2 %collective-permute-start = (bf16[160,768]{1,0:T(8,128)(2,1)}, bf16[160,768]{1,0:T(8,128)(2,1)S(1)}, u32[]{:S(2)}, u32[]{:S(2)}) collective-permute-start(bf16[160,768]{1,0:T(8,128)(2,1)} %bitcast.15), channel_id=1, source_target_pairs={{0,2},{1,3},{2,4},{3,5},{4,6},{5,7},{6,8},{7,9},{8,10},{9,11},{10,... | collective-permute-start | bytes 737288 | tf_op jit(solution)/shard_map/ppermute | solution.py:160
  5.8 14.0 %collective-permute-start.1 = (bf16[160,768]{1,0:T(8,128)(2,1)}, bf16[160,768]{1,0:T(8,128)(2,1)S(1)}, u32[]{:S(2)}, u32[]{:S(2)}) collective-permute-start(bf16[160,768]{1,0:T(8,128)(2,1)} %bitcast.16), channel_id=1, source_target_pairs={{2,0},{3,1},{4,2},{5,3},{6,4},{7,5},{8,6},{9,7},{10,8},{11,9},{12,... | collective-permute-start | bytes 737288 | tf_op jit(solution)/shard_map/ppermute | solution.py:161
  19.9 4.2 %collective-permute-done.refs_1_ = bf16[160,768]{1,0:T(8,128)(2,1)S(1)} collective-permute-done((bf16[160,768]{1,0:T(8,128)(2,1)}, bf16[160,768]{1,0:T(8,128)(2,1)S(1)}, u32[]{:S(2)}, u32[]{:S(2)}) %collective-permute-start) | collective-permute-done | bytes 245792 | tf_op jit(solution)/shard_map/ppermute | solution.py:160
  24.1 1.9 %collective-permute-start.2 = (bf16[160,768]{1,0:T(8,128)(2,1)S(1)}, bf16[160,768]{1,0:T(8,128)(2,1)S(1)}, u32[]{:S(2)}, u32[]{:S(2)}) collective-permute-start(bf16[160,768]{1,0:T(8,128)(2,1)S(1)} %collective-permute-done.refs_1_), channel_id=1, source_target_pairs={{0,2},{1,3},{2,4},{3,5},{4,6},{5,7},{6,8},{7,9},{8,10},{9,11},{10,... | collective-permute-start | bytes 737288 | tf_op jit(solution)/shard_map/ppermute | solution.py:160
  26.0 0.0 collective-permute-done.1.refs_2_
  26.0 5.1 %collective-permute-start.3 = (bf16[160,768]{1,0:T(8,128)(2,1)S(1)}, bf16[160,768]{1,0:T(8,128)(2,1)S(1)}, u32[]{:S(2)}, u32[]{:S(2)}) collective-permute-start(bf16[160,768]{1,0:T(8,128)(2,1)S(1)} %collective-permute-done.1.refs_2_), channel_id=1, source_target_pairs={{2,0},{3,1},{4,2},{5,3},{6,4},{7,5},{8,6},{9,7},{10,8},{11,9},{12,... | collective-permute-start | bytes 737288 | tf_op jit(solution)/shard_map/ppermute | solution.py:161
  31.2 3.2 %collective-permute-done.2.refs_3_ = bf16[160,768]{1,0:T(8,128)(2,1)S(1)} collective-permute-done((bf16[160,768]{1,0:T(8,128)(2,1)S(1)}, bf16[160,768]{1,0:T(8,128)(2,1)S(1)}, u32[]{:S(2)}, u32[]{:S(2)}) %collective-permute-start.2) | collective-permute-done | bytes 245792 | tf_op jit(solution)/shard_map/ppermute | solution.py:160
  34.3 1.9 %collective-permute-start.4 = (bf16[160,768]{1,0:T(8,128)(2,1)S(1)}, bf16[160,768]{1,0:T(8,128)(2,1)S(1)}, u32[]{:S(2)}, u32[]{:S(2)}) collective-permute-start(bf16[160,768]{1,0:T(8,128)(2,1)S(1)} %collective-permute-done.2.refs_3_), channel_id=1, source_target_pairs={{0,2},{1,3},{2,4},{3,5},{4,6},{5,7},{6,8},{7,9},{8,10},{9,11},{10,... | collective-permute-start | bytes 737288 | tf_op jit(solution)/shard_map/ppermute | solution.py:160
  36.3 0.7 convert_bitcast_fusion
  37.0 0.0 collective-permute-done.3.refs_4_
  37.0 5.1 %collective-permute-start.5 = (bf16[160,768]{1,0:T(8,128)(2,1)S(1)}, bf16[160,768]{1,0:T(8,128)(2,1)S(1)}, u32[]{:S(2)}, u32[]{:S(2)}) collective-permute-start(bf16[160,768]{1,0:T(8,128)(2,1)S(1)} %collective-permute-done.3.refs_4_), channel_id=1, source_target_pairs={{2,0},{3,1},{4,2},{5,3},{6,4},{7,5},{8,6},{9,7},{10,8},{11,9},{12,... | collective-permute-start | bytes 737288 | tf_op jit(solution)/shard_map/ppermute | solution.py:161
  42.1 1.6 %collective-permute-done.4.refs_5_ = bf16[160,768]{1,0:T(8,128)(2,1)S(1)} collective-permute-done((bf16[160,768]{1,0:T(8,128)(2,1)S(1)}, bf16[160,768]{1,0:T(8,128)(2,1)S(1)}, u32[]{:S(2)}, u32[]{:S(2)}) %collective-permute-start.4) | collective-permute-done | bytes 245792 | tf_op jit(solution)/shard_map/ppermute | solution.py:160
  43.7 1.9 %collective-permute-start.6 = (bf16[160,768]{1,0:T(8,128)(2,1)S(1)}, bf16[160,768]{1,0:T(8,128)(2,1)S(1)}, u32[]{:S(2)}, u32[]{:S(2)}) collective-permute-start(bf16[160,768]{1,0:T(8,128)(2,1)S(1)} %collective-permute-done.4.refs_5_), channel_id=1, source_target_pairs={{0,2},{1,3},{2,4},{3,5},{4,6},{5,7},{6,8},{7,9},{8,10},{9,11},{10,... | collective-permute-start | bytes 737288 | tf_op jit(solution)/shard_map/ppermute | solution.py:163
  45.6 0.7 bitcast_convert_fusion
  46.3 0.0 copy-start.1
  46.3 1.1 copy-done.1
  47.4 0.0 copy-start.2
  47.4 0.9 copy-done.2
  48.4 0.0 copy-start.3
  48.4 0.8 copy-done.3
  49.1 0.4 shard_map.95
  49.6 0.0 collective-permute-done.5.refs_6_
  49.6 3.4 %collective-permute-done.6.refs_7_ = bf16[160,768]{1,0:T(8,128)(2,1)S(1)} collective-permute-done((bf16[160,768]{1,0:T(8,128)(2,1)S(1)}, bf16[160,768]{1,0:T(8,128)(2,1)S(1)}, u32[]{:S(2)}, u32[]{:S(2)}) %collective-permute-start.6) | collective-permute-done | bytes 245792 | tf_op jit(solution)/shard_map/ppermute | solution.py:163
  52.9 0.7 shard_map.96
  53.6 1.9 %collective-permute-start.7 = (bf16[1280,768]{1,0:T(8,128)(2,1)S(1)}, bf16[1280,768]{1,0:T(8,128)(2,1)S(1)}, u32[]{:S(2)}, u32[]{:S(2)}) collective-permute-start(bf16[1280,768]{1,0:T(8,128)(2,1)S(1)} %get-tuple-element.13.mine_ref), channel_id=1, source_target_pairs={{1,0},{0,1},{3,2},{2,3},{5,4},{4,5},{7,6},{6,7},{9,8},{8,9},{11,10... | collective-permute-start | bytes 5898248 | tf_op jit(solution)/shard_map/ppermute | solution.py:199
  55.5 3.9 %collective-permute-done.7.other_ref = bf16[1280,768]{1,0:T(8,128)(2,1)S(1)} collective-permute-done((bf16[1280,768]{1,0:T(8,128)(2,1)S(1)}, bf16[1280,768]{1,0:T(8,128)(2,1)S(1)}, u32[]{:S(2)}, u32[]{:S(2)}) %collective-permute-start.7) | collective-permute-done | bytes 1966112 | tf_op jit(solution)/shard_map/ppermute | solution.py:199
  59.5 0.0 copy-done
  59.5 0.7 shard_map.97
  60.2 10.4 %all_to_all.10.recv_ref = f32[16,8,128]{2,1,0:T(8,128)S(1)} all-to-all(f32[16,8,128]{2,1,0:T(8,128)S(1)} %shard_map.97), channel_id=1, replica_groups=mesh['dp'=64,'tensor'=16] {'tensor'}, dimensions={0} | all-to-all | bytes 131072 | tf_op jit(solution)/shard_map/all_to_all | solution.py:207
  70.6 1.3 %shard_map.98 = bf16[64,56,128]{2,1,0:T(8,128)(2,1)S(1)} custom-call(f32[16,8,128]{2,1,0:T(8,128)S(1)} %all_to_all.10.recv_ref, f32[3,8,128]{2,1,0:T(8,128)S(1)} %get-tuple-element.14.aux_ref, f32[8,128]{1,0:T(8,128)S(1)} %get-tuple-element.15.sums_ref, bf16[160,768]{1,0:T(8,128)(2,1)S(1)} %bitcast.14, bf16[1280,768]{1,0:T(8,128)(2,1)S(1)} %get-tuple-element.13.mine_ref, ...), custom_call_target="tpu_custom_call" | custom-call | tf_op jit(solution)/shard_map/pallas_call | solution.py:208
  71.9 41.6 %all_to_all.11.recv_ref = bf16[64,56,128]{2,1,0:T(8,128)(2,1)S(1)} all-to-all(bf16[64,56,128]{2,1,0:T(8,128)(2,1)S(1)} %shard_map.98), channel_id=1, replica_groups=mesh['dp'=64,'tensor'=16] {'dp'}, dimensions={0} | all-to-all | bytes 1835008 | tf_op jit(solution)/shard_map/all_to_all | solution.py:215
  113.5 0.8 shard_map.99
  (2 shorter events, 0.0 us)
Async XLA Ops:
  0.6 23.5 %collective-permute-start = (bf16[160,768]{1,0:T(8,128)(2,1)}, bf16[160,768]{1,0:T(8,128)(2,1)S(1)}, u32[]{:S(2)}, u32[]{:S(2)}) collective-permute-start(bf16[160,768]{1,0:T(8,128)(2,1)} %bitcast.15), channel_id=1, source_target_pairs={{0,2},{1,3},{2,4},{3,5},{4,6},{5,7},{6,8},{7,9},{8,10},{9,11},{10,... | collective-permute-start | bytes 737288 | tf_op jit(solution)/shard_map/ppermute | solution.py:160
  5.8 20.2 %collective-permute-start.1 = (bf16[160,768]{1,0:T(8,128)(2,1)}, bf16[160,768]{1,0:T(8,128)(2,1)S(1)}, u32[]{:S(2)}, u32[]{:S(2)}) collective-permute-start(bf16[160,768]{1,0:T(8,128)(2,1)} %bitcast.16), channel_id=1, source_target_pairs={{2,0},{3,1},{4,2},{5,3},{6,4},{7,5},{8,6},{9,7},{10,8},{11,9},{12,... | collective-permute-start | bytes 737288 | tf_op jit(solution)/shard_map/ppermute | solution.py:161
  24.1 10.2 %collective-permute-start.2 = (bf16[160,768]{1,0:T(8,128)(2,1)S(1)}, bf16[160,768]{1,0:T(8,128)(2,1)S(1)}, u32[]{:S(2)}, u32[]{:S(2)}) collective-permute-start(bf16[160,768]{1,0:T(8,128)(2,1)S(1)} %collective-permute-done.refs_1_), channel_id=1, source_target_pairs={{0,2},{1,3},{2,4},{3,5},{4,6},{5,7},{6,8},{7,9},{8,10},{9,11},{10,... | collective-permute-start | bytes 737288 | tf_op jit(solution)/shard_map/ppermute | solution.py:160
  26.0 10.9 %collective-permute-start.3 = (bf16[160,768]{1,0:T(8,128)(2,1)S(1)}, bf16[160,768]{1,0:T(8,128)(2,1)S(1)}, u32[]{:S(2)}, u32[]{:S(2)}) collective-permute-start(bf16[160,768]{1,0:T(8,128)(2,1)S(1)} %collective-permute-done.1.refs_2_), channel_id=1, source_target_pairs={{2,0},{3,1},{4,2},{5,3},{6,4},{7,5},{8,6},{9,7},{10,8},{11,9},{12,... | collective-permute-start | bytes 737288 | tf_op jit(solution)/shard_map/ppermute | solution.py:161
  34.3 9.3 %collective-permute-start.4 = (bf16[160,768]{1,0:T(8,128)(2,1)S(1)}, bf16[160,768]{1,0:T(8,128)(2,1)S(1)}, u32[]{:S(2)}, u32[]{:S(2)}) collective-permute-start(bf16[160,768]{1,0:T(8,128)(2,1)S(1)} %collective-permute-done.2.refs_3_), channel_id=1, source_target_pairs={{0,2},{1,3},{2,4},{3,5},{4,6},{5,7},{6,8},{7,9},{8,10},{9,11},{10,... | collective-permute-start | bytes 737288 | tf_op jit(solution)/shard_map/ppermute | solution.py:160
  37.0 12.6 %collective-permute-start.5 = (bf16[160,768]{1,0:T(8,128)(2,1)S(1)}, bf16[160,768]{1,0:T(8,128)(2,1)S(1)}, u32[]{:S(2)}, u32[]{:S(2)}) collective-permute-start(bf16[160,768]{1,0:T(8,128)(2,1)S(1)} %collective-permute-done.3.refs_4_), channel_id=1, source_target_pairs={{2,0},{3,1},{4,2},{5,3},{6,4},{7,5},{8,6},{9,7},{10,8},{11,9},{12,... | collective-permute-start | bytes 737288 | tf_op jit(solution)/shard_map/ppermute | solution.py:161
  43.7 9.3 %collective-permute-start.6 = (bf16[160,768]{1,0:T(8,128)(2,1)S(1)}, bf16[160,768]{1,0:T(8,128)(2,1)S(1)}, u32[]{:S(2)}, u32[]{:S(2)}) collective-permute-start(bf16[160,768]{1,0:T(8,128)(2,1)S(1)} %collective-permute-done.4.refs_5_), channel_id=1, source_target_pairs={{0,2},{1,3},{2,4},{3,5},{4,6},{5,7},{6,8},{7,9},{8,10},{9,11},{10,... | collective-permute-start | bytes 737288 | tf_op jit(solution)/shard_map/ppermute | solution.py:163
  46.3 1.1 %copy-start.1 = (bf16[160,2560]{1,0:T(8,128)(2,1)S(1)}, bf16[160,2560]{1,0:T(8,128)(2,1)}, u32[]{:S(2)}) copy-start(bf16[160,2560]{1,0:T(8,128)(2,1)} %w_ref.1) | copy-start | bytes 2457604
  47.4 0.9 copy-start.2
  48.4 0.8 copy-start.3
  49.1 10.4 %copy-start = (bf16[768,160]{0,1:T(8,128)(2,1)S(1)}, bf16[768,160]{0,1:T(8,128)(2,1)}, u32[]{:S(2)}) copy-start(bf16[768,160]{0,1:T(8,128)(2,1)} %param.8) | copy-start | bytes 737284
  53.6 5.9 %collective-permute-start.7 = (bf16[1280,768]{1,0:T(8,128)(2,1)S(1)}, bf16[1280,768]{1,0:T(8,128)(2,1)S(1)}, u32[]{:S(2)}, u32[]{:S(2)}) collective-permute-start(bf16[1280,768]{1,0:T(8,128)(2,1)S(1)} %get-tuple-element.13.mine_ref), channel_id=1, source_target_pairs={{1,0},{0,1},{3,2},{2,3},{5,4},{4,5},{7,6},{6,7},{9,8},{8,9},{11,10... | collective-permute-start | bytes 5898248 | tf_op jit(solution)/shard_map/ppermute | solution.py:199
